TPU v7x, 32 devices: a whole 2x2x4 slice. The times are simulated.
32 devices in a mesh: rows: 8 (over y, x, core), cp: 4 (over z).
Axes of the slice: x: 2, y: 2, z: 4, core: 2. Of those that a mesh axis runs over, the one named last changes fastest.
Arguments:
- tokens: bfloat16 [8, 2, 1024, 1024], P('rows', None, 'cp'), may hold values from -6 to 6
- doc_starts: int32 [8, 4], P('rows'), may hold values from 0 to 2047, as said below
- qkv_weight: bfloat16 [1024, 3072], P('rows', 'cp'), may hold values from -0.1875 to 0.1875
- out_weight: bfloat16 [1024, 1024], P('rows', 'cp'), may hold values from -0.1875 to 0.1875
- up_weight: bfloat16 [1024, 4096], P('rows', 'cp'), may hold values from -0.1875 to 0.1875
- down_weight: bfloat16 [4096, 1024], P('cp', 'rows'), may hold values from -0.09375 to 0.09375
- norm_gains: bfloat16 [4096], P(('rows', 'cp')), may hold values from 0.5 to 1.5
- cotangent: bfloat16 [8, 2, 1024, 1024], P('rows', None, 'cp'), may hold values from -6 to 6
Outputs:
- mixed: bfloat16 [8, 2, 1024, 1024], P('rows', None, 'cp')
- tokens_grad: float32 [8, 2, 1024, 1024], P('rows', None, 'cp')
- qkv_grad: float32 [1024, 3072], P('rows', 'cp')
- out_grad: float32 [1024, 1024], P('rows', 'cp')
- up_grad: float32 [1024, 4096], P('rows', 'cp')
- down_grad: float32 [4096, 1024], P('cp', 'rows')
- gains_grad: float32 [4096], P(('rows', 'cp'))
Inputs may be any that keep to these rules, and one draw needn't show every extreme that they name: `doc_starts`: in each row the 4 document starts rise strictly and the first is 0; a position belongs to the document with the last start at or before it.
All inputs are finite; a program needn't handle non-finite values.
Results may differ from a plain program's by a relative error of at most 0.023.
Values may be sent and summed in bfloat16 or wider, within the bound.
No kernel may reach another device: no remote copies, remote signals or barrier semaphores. Data moves between devices by JAX's collectives and lax.ppermute only.
A program may use at most 640 MiB of HBM per device.

v0:
```python
import math

import jax
import jax.numpy as jnp
from jax import lax
from jax.sharding import PartitionSpec as P

HEADS = 16
HEAD_DIM = 64


NORM_EPS = 1e-05
MASKED = -1e30


def layer_norm(values):
    average = jnp.mean(values, axis=-1, keepdims=True)
    centred = values - average
    spread = jnp.mean(centred * centred, axis=-1, keepdims=True)
    return centred * lax.rsqrt(spread + NORM_EPS)


def norm_back(values, upstream):
    _, pull_back = jax.vjp(layer_norm, values)
    return pull_back(upstream)[0]


def gelu_tanh(values):
    return jax.nn.gelu(values, approximate=True)


def rotate(values, cosine, sine_part):
    half_width = values.shape[-1] // 2
    first_half = values[..., :half_width]
    second_half = values[..., half_width:]
    return jnp.concatenate(
        [
            first_half * cosine - second_half * sine_part,
            second_half * cosine + first_half * sine_part,
        ],
        axis=-1,
    )


def rounded(values):
    return lax.optimization_barrier(values.astype(jnp.bfloat16)).astype(jnp.float32)


def doc_start_of(starts, positions):
    return jnp.max(
        jnp.where(starts[:, None, :] <= positions[None, :, None], starts[:, None, :], 0), axis=-1
    )


def body(tokens, doc_starts, qkv_weight, out_weight, up_weight, down_weight, norm_gains, cotangent):
    rows_count = lax.axis_size("rows")
    cp_count = lax.axis_size("cp")
    qkv_rows, out_rows, up_rows, down_rows, gain_piece = (
        lax.all_gather(qkv_weight, "rows", axis=0, tiled=True),
        lax.all_gather(out_weight, "rows", axis=0, tiled=True),
        lax.all_gather(up_weight, "rows", axis=0, tiled=True),
        lax.all_gather(down_weight, "rows", axis=1, tiled=True),
        lax.all_gather(norm_gains, "rows", axis=0, tiled=True),
    )
    qkv_full, out_full, gain_mixed = (
        lax.all_gather(qkv_rows, "cp", axis=1, tiled=True),
        lax.all_gather(out_rows, "cp", axis=1, tiled=True),
        lax.all_gather(gain_piece, "cp", axis=0, tiled=True),
    )
    gain_full = jnp.transpose(gain_mixed.reshape(cp_count, rows_count, -1), (1, 0, 2)).reshape(-1)
    row_count, _, span_len, width = tokens.shape
    half_len = span_len * cp_count
    row_len = 2 * half_len
    queries_dev = 2 * span_len
    token_total = row_count * queries_dev
    group_total = row_count * row_len
    gain_rows = gain_full.astype(jnp.float32).reshape(4, width)
    score_scale = HEAD_DIM ** (-0.5)
    local_pos = lax.axis_index("cp") * span_len + jnp.arange(span_len, dtype=jnp.int32)
    query_pos = jnp.concatenate([local_pos, row_len - 1 - local_pos])
    half_pos = jnp.arange(half_len, dtype=jnp.int32)
    key_pos = jnp.concatenate([half_pos, row_len - 1 - half_pos])
    query_start = doc_start_of(doc_starts, query_pos)
    key_start = doc_start_of(doc_starts, key_pos)
    freq_index = jnp.arange(HEAD_DIM // 2, dtype=jnp.float32)
    inverse_freq = jnp.exp(-math.log(10000.0) * 2.0 * freq_index / HEAD_DIM)
    angles = (query_pos[None, :] - query_start).astype(jnp.float32)[..., None] * inverse_freq
    cosine = jnp.cos(angles)[:, :, None, :]
    sine_part = jnp.sin(angles)[:, :, None, :]
    head_shape = (row_count, queries_dev, HEADS, HEAD_DIM)
    flat_shape = (row_count, queries_dev, width)
    fold_shape = (row_count, 2, span_len, width)
    group_shape = (row_count, 2, half_len, width)
    full_shape = (row_count, row_len, HEADS, HEAD_DIM)
    inputs = tokens.astype(jnp.float32).reshape(flat_shape)
    normed_in = layer_norm(inputs)
    normed = (normed_in * gain_rows[0]).astype(jnp.bfloat16)
    linear = jnp.dot(normed, qkv_full, preferred_element_type=jnp.float32)
    query_rows = rotate(linear[..., :width].reshape(head_shape), cosine, sine_part).astype(
        jnp.bfloat16
    )
    key_local = rotate(
        linear[..., width : 2 * width].reshape(head_shape), cosine, sine_part
    ).astype(jnp.bfloat16)
    value_local = linear[..., 2 * width :].reshape(head_shape).astype(jnp.bfloat16)
    key_sent, value_sent = (
        lax.all_gather(key_local.reshape(fold_shape), "cp", axis=2, tiled=True),
        lax.all_gather(value_local.reshape(fold_shape), "cp", axis=2, tiled=True),
    )
    key_rows = key_sent.reshape(full_shape)
    value_rows = value_sent.reshape(full_shape)
    block_size = min(512, row_len)
    block_count = row_len // block_size
    block_range = jnp.arange(block_count)

    def block_scores(block_index):
        first_key = block_index * block_size
        key_block = lax.dynamic_slice_in_dim(key_rows, first_key, block_size, 1)
        pos_block = lax.dynamic_slice_in_dim(key_pos, first_key, block_size, 0)
        start_block = lax.dynamic_slice_in_dim(key_start, first_key, block_size, 1)
        raw_scores = jnp.einsum(
            "rqhd,rkhd->rhqk", query_rows, key_block, preferred_element_type=jnp.float32
        )
        allowed = (query_start[:, None, :, None] == start_block[:, None, None, :]) & (
            pos_block[None, None, None, :] <= query_pos[None, None, :, None]
        )
        return (raw_scores * score_scale, allowed)

    def max_step(carry, block_index):
        running_max, running_sum = carry
        scores, allowed = block_scores(block_index)
        scores = jnp.where(allowed, scores, MASKED)
        new_max = jnp.maximum(running_max, jnp.max(scores, axis=-1))
        running_sum = running_sum * jnp.exp(running_max - new_max) + jnp.sum(
            jnp.where(allowed, jnp.exp(scores - new_max[..., None]), 0.0), axis=-1
        )
        return ((new_max, running_sum), None)

    stat_shape = (row_count, HEADS, queries_dev)
    (running_max, running_sum), _ = lax.scan(
        max_step,
        (jnp.full(stat_shape, MASKED, jnp.float32), jnp.zeros(stat_shape, jnp.float32)),
        block_range,
    )
    log_total = running_max + jnp.log(running_sum)

    def value_step(totals, block_index):
        scores, allowed = block_scores(block_index)
        probs = jnp.where(allowed, jnp.exp(scores - log_total[..., None]), 0.0).astype(jnp.bfloat16)
        value_block = lax.dynamic_slice_in_dim(value_rows, block_index * block_size, block_size, 1)
        return (
            totals
            + jnp.einsum("rhqk,rkhd->rqhd", probs, value_block, preferred_element_type=jnp.float32),
            None,
        )

    attended, _ = lax.scan(value_step, jnp.zeros(head_shape, jnp.float32), block_range)
    mixed_heads = attended.reshape(flat_shape).astype(jnp.bfloat16)
    branch = jnp.dot(mixed_heads, out_full, preferred_element_type=jnp.float32)
    branch_hat = layer_norm(branch)
    hidden = inputs + branch_hat * gain_rows[1]
    hidden_hat = layer_norm(hidden)
    normed_mid = (hidden_hat * gain_rows[2]).astype(jnp.bfloat16)
    ffn_in = lax.all_gather(normed_mid.reshape(fold_shape), "cp", axis=2, tiled=True).reshape(
        group_total, width
    )
    up_proj = jnp.dot(ffn_in, up_rows, preferred_element_type=jnp.float32)
    activation = gelu_tanh(up_proj).astype(jnp.bfloat16)
    down_terms = jnp.dot(activation, down_rows, preferred_element_type=jnp.float32)
    down_proj = (
        lax.psum_scatter(
            down_terms.reshape(group_shape).astype(jnp.bfloat16),
            "cp",
            scatter_dimension=2,
            tiled=True,
        )
        .astype(jnp.float32)
        .reshape(flat_shape)
    )
    down_hat = layer_norm(down_proj)
    mixed = (hidden + down_hat * gain_rows[3]).astype(jnp.bfloat16).reshape(tokens.shape)
    upstream = cotangent.astype(jnp.float32).reshape(flat_shape)
    gain_four = jnp.sum(upstream * down_hat, axis=(0, 1))
    grad_down_out = norm_back(down_proj, upstream * gain_rows[3]).astype(jnp.bfloat16)
    grad_out_rows = lax.all_gather(
        grad_down_out.reshape(fold_shape), "cp", axis=2, tiled=True
    ).reshape(group_total, width)
    down_local = jnp.einsum(
        "tf,td->fd", activation, grad_out_rows, preferred_element_type=jnp.float32
    )
    grad_act = jnp.einsum("td,fd->tf", grad_out_rows, down_rows, preferred_element_type=jnp.float32)
    _, gelu_pull = jax.vjp(gelu_tanh, up_proj)
    grad_up = gelu_pull(grad_act)[0].astype(jnp.bfloat16)
    up_local = jnp.einsum("tc,tf->cf", ffn_in, grad_up, preferred_element_type=jnp.float32)
    mid_terms = jnp.einsum("tf,cf->tc", grad_up, up_rows, preferred_element_type=jnp.float32)
    grad_mid = (
        lax.psum_scatter(
            mid_terms.reshape(group_shape).astype(jnp.bfloat16),
            "cp",
            scatter_dimension=2,
            tiled=True,
        )
        .astype(jnp.float32)
        .reshape(flat_shape)
    )
    gain_three = jnp.sum(grad_mid * hidden_hat, axis=(0, 1))
    grad_hidden = upstream + norm_back(hidden, grad_mid * gain_rows[2])
    gain_two = jnp.sum(grad_hidden * branch_hat, axis=(0, 1))
    grad_branch = norm_back(branch, grad_hidden * gain_rows[1]).astype(jnp.bfloat16)
    out_local = jnp.einsum(
        "tc,te->ce",
        mixed_heads.reshape(token_total, width),
        grad_branch.reshape(token_total, width),
        preferred_element_type=jnp.float32,
    )
    grad_heads = (
        jnp.einsum("rqe,ce->rqc", grad_branch, out_full, preferred_element_type=jnp.float32)
        .astype(jnp.bfloat16)
        .reshape(head_shape)
    )
    delta_sum = jnp.transpose(
        jnp.sum(grad_heads.astype(jnp.float32) * attended, axis=-1), (0, 2, 1)
    )

    def score_grads(block_index):
        scores, allowed = block_scores(block_index)
        probs = jnp.where(allowed, jnp.exp(scores - log_total[..., None]), 0.0)
        first_key = block_index * block_size
        key_block = lax.dynamic_slice_in_dim(key_rows, first_key, block_size, 1)
        value_block = lax.dynamic_slice_in_dim(value_rows, first_key, block_size, 1)
        grad_probs = jnp.einsum(
            "rqhd,rkhd->rhqk", grad_heads, value_block, preferred_element_type=jnp.float32
        )
        grad_scores = (probs * (grad_probs - delta_sum[..., None]) * score_scale).astype(
            jnp.bfloat16
        )
        return (probs, grad_scores, key_block)

    def grad_step(grad_query, block_index):
        probs, grad_scores, key_block = score_grads(block_index)
        grad_query = grad_query + jnp.einsum(
            "rhqk,rkhd->rqhd", grad_scores, key_block, preferred_element_type=jnp.float32
        )
        key_part = jnp.einsum(
            "rhqk,rqhd->rkhd", grad_scores, query_rows, preferred_element_type=jnp.float32
        )
        value_part = jnp.einsum(
            "rhqk,rqhd->rkhd",
            probs.astype(jnp.bfloat16),
            grad_heads,
            preferred_element_type=jnp.float32,
        )
        return (grad_query, (key_part, value_part))

    grad_query, (key_parts, value_parts) = lax.scan(
        grad_step, jnp.zeros(head_shape, jnp.float32), block_range
    )
    key_terms = jnp.moveaxis(key_parts, 0, 1).reshape(group_shape)
    value_terms = jnp.moveaxis(value_parts, 0, 1).reshape(group_shape)
    key_sum, value_sum = (
        lax.psum_scatter(
            key_terms.astype(jnp.bfloat16), "cp", scatter_dimension=2, tiled=True
        ).astype(jnp.float32),
        lax.psum_scatter(
            value_terms.astype(jnp.bfloat16), "cp", scatter_dimension=2, tiled=True
        ).astype(jnp.float32),
    )
    query_unturned = rotate(rounded(grad_query), cosine, -sine_part).reshape(flat_shape)
    key_unturned = rotate(rounded(key_sum.reshape(head_shape)), cosine, -sine_part).reshape(
        flat_shape
    )
    grad_linear = jnp.concatenate(
        [query_unturned, key_unturned, value_sum.reshape(flat_shape)], axis=-1
    ).astype(jnp.bfloat16)
    qkv_local = jnp.einsum(
        "tc,te->ce",
        normed.reshape(token_total, width),
        grad_linear.reshape(token_total, 3 * width),
        preferred_element_type=jnp.float32,
    )
    grad_normed = jnp.einsum(
        "rqe,ce->rqc", grad_linear, qkv_full, preferred_element_type=jnp.float32
    )
    gain_one = jnp.sum(grad_normed * normed_in, axis=(0, 1))
    tokens_grad = (grad_hidden + norm_back(inputs, grad_normed * gain_rows[0])).reshape(
        tokens.shape
    )
    gain_local = jnp.concatenate([gain_one, gain_two, gain_three, gain_four])
    gain_order = jnp.transpose(gain_local.reshape(rows_count, cp_count, -1), (1, 0, 2)).reshape(-1)
    qkv_mid, out_mid, gain_mid = (
        lax.psum_scatter(
            qkv_local.astype(jnp.bfloat16), "cp", scatter_dimension=1, tiled=True
        ).astype(jnp.float32),
        lax.psum_scatter(
            out_local.astype(jnp.bfloat16), "cp", scatter_dimension=1, tiled=True
        ).astype(jnp.float32),
        lax.psum_scatter(
            gain_order.astype(jnp.bfloat16), "cp", scatter_dimension=0, tiled=True
        ).astype(jnp.float32),
    )
    qkv_sum, out_sum, up_sum, down_sum, gain_sum = (
        lax.psum_scatter(
            qkv_mid.astype(jnp.bfloat16), "rows", scatter_dimension=0, tiled=True
        ).astype(jnp.float32),
        lax.psum_scatter(
            out_mid.astype(jnp.bfloat16), "rows", scatter_dimension=0, tiled=True
        ).astype(jnp.float32),
        lax.psum_scatter(
            up_local.astype(jnp.bfloat16), "rows", scatter_dimension=0, tiled=True
        ).astype(jnp.float32),
        lax.psum_scatter(
            down_local.astype(jnp.bfloat16), "rows", scatter_dimension=1, tiled=True
        ).astype(jnp.float32),
        lax.psum_scatter(
            gain_mid.astype(jnp.bfloat16), "rows", scatter_dimension=0, tiled=True
        ).astype(jnp.float32),
    )
    return (mixed, tokens_grad, qkv_sum, out_sum, up_sum, down_sum, gain_sum)


def solution(mesh):
    in_specs = (
        P("rows", None, "cp", None),
        P("rows", None),
        P("rows", "cp"),
        P("rows", "cp"),
        P("rows", "cp"),
        P("cp", "rows"),
        P(("rows", "cp")),
        P("rows", None, "cp", None),
    )
    out_specs = (
        P("rows", None, "cp", None),
        P("rows", None, "cp", None),
        P("rows", "cp"),
        P("rows", "cp"),
        P("rows", "cp"),
        P("cp", "rows"),
        P(("rows", "cp")),
    )
    return jax.shard_map(body, mesh=mesh, in_specs=in_specs, out_specs=out_specs, check_vma=False)
```

profile of v0, /device:TPU:0, one launch (start us, length us, event | category | flops | bytes accessed | tf_op | source)
XLA Modules:
  0.0 2957.1 jit_solution(7835324012992124875)
XLA Ops:
  8.0 30.4 %all-gather.11.cloned.1.call-done = bf16[1024,768]{1,0:T(8,128)(2,1)} async-done(((bf16[128,768]{1,0:T(8,128)(2,1)}), bf16[1024,768]{1,0:T(8,128)(2,1)}) %all-gather.11.cloned.1.call-update) | async-done | bytes 1572880 | tf_op jit(solution)/shard_map/all_gather | solution.py:59
  39.7 8.7 all-gather
  48.4 14.1 all_gather.37
  63.5 92.0 %all-gather.13.cloned.1.call-done = bf16[1024,3072]{1,0:T(8,128)(2,1)} async-done(((bf16[1024,768]{1,0:T(8,128)(2,1)}), bf16[1024,3072]{1,0:T(8,128)(2,1)}) %all-gather.13.cloned.1.call-update) | async-done | bytes 6291472 | tf_op jit(solution)/shard_map/all_gather | solution.py:66
  180.8 10.8 all_gather.42
  192.9 50.9 %all-gather.15.cloned.1.call-done = bf16[1,2,1024,1024]{3,2,1,0:T(8,128)(2,1)} async-done(((bf16[1,2,256,1024]{3,2,1,0:T(8,128)(2,1)}), bf16[1,2,1024,1024]{3,2,1,0:T(8,128)(2,1)}) %all-gather.15.cloned.1.call-update) | async-done | bytes 4194320 | tf_op jit(solution)/shard_map/all_gather | solution.py:108
  243.8 11.5 copy.78
  263.1 61.3 %all-gather.17.cloned.1.call-done = bf16[1,2,1024,1024]{2,1,3,0:T(2,128)(2,1)} async-done(((bf16[1,2,256,1024]{2,1,3,0:T(2,128)(2,1)}), bf16[1,2,1024,1024]{2,1,3,0:T(2,128)(2,1)}) %all-gather.17.cloned.1.call-update) | async-done | bytes 4194320 | tf_op jit(solution)/shard_map/all_gather | solution.py:107
  332.3 38.2 %while.39 = (s32[]{:T(128)}, f32[1,16,512]{2,1,0:T(8,128)S(1)}, f32[1,16,512]{2,1,0:T(8,128)S(1)}, s32[1,512]{1,0:T(1,128)S(1)}, s32[4]{0:T(128)S(1)}, /*index=5...) while((s32[]{:T(128)}, f32[1,16,512]{2,1,0:T(8,128)S(1)}, ...), condition=%wide.region_7.8_spmd.clone, body=%wide.region_4.7_spmd.clone.sunk | while | flops 571252736 | bytes 36880604 | solution.py:140
  370.5 39.6 %while.40 = (s32[]{:T(128)}, f32[1,512,16,64]{1,3,2,0:T(8,128)}, s32[4]{0:T(128)S(1)}, bf16[1,2048,16,64]{1,3,2,0:T(8,128)(2,1)}, s32[1,512]{1,0:T(1,128)S(1)}, ...) while((s32[]{:T(128)}, f32[1,512,16,64]{1,3,2,0:T(8,128)}, ...), condition=%wide.region_9.10_spmd.clone, body=%wide.region_8.9_spmd.clone.sunk | while | flops 1092354048 | bytes 7915232 | solution.py:157
  419.1 78.4 %all-gather.21.cloned.1.call-done = bf16[1,2,1024,1024]{3,2,1,0:T(8,128)(2,1)} async-done(((bf16[1,2,256,1024]{3,2,1,0:T(8,128)(2,1)}), bf16[1,2,1024,1024]{3,2,1,0:T(8,128)(2,1)}) %all-gather.21.cloned.1.call-update) | async-done | bytes 4194320 | tf_op jit(solution)/shard_map/all_gather | solution.py:164
  497.5 10.6 fusion.91
  508.2 18.0 all-gather.25.cloned.1.call-done
  526.2 11.5 convolution_convert_fusion.2
  537.9 76.7 %reduce-scatter.17.cloned.1.call-done = bf16[1,2,256,1024]{3,2,1,0:T(8,128)(2,1)} async-done(((bf16[1,2,1024,1024]{3,2,1,0:T(8,128)(2,1)}), bf16[1,2,256,1024]{3,2,1,0:T(8,128)(2,1)}) %reduce-scatter.17.cloned.1.call-update) | async-done | bytes 1048592 | tf_op jit(solution)/shard_map/reduce_scatter | solution.py:171
  621.9 81.4 %all-gather.27.cloned.1.call-done = bf16[1,2,1024,1024]{3,2,1,0:T(8,128)(2,1)} async-done(((bf16[1,2,256,1024]{3,2,1,0:T(8,128)(2,1)}), bf16[1,2,1024,1024]{3,2,1,0:T(8,128)(2,1)}) %all-gather.27.cloned.1.call-update) | async-done | bytes 4194320 | tf_op jit(solution)/shard_map/all_gather | solution.py:185
  703.3 12.6 fusion.50
  722.4 75.4 %reduce-scatter.19.cloned.1.call-done = bf16[1,2,256,1024]{3,2,1,0:T(8,128)(2,1)} async-done(((bf16[1,2,1024,1024]{3,2,1,0:T(8,128)(2,1)}), bf16[1,2,256,1024]{3,2,1,0:T(8,128)(2,1)}) %reduce-scatter.19.cloned.1.call-update) | async-done | bytes 1048592 | tf_op jit(solution)/shard_map/reduce_scatter | solution.py:197
  823.6 155.7 %while.41 = (s32[]{:T(128)}, f32[1,512,16,64]{1,3,2,0:T(8,128)S(1)}, bf16[4,1,512,16,64]{2,4,3,1,0:T(8,128)(2,1)}, bf16[4,1,512,16,64]{2,4,3,1,0:T(8,128)(2,1)},...) while((s32[]{:T(128)}, ...), condition=%wide.region_26.27_spmd.clone, body=%wide.region_25.26_spmd.clone.sunk | while | flops 2732326912 | bytes 125682000 | solution.py:255
  825.2 9.6 fusion.142
  834.7 10.4 bitcast_dynamic-update-slice_fusion.5
  845.1 9.9 fusion.143
  864.2 9.4 fusion.142
  873.6 10.3 bitcast_dynamic-update-slice_fusion.5
  883.9 10.0 fusion.143
  903.1 9.3 fusion.142
  912.4 10.3 bitcast_dynamic-update-slice_fusion.5
  922.7 9.9 fusion.143
  941.8 9.3 fusion.142
  951.1 10.3 bitcast_dynamic-update-slice_fusion.5
  961.4 9.9 fusion.143
  979.3 8.5 copy.85
  987.8 10.2 convert_element_type.284
  998.0 176.5 %copy.92 = bf16[1,2,1024,1024]{1,3,0,2:T(8,128)(2,1)} copy(bf16[1,2,1024,1024]{2,1,3,0:T(2,128)(2,1)} %convert_element_type.284) | data formatting | bytes 8388608
  1174.4 486.0 %reshape.1457 = bf16[1024,2048]{1,0:T(8,128)(2,1)} reshape(bf16[1024,1,1024,2]{3,2,1,0:T(8,128)(2,1)} %bitcast.82) | data formatting | bytes 8388608
  1668.4 10.2 convert_element_type.288
  1678.6 176.5 %copy.94 = bf16[1,2,1024,1024]{1,3,0,2:T(8,128)(2,1)} copy(bf16[1,2,1024,1024]{2,1,3,0:T(2,128)(2,1)} %convert_element_type.288) | data formatting | bytes 8388608
  1855.0 486.0 %reshape.1459 = bf16[1024,2048]{1,0:T(8,128)(2,1)} reshape(bf16[1024,1,1024,2]{3,2,1,0:T(8,128)(2,1)} %bitcast.85) | data formatting | bytes 8388608
  2341.3 10.1 convolution_convert_fusion.3
  2354.1 9.4 convolution_convert_fusion.4
  2366.1 146.5 %reshape.1458 = bf16[256,1,1024,2]{3,2,1,0:T(8,128)(2,1)} reshape(bf16[256,2048]{1,0:T(8,128)(2,1)} %reduce-scatter.31.cloned.1.call-done) | data formatting | bytes 2097152
  2512.5 59.5 %copy.93 = bf16[1,2,256,1024]{2,1,3,0:T(2,128)(2,1)S(1)} copy(bf16[1,2,256,1024]{1,3,0,2:T(8,128)(2,1)} %bitcast.83) | data formatting | bytes 2097152
  2576.3 146.4 %reshape.1460 = bf16[256,1,1024,2]{3,2,1,0:T(8,128)(2,1)} reshape(bf16[256,2048]{1,0:T(8,128)(2,1)} %reduce-scatter.33.cloned.1.call-done) | data formatting | bytes 2097152
  2722.8 59.4 %copy.95 = bf16[1,2,256,1024]{2,1,3,0:T(2,128)(2,1)S(1)} copy(bf16[1,2,256,1024]{1,3,0,2:T(8,128)(2,1)} %bitcast.86) | data formatting | bytes 2097152
  2786.3 8.5 convolution_convert_fusion
  2803.2 103.0 %reduce-scatter.21.cloned.1.call-done = bf16[1024,768]{1,0:T(8,128)(2,1)} async-done(((bf16[1024,3072]{1,0:T(8,128)(2,1)}), bf16[1024,768]{1,0:T(8,128)(2,1)}) %reduce-scatter.21.cloned.1.call-update) | async-done | bytes 1572880 | tf_op jit(solution)/shard_map/reduce_scatter | solution.py:291
  2915.6 11.1 all-reduce
  2926.8 12.1 all-reduce.1
  (344 shorter events, 249.1 us)
Async XLA Ops:
  7.2 31.2 %copy-start.6 = (bf16[1,2,256,1024]{3,2,1,0:T(8,128)(2,1)S(1)}, bf16[1,2,256,1024]{3,2,1,0:T(8,128)(2,1)}, u32[]{:S(2)}) copy-start(bf16[1,2,256,1024]{3,2,1,0:T(8,128)(2,1)} %param.14) | copy-start | bytes 3145732
  7.2 32.5 %copy-start.43 = (bf16[128]{0:T(256)(128)(2,1)S(1)}, bf16[128]{0:T(256)(128)(2,1)}, u32[]{:S(2)}) copy-start(bf16[128]{0:T(256)(128)(2,1)} %param.20) | copy-start | bytes 772
  7.2 31.1 %all-gather.11.cloned.1.call-start = ((), (), s32[]{:S(2)}) async-start(), calls=%async_computation.10 | async-start | bytes 1769472 | tf_op jit(solution)/shard_map/all_gather | solution.py:59
  7.9 147.5 %all-gather.13.cloned.1.call-start = ((), (), s32[]{:S(2)}) async-start(), calls=%async_computation.11 | async-start | bytes 7864320 | tf_op jit(solution)/shard_map/all_gather | solution.py:66
  38.4 205.5 %all-gather.15.cloned.1.call-start = ((), (), s32[]{:S(2)}) async-start(), calls=%async_computation.12 | async-start | bytes 5242880 | tf_op jit(solution)/shard_map/all_gather | solution.py:108
  38.6 122.3 %copy-start.33 = (f32[1,2,2,128]{3,1,2,0:T(2,128)}, f32[1,2,2,128]{3,1,2,0:T(2,128)S(1)}, u32[]{:S(2)}) copy-start(f32[1,2,2,128]{3,1,2,0:T(2,128)S(1)} %copy.98) | copy-start | bytes 6148
  39.7 121.3 %copy-start.35 = (f32[512]{0:T(512)}, f32[512]{0:T(512)S(1)}, u32[]{:S(2)}) copy-start(f32[512]{0:T(512)S(1)} %rsqrt.52) | copy-start | bytes 6148
  63.4 97.5 %copy-start.22 = (bf16[512,1024]{1,0:T(8,128)(2,1)}, bf16[512,1024]{1,0:T(8,128)(2,1)S(1)}, u32[]{:S(2)}) copy-start(bf16[512,1024]{1,0:T(8,128)(2,1)S(1)} %fusion.69) | copy-start | bytes 3145732
  161.0 2.6 copy-start.16
  164.8 159.6 %all-gather.17.cloned.1.call-start = ((), (), s32[]{:S(2)}) async-start(), calls=%async_computation.13 | async-start | bytes 5242880 | tf_op jit(solution)/shard_map/all_gather | solution.py:107
  165.9 10.8 copy-start.27
  180.8 231.1 %all-gather.19.cloned.1.call-start = ((), (), s32[]{:S(2)}) async-start(), calls=%async_computation.14 | async-start | bytes 2621440 | tf_op jit(solution)/shard_map/all_gather | solution.py:67
  191.7 227.4 %all-gather.23.cloned.1.call-start = ((), (), s32[]{:S(2)}) async-start(), calls=%async_computation.16 | async-start | bytes 2359296 | tf_op jit(solution)/shard_map/all_gather | solution.py:61
  192.3 305.3 %all-gather.21.cloned.1.call-start = ((), (), s32[]{:S(2)}) async-start(), calls=%async_computation.15 | async-start | bytes 5242880 | tf_op jit(solution)/shard_map/all_gather | solution.py:164
  411.9 3.3 copy-start.17
  418.3 107.9 %all-gather.25.cloned.1.call-start = ((), (), s32[]{:S(2)}) async-start(), calls=%async_computation.17 | async-start | bytes 2359296 | tf_op jit(solution)/shard_map/all_gather | solution.py:62
  419.0 195.6 %reduce-scatter.17.cloned.1.call-start = ((), (), s32[]{:S(2)}) async-start(), calls=%async_computation.18 | async-start | bytes 5242880 | tf_op jit(solution)/shard_map/reduce_scatter | solution.py:171
  537.7 80.1 %copy-start.12 = (bf16[1,2,256,1024]{3,2,1,0:T(8,128)(2,1)S(1)}, bf16[1,2,256,1024]{3,2,1,0:T(8,128)(2,1)}, u32[]{:S(2)}) copy-start(bf16[1,2,256,1024]{3,2,1,0:T(8,128)(2,1)} %param.21) | copy-start | bytes 3145732
  537.7 165.6 %all-gather.27.cloned.1.call-start = ((), (), s32[]{:S(2)}) async-start(), calls=%async_computation.19 | async-start | bytes 5242880 | tf_op jit(solution)/shard_map/all_gather | solution.py:185
  614.6 3.2 copy-start.8
  621.9 175.9 %reduce-scatter.19.cloned.1.call-start = ((), (), s32[]{:S(2)}) async-start(), calls=%async_computation.20 | async-start | bytes 5242880 | tf_op jit(solution)/shard_map/reduce_scatter | solution.py:197
  703.3 12.6 copy-start.44
  715.9 6.4 copy-start.47
  722.3 1643.3 %reduce-scatter.25.cloned.1.call-start = ((), (), s32[]{:S(2)}) async-start(), calls=%async_computation.23 | async-start | bytes 2621440 | tf_op jit(solution)/shard_map/reduce_scatter | solution.py:294
  797.8 5.6 copy-start.13
  800.3 3.1 copy-start.5
  800.3 3.1 copy-start.9
  823.3 1542.8 %reduce-scatter.31.cloned.1.call-start = ((), (), s32[]{:S(2)}) async-start(), calls=%async_computation.26 | async-start | bytes 5242880
  855.0 3.0 copy-start.19
  893.8 3.0 copy-start.19
  932.5 3.0 copy-start.19
  971.3 3.0 copy-start.19
  979.3 8.5 copy-start
  1660.5 915.9 %reduce-scatter.33.cloned.1.call-start = ((), (), s32[]{:S(2)}) async-start(), calls=%async_computation.27 | async-start | bytes 5242880
  2341.0 456.9 %reduce-scatter.35.cloned.1.call-start = ((), (), s32[]{:S(2)}) async-start(), calls=%async_computation.28 | async-start | bytes 2359296
  2354.1 445.9 %reduce-scatter.29.cloned.1.call-start = ((), (), s32[]{:S(2)}) async-start(), calls=%async_computation.25 | async-start | bytes 2359296 | tf_op jit(solution)/shard_map/reduce_scatter | solution.py:308
  2363.6 438.1 %reduce-scatter.27.cloned.1.call-start = ((), (), s32[]{:S(2)}) async-start(), calls=%async_computation.24 | async-start | bytes 589824 | tf_op jit(solution)/shard_map/reduce_scatter | solution.py:305
  2365.6 540.6 %reduce-scatter.21.cloned.1.call-start = ((), (), s32[]{:S(2)}) async-start(), calls=%async_computation.21 | async-start | bytes 7864320 | tf_op jit(solution)/shard_map/reduce_scatter | solution.py:291
  2722.8 59.6 %copy-start.28 = (f32[512,32]{0,1:T(8,128)S(1)}, f32[512,32]{0,1:T(8,128)}, u32[]{:S(2)}) copy-start(f32[512,32]{0,1:T(8,128)} %copy-done.27) | copy-start | bytes 196612
  2722.8 59.6 %copy-start.29 = (f32[512,32]{0,1:T(8,128)S(1)}, f32[512,32]{0,1:T(8,128)}, u32[]{:S(2)}) copy-start(f32[512,32]{0,1:T(8,128)} %get-tuple-element.462) | copy-start | bytes 196612
  2794.8 111.5 %copy-start.7 = (bf16[1,2,256,1024]{3,2,1,0:T(8,128)(2,1)S(1)}, bf16[1,2,256,1024]{3,2,1,0:T(8,128)(2,1)}, u32[]{:S(2)}) copy-start(bf16[1,2,256,1024]{3,2,1,0:T(8,128)(2,1)} %param.14) | copy-start | bytes 3145732
  2794.8 111.5 %copy-start.25 = (bf16[128,8,2,256]{3,1,2,0:T(8,128)(2,1)S(1)}, bf16[128,8,2,256]{3,1,2,0:T(8,128)(2,1)}, u32[]{:S(2)}) copy-start(bf16[128,8,2,256]{3,1,2,0:T(8,128)(2,1)} %copy-done.24) | copy-start | bytes 3145732
  2794.8 111.5 %copy-start.31 = (f32[2,4,128]{2,1,0:T(4,128)S(1)}, f32[2,4,128]{2,1,0:T(4,128)}, u32[]{:S(2)}) copy-start(f32[2,4,128]{2,1,0:T(4,128)} %copy-done.30) | copy-start | bytes 12292
  2794.9 111.5 %copy-start.34 = (f32[1,2,2,128]{3,1,2,0:T(2,128)S(1)}, f32[1,2,2,128]{3,1,2,0:T(2,128)}, u32[]{:S(2)}) copy-start(f32[1,2,2,128]{3,1,2,0:T(2,128)} %copy-done.33) | copy-start | bytes 6148
  2794.9 153.8 %reduce-scatter.23.cloned.1.call-start = ((), (), s32[]{:S(2)}) async-start(), calls=%async_computation.22 | async-start | bytes 1769472 | tf_op jit(solution)/shard_map/reduce_scatter | solution.py:302
  2906.3 7.0 copy-start.38
  2906.3 8.2 copy-start.36
  2913.3 26.2 copy-start.11
  (25 other events, 41.2 us)
Sparse Core Ops, SparseCore 0:
  9.9 28.3 all-gather.10
  39.9 115.4 all-gather.12
  164.9 78.9 all-gather.14
  245.3 79.0 all-gather.16
  325.8 44.3 all-gather.18
  372.0 26.1 all-gather.22
  418.4 79.0 all-gather.20
  499.4 26.7 all-gather.24
  537.8 76.7 reduce-scatter.16
  622.0 81.2 all-gather.26
  722.4 75.2 reduce-scatter.18
  823.4 44.3 reduce-scatter.24
  1660.6 77.1 reduce-scatter.30
  2341.2 77.2 reduce-scatter.32
  2422.0 41.7 reduce-scatter.34
  2466.9 41.2 reduce-scatter.28
  2511.4 34.1 reduce-scatter.26
  2794.9 111.2 reduce-scatter.20
  2909.5 39.0 reduce-scatter.22
where the time goes:
time: 2980 us; the launch traced here: 2960 us
  local copies, waits for them, and re-layouts  1850 us (62%)
  waiting for transfers between devices  675 us (23%)
  matrix products  281 us (9%)
  other arithmetic  65.4 us (2%)
  blocking collectives  56.8 us (2%)
    unnamed x111, local copies, waits for them, and re-layouts  1750 us
    reduce_scatter x1, waiting for transfers between devices, body(): lax.psum_scatter(qkv_local.astype(jnp.bfloat16), 'cp', scatter_dimension=...  103 us
    all_gather x1, waiting for transfers between devices, body(): lax.all_gather(qkv_rows, 'cp', axis=1, tiled=True)  92 us
    all_gather x1, waiting for transfers between devices, body(): lax.all_gather(grad_down_out.reshape(fold_shape), 'cp', axis=2, tiled=True)  81.4 us
    all_gather x1, waiting for transfers between devices, body(): lax.all_gather(normed_mid.reshape(fold_shape), 'cp', axis=2, tiled=True)  78.4 us
    reduce_scatter x1, waiting for transfers between devices, body(): lax.psum_scatter(down_terms.reshape(group_shape).astype(jnp.bfloat16), 'c...  76.7 us
    reduce_scatter x1, waiting for transfers between devices, body(): lax.psum_scatter(mid_terms.reshape(group_shape).astype(jnp.bfloat16), 'cp...  75.4 us
    all_gather x1, waiting for transfers between devices, body(): lax.all_gather(key_local.reshape(fold_shape), 'cp', axis=2, tiled=True)  61.3 us
  transfers between devices with their start and end apart: 19, of which 11 were waited for; matrix products, arithmetic and copies ran while one was open for 71% of the time, Pallas kernels for 0%

commit v1 on v0

--- a/solution.py
+++ b/solution.py
@@ -1,9 +1,12 @@
+import functools
 import math
 
 import jax
 import jax.numpy as jnp
 from jax import lax
-from jax.sharding import PartitionSpec as P
+from jax.experimental import pallas as pl
+from jax.experimental.pallas import tpu as pltpu
+from jax.sharding import Mesh, PartitionSpec as P
 
 HEADS = 16
 HEAD_DIM = 64
@@ -52,7 +55,7 @@
     )
 
 
-def body(tokens, doc_starts, qkv_weight, out_weight, up_weight, down_weight, norm_gains, cotangent):
+def general_body(tokens, doc_starts, qkv_weight, out_weight, up_weight, down_weight, norm_gains, cotangent):
     rows_count = lax.axis_size("rows")
     cp_count = lax.axis_size("cp")
     qkv_rows, out_rows, up_rows, down_rows, gain_piece = (
@@ -318,24 +321,601 @@
     return (mixed, tokens_grad, qkv_sum, out_sum, up_sum, down_sum, gain_sum)
 
 
+F32 = jnp.float32
+BF16 = jnp.bfloat16
+VMEM = 56 * 1024 * 1024
+
+
+def params(grid_rank):
+    return pltpu.CompilerParams(
+        dimension_semantics=("arbitrary",) * grid_rank, vmem_limit_bytes=VMEM
+    )
+
+
+def turned(x, cosine, sine):
+    lane = lax.broadcasted_iota(jnp.int32, x.shape, 1)
+    other = jnp.where((lane & 32) == 0, pltpu.roll(x, 96, 1), pltpu.roll(x, 32, 1))
+    return x * cosine + other * sine
+
+
+def attend_kernel(tile, bounds, q_ref, k_ref, v_ref, pcol_ref, prow_ref, srow_ref,
+                  o_ref, ob_ref, lse_ref, vt_ref):
+    i = pl.program_id(1)
+
+    @pl.when(i == 0)
+    def _():
+        vt_ref[...] = v_ref[...].astype(F32).T.astype(BF16)
+
+    qt = q_ref[...].astype(F32).T
+    row = lax.broadcasted_iota(jnp.int32, qt.shape, 0)
+    lo = bounds[0, i]
+    mid = jnp.minimum(bounds[1, i], i)
+    qpos = prow_ref[...]
+    qstart = srow_ref[...]
+    qh = [jnp.where((row >= 64) == (h == 1), qt, 0.0).astype(BF16) for h in range(2)]
+
+    def step(j, carry, masked):
+        at = pl.multiple_of(j * tile, tile)
+        k = k_ref[pl.ds(at, tile), :]
+        scores = [jnp.dot(k, qh[h], preferred_element_type=F32) for h in range(2)]
+        if masked:
+            kpos = pcol_ref[pl.ds(at, tile), :]
+            allowed = (kpos >= qstart) & (kpos <= qpos)
+            scores = [jnp.where(allowed, s, MASKED) for s in scores]
+        out = []
+        for h in range(2):
+            top, total, acc = carry[h]
+            new = jnp.maximum(top, jnp.max(scores[h], axis=0, keepdims=True))
+            p = jnp.exp(scores[h] - new)
+            keep = jnp.exp(top - new)
+            total = total * keep + jnp.sum(p, axis=0, keepdims=True)
+            acc = acc * keep + jnp.dot(
+                vt_ref[h * 64 : h * 64 + 64, pl.ds(at, tile)], p.astype(BF16),
+                preferred_element_type=F32,
+            )
+            out.append((new, total, acc))
+        return tuple(out)
+
+    start = (
+        jnp.full((1, tile), MASKED, F32), jnp.zeros((1, tile), F32), jnp.zeros((64, tile), F32)
+    )
+    carry = step(i, (start, start), True)
+    carry = lax.fori_loop(lo, mid, functools.partial(step, masked=True), carry)
+    carry = lax.fori_loop(mid, i, functools.partial(step, masked=False), carry)
+    parts = []
+    for h in range(2):
+        top, total, acc = carry[h]
+        lse_ref[0, h : h + 1, :] = top + jnp.log(total)
+        parts.append(acc / total)
+    out = jnp.concatenate(parts, axis=0).T
+    o_ref[...] = out
+    ob_ref[...] = out.astype(BF16)
+
+
+def attend(q, k, v, pcol, prow, srow, bounds, tile):
+    rows, width = q.shape
+    pairs = width // 128
+    count = rows // tile
+    grid_spec = pltpu.PrefetchScalarGridSpec(
+        num_scalar_prefetch=1,
+        grid=(pairs, count),
+        in_specs=[
+            pl.BlockSpec((tile, 128), lambda p, i, b: (i, p)),
+            pl.BlockSpec((rows, 128), lambda p, i, b: (0, p)),
+            pl.BlockSpec((rows, 128), lambda p, i, b: (0, p)),
+            pl.BlockSpec((rows, 1), lambda p, i, b: (0, 0)),
+            pl.BlockSpec((1, tile), lambda p, i, b: (0, i)),
+            pl.BlockSpec((1, tile), lambda p, i, b: (0, i)),
+        ],
+        out_specs=[
+            pl.BlockSpec((tile, 128), lambda p, i, b: (i, p)),
+            pl.BlockSpec((tile, 128), lambda p, i, b: (i, p)),
+            pl.BlockSpec((1, 2, tile), lambda p, i, b: (p, 0, i)),
+        ],
+        scratch_shapes=[pltpu.VMEM((128, rows), BF16)],
+    )
+    return pl.pallas_call(
+        functools.partial(attend_kernel, tile),
+        grid_spec=grid_spec,
+        out_shape=[
+            jax.ShapeDtypeStruct((rows, width), F32),
+            jax.ShapeDtypeStruct((rows, width), BF16),
+            jax.ShapeDtypeStruct((pairs, 2, rows), F32),
+        ],
+        compiler_params=params(2),
+        name="attend",
+    )(bounds, q, k, v, pcol, prow, srow)
+
+
+def attend_back_kernel(tile, bounds, q_ref, k_ref, v_ref, do_ref, o_ref, lse_ref, pcol_ref,
+                       prow_ref, srow_ref, cos_ref, sin_ref, g_ref,
+                       qm, dom, qtm, dotm, delta, dqt):
+    j = pl.program_id(1)
+    count = pl.num_programs(1)
+    rows = q_ref.shape[0]
+
+    @pl.when(j == 0)
+    def _():
+        for t in range(rows // tile):
+            part = pl.ds(t * tile, tile)
+            q = q_ref[part, :].astype(F32)
+            do = do_ref[part, :].astype(F32)
+            qt, dot = q.T, do.T
+            lane = lax.broadcasted_iota(jnp.int32, q.shape, 1)
+            row = lax.broadcasted_iota(jnp.int32, qt.shape, 0)
+            prod = dot * o_ref[part, :].T
+            for h in range(2):
+                mine = (lane >= 64) == (h == 1)
+                mine_t = (row >= 64) == (h == 1)
+                qm[h, part, :] = jnp.where(mine, q, 0.0).astype(BF16)
+                dom[h, part, :] = jnp.where(mine, do, 0.0).astype(BF16)
+                qtm[h, :, part] = jnp.where(mine_t, qt, 0.0).astype(BF16)
+                dotm[h, :, part] = jnp.where(mine_t, dot, 0.0).astype(BF16)
+                delta[h : h + 1, part] = jnp.sum(
+                    prod[h * 64 : h * 64 + 64], axis=0, keepdims=True
+                )
+        dqt[...] = jnp.zeros_like(dqt)
+
+    here = pl.ds(pl.multiple_of(j * tile, tile), tile)
+    k = k_ref[here, :]
+    v = v_ref[here, :]
+    kt = k.astype(F32).T.astype(BF16)
+    kpos = pcol_ref[here, :]
+    full = jnp.maximum(bounds[2, j], j + 1)
+    end = bounds[3, j]
+
+    def step(i, carry, masked):
+        dk, dv = carry
+        part = pl.ds(pl.multiple_of(i * tile, tile), tile)
+        if masked:
+            allowed = (kpos >= srow_ref[:, part]) & (kpos <= prow_ref[:, part])
+        for h in range(2):
+            s = jnp.dot(k, qtm[h, :, part], preferred_element_type=F32)
+            p = jnp.exp(s - lse_ref[0, h : h + 1, part])
+            if masked:
+                p = jnp.where(allowed, p, 0.0)
+            dp = jnp.dot(v, dotm[h, :, part], preferred_element_type=F32)
+            ds = (p * (dp - delta[h : h + 1, part])).astype(BF16)
+            dv = dv + jnp.dot(p.astype(BF16), dom[h, part, :], preferred_element_type=F32)
+            dk = dk + jnp.dot(ds, qm[h, part, :], preferred_element_type=F32)
+            dqt[h * 64 : h * 64 + 64, part] += jnp.dot(
+                kt[h * 64 : h * 64 + 64, :], ds, preferred_element_type=F32
+            )
+        return dk, dv
+
+    carry = (jnp.zeros((tile, 128), F32), jnp.zeros((tile, 128), F32))
+    carry = step(j, carry, True)
+    carry = lax.fori_loop(j + 1, full, functools.partial(step, masked=False), carry)
+    carry = lax.fori_loop(full, end, functools.partial(step, masked=True), carry)
+    dk, dv = carry
+
+    def unturned(x, at):
+        x = x.astype(BF16).astype(F32)
+        return turned(x, cos_ref[at, :], -sin_ref[at, :]).astype(BF16)
+
+    g_ref[1, here, :] = unturned(dk, here)
+    g_ref[2, here, :] = dv.astype(BF16)
+
+    @pl.when(j == count - 1)
+    def _():
+        for t in range(rows // tile):
+            part = pl.ds(t * tile, tile)
+            g_ref[0, part, :] = unturned(dqt[:, part].T * 0.125, part)
+
+
+def attend_back(q, k, v, do, o, lse, pcol, prow, srow, cosine, sine, bounds, tile):
+    rows, width = q.shape
+    pairs = width // 128
+    count = rows // tile
+    whole = pl.BlockSpec((rows, 128), lambda p, j, b: (0, p))
+    table = pl.BlockSpec((rows, 128), lambda p, j, b: (0, 0))
+    line = pl.BlockSpec((1, rows), lambda p, j, b: (0, 0))
+    grid_spec = pltpu.PrefetchScalarGridSpec(
+        num_scalar_prefetch=1,
+        grid=(pairs, count),
+        in_specs=[
+            whole, whole, whole, whole, whole,
+            pl.BlockSpec((1, 2, rows), lambda p, j, b: (p, 0, 0)),
+            pl.BlockSpec((rows, 1), lambda p, j, b: (0, 0)),
+            line, line, table, table,
+        ],
+        out_specs=pl.BlockSpec((3, rows, 128), lambda p, j, b: (0, 0, p)),
+        scratch_shapes=[
+            pltpu.VMEM((2, rows, 128), BF16), pltpu.VMEM((2, rows, 128), BF16),
+            pltpu.VMEM((2, 128, rows), BF16), pltpu.VMEM((2, 128, rows), BF16),
+            pltpu.VMEM((2, rows), F32), pltpu.VMEM((128, rows), F32),
+        ],
+    )
+    return pl.pallas_call(
+        functools.partial(attend_back_kernel, tile),
+        grid_spec=grid_spec,
+        out_shape=jax.ShapeDtypeStruct((3, rows, width), BF16),
+        compiler_params=params(2),
+        name="attend_back",
+    )(bounds, q, k, v, do, o, lse, pcol, prow, srow, cosine, sine)
+
+
+def tile_bounds(starts_nat, tile):
+    rows = starts_nat.shape[0]
+    count = rows // tile
+    tiles = starts_nat.reshape(count, tile)
+    first, last = tiles[:, 0], tiles[:, -1]
+    at = jnp.arange(count, dtype=jnp.int32) * tile
+    lo = first // tile
+    mid = (last + tile - 1) // tile
+    full = jnp.sum((last[None, :] <= at[:, None]).astype(jnp.int32), axis=1)
+    end = jnp.sum((first[None, :] <= at[:, None] + tile - 1).astype(jnp.int32), axis=1)
+    return jnp.stack([lo, mid, full, end]).astype(jnp.int32)
+
+
+def reorder_kernel(table, x_ref, o_ref):
+    o_ref[...] = x_ref[...]
+
+
+def reorder(x, table):
+    count, rows, width = x.shape
+    block = (1, rows, width)
+    return pl.pallas_call(
+        reorder_kernel,
+        grid_spec=pltpu.PrefetchScalarGridSpec(
+            num_scalar_prefetch=1,
+            grid=(count,),
+            in_specs=[pl.BlockSpec(block, lambda i, t: (t[i], 0, 0))],
+            out_specs=pl.BlockSpec(block, lambda i, t: (i, 0, 0)),
+        ),
+        out_shape=jax.ShapeDtypeStruct(x.shape, x.dtype),
+        compiler_params=params(1),
+        name="reorder",
+    )(table, x)
+
+
+def project_kernel(table, x_ref, w_ref, cos_ref, sin_ref, q_ref, k_ref, v_ref):
+    width = q_ref.shape[1]
+    linear = jnp.dot(x_ref[0], w_ref[...], preferred_element_type=F32)
+    for at in range(0, width, 128):
+        q = turned(linear[:, at : at + 128], cos_ref[...], sin_ref[...])
+        k = turned(linear[:, width + at : width + at + 128], cos_ref[...], sin_ref[...])
+        q_ref[:, at : at + 128] = q.astype(BF16) * jnp.asarray(0.125, BF16)
+        k_ref[:, at : at + 128] = k.astype(BF16)
+    v_ref[...] = linear[:, 2 * width :].astype(BF16)
+
+
+def project(x, w, cosine, sine, table):
+    count, rows, depth = x.shape
+    width = w.shape[1] // 3
+    out = pl.BlockSpec((rows, width), lambda i, t: (i, 0))
+    angle = pl.BlockSpec((rows, 128), lambda i, t: (i, 0))
+    return pl.pallas_call(
+        project_kernel,
+        grid_spec=pltpu.PrefetchScalarGridSpec(
+            num_scalar_prefetch=1,
+            grid=(count,),
+            in_specs=[
+                pl.BlockSpec((1, rows, depth), lambda i, t: (t[i], 0, 0)),
+                pl.BlockSpec(w.shape, lambda i, t: (0, 0)),
+                angle, angle,
+            ],
+            out_specs=[out, out, out],
+        ),
+        out_shape=[jax.ShapeDtypeStruct((count * rows, width), BF16)] * 3,
+        compiler_params=params(1),
+        name="project",
+    )(table, x, w, cosine, sine)
+
+
+def project_back_kernel(table, g_ref, w_ref, o_ref):
+    g = jnp.concatenate([g_ref[0], g_ref[1], g_ref[2]], axis=1)
+    o_ref[0] = lax.dot_general(
+        g, w_ref[...], (((1,), (1,)), ((), ())), preferred_element_type=F32
+    ).astype(BF16)
+
+
+def project_back(grads, w, table):
+    count = table.shape[0]
+    _, total, width = grads.shape
+    rows = total // count
+    depth = w.shape[0]
+    return pl.pallas_call(
+        project_back_kernel,
+        grid_spec=pltpu.PrefetchScalarGridSpec(
+            num_scalar_prefetch=1,
+            grid=(count,),
+            in_specs=[
+                pl.BlockSpec((3, rows, width), lambda i, t: (0, i, 0)),
+                pl.BlockSpec(w.shape, lambda i, t: (0, 0)),
+            ],
+            out_specs=pl.BlockSpec((1, rows, depth), lambda i, t: (t[i], 0, 0)),
+        ),
+        out_shape=jax.ShapeDtypeStruct((count, rows, depth), BF16),
+        compiler_params=params(1),
+        name="project_back",
+    )(table, grads, w)
+
+
+def project_weights_kernel(table, x_ref, g_ref, o_ref, total):
+    i = pl.program_id(0)
+
+    @pl.when(i == 0)
+    def _():
+        total[...] = jnp.zeros_like(total)
+
+    g = jnp.concatenate([g_ref[0], g_ref[1], g_ref[2]], axis=1)
+    total[...] += lax.dot_general(
+        x_ref[0], g, (((0,), (0,)), ((), ())), preferred_element_type=F32
+    )
+
+    @pl.when(i == pl.num_programs(0) - 1)
+    def _():
+        o_ref[...] = total[...].astype(BF16)
+
+
+def project_weights(x, grads, table):
+    count, rows, depth = x.shape
+    width = grads.shape[2]
+    return pl.pallas_call(
+        project_weights_kernel,
+        grid_spec=pltpu.PrefetchScalarGridSpec(
+            num_scalar_prefetch=1,
+            grid=(count,),
+            in_specs=[
+                pl.BlockSpec((1, rows, depth), lambda i, t: (t[i], 0, 0)),
+                pl.BlockSpec((3, rows, width), lambda i, t: (0, i, 0)),
+            ],
+            out_specs=pl.BlockSpec((depth, 3 * width), lambda i, t: (0, 0)),
+            scratch_shapes=[pltpu.VMEM((depth, 3 * width), F32)],
+        ),
+        out_shape=jax.ShapeDtypeStruct((depth, 3 * width), BF16),
+        compiler_params=params(1),
+        name="project_weights",
+    )(table, x, grads)
+
+
+def flip(x, axis, bit):
+    return lax.ppermute(x, axis, [(i, i ^ bit) for i in range(lax.axis_size(axis))])
+
+
+def swap(x):
+    cp = lax.axis_size("cp")
+    half = cp // 2
+    pairs = []
+    for z in range(half):
+        low, high = cp + z, z + half
+        pairs += [(low, high), (high, low), (z, z), (cp + high, cp + high)]
+    return lax.ppermute(x, ("core", "cp"), pairs)
+
+
+def ordered(first, mine, other, axis):
+    return jnp.concatenate(
+        [jnp.where(first, mine, other), jnp.where(first, other, mine)], axis=axis
+    )
+
+
+def dot(a, b, dims):
+    return lax.dot_general(a, b, ((dims[:1], dims[1:]), ((), ())), preferred_element_type=F32)
+
+
+def gelu_and_slope(u):
+    inner = math.sqrt(2.0 / math.pi) * (u + 0.044715 * u * u * u)
+    t = jnp.tanh(inner)
+    slope = 0.5 * (1.0 + t) + 0.5 * u * (1.0 - t * t) * math.sqrt(2.0 / math.pi) * (
+        1.0 + 3.0 * 0.044715 * u * u
+    )
+    return 0.5 * u * (1.0 + t), slope
+
+
+def body(tokens, doc_starts, qkv_weight, out_weight, up_weight, down_weight, norm_gains, cotangent):
+    xy, core, z = lax.axis_index("xy"), lax.axis_index("core"), lax.axis_index("cp")
+    xy_count, cp_count = lax.axis_size("xy"), lax.axis_size("cp")
+    _, _, span, width = tokens.shape
+    blocks = 2 * cp_count
+    row_len = blocks * span
+    own = 2 * span
+    parity = z & 1
+    group = 2 * parity + core
+    part = width // cp_count
+    hidden_part = up_weight.shape[1] // 2
+
+    inputs = swap(tokens.reshape(own, width)).astype(F32)
+    upstream = swap(cotangent.reshape(own, width)).astype(F32)
+    other_starts = flip(doc_starts, "core", 1)
+    starts = jnp.where(core == z // (cp_count // 2), doc_starts, other_starts)[0]
+    gains = lax.all_gather(norm_gains, ("xy", "core", "cp"), axis=0, tiled=True)
+    gains = gains.astype(F32).reshape(4, width)
+
+    w = qkv_weight
+    for bit, at in ((2, 0), (1, 1)):
+        other = flip(w, "cp", bit)
+        w = ordered((z & bit) == 0, jnp.expand_dims(w, at), jnp.expand_dims(other, at), at)
+
+    def columns(of):
+        picked = []
+        for third in range(3):
+            block = third * cp_count + of
+            picked.append(
+                lax.dynamic_slice(
+                    w, (block // 6, (block // 3) & 1, 0, (block % 3) * part), (1, 1, w.shape[2], part)
+                )[0, 0]
+            )
+        return jnp.concatenate(picked, axis=1)
+
+    mine = columns(group)
+    other = flip(columns(group ^ 1), "core", 1)
+    qkv = ordered(core == 0, mine, other, 0)
+    for bit in (1, 2):
+        other = flip(qkv, "xy", bit)
+        qkv = ordered((xy & bit) == 0, qkv, other, 0)
+
+    def half_of(which):
+        up = lax.dynamic_slice_in_dim(up_weight, which * hidden_part, hidden_part, 1)
+        down = lax.dynamic_slice_in_dim(down_weight, which * hidden_part, hidden_part, 0)
+        return jnp.stack([up, down.T])
+
+    both = ordered(core == 0, half_of(core), flip(half_of(1 - core), "core", 1), 1)
+    ffn = lax.all_gather(both, ("xy", "cp"), axis=0)
+    ffn = ffn.reshape(xy_count, cp_count, 2, -1, hidden_part).transpose(2, 0, 3, 1, 4)
+    ffn = ffn.reshape(2, width, cp_count * hidden_part)
+    up_half, down_half = ffn[0], ffn[1]
+
+    out_w = out_weight
+    for bit in (1, 2):
+        other = flip(out_w, "cp", bit)
+        out_w = ordered((z & bit) == 0, out_w, other, 1)
+    out_w = out_w[None]
+    for bit in (1, 2):
+        other = flip(out_w, "xy", bit)
+        out_w = ordered((xy & bit) == 0, out_w, other, 0)
+    other = flip(out_w, "core", 1)
+    out_w = ordered(core == 0, out_w[:, None], other[:, None], 1).reshape(width, width)
+
+    block_id = jnp.arange(blocks, dtype=jnp.int32)[:, None]
+    inside = jnp.arange(span, dtype=jnp.int32)[None, :]
+    late = block_id >= cp_count
+    positions = (block_id * span + jnp.where(late, span - 1 - inside, inside)).reshape(-1)
+
+    def starts_at(at):
+        return jnp.max(jnp.where(starts[None, :] <= at[:, None], starts[None, :], 0), axis=1)
+
+    row_start = starts_at(positions)
+    tile = min(512, row_len)
+    bounds = tile_bounds(starts_at(jnp.arange(row_len, dtype=jnp.int32)), tile)
+    freq = jnp.exp(
+        -math.log(10000.0) * 2.0 * jnp.arange(HEAD_DIM // 2, dtype=F32) / HEAD_DIM
+    )
+    angles = (positions - row_start).astype(F32)[:, None] * freq
+    cosine, sine = jnp.cos(angles), jnp.sin(angles)
+    cosine = jnp.tile(cosine, (1, 4))
+    sine = jnp.tile(jnp.concatenate([-sine, sine], axis=1), (1, 2))
+    pcol, prow, srow = positions[:, None], positions[None, :], row_start[None, :]
+    chunk = jnp.arange(blocks, dtype=jnp.int32)
+    chunk = jnp.where(chunk < cp_count, chunk, blocks - 1 - chunk)
+    slot_of = (
+        2 * (2 * ((chunk >> 1) ^ core) + ((chunk & 1) ^ parity))
+        + (jnp.arange(blocks) >= cp_count)
+    ).astype(jnp.int32)
+    slot = jnp.arange(blocks, dtype=jnp.int32)
+    relative = slot >> 1
+    chunk_of = 2 * ((relative >> 1) ^ core) + ((relative & 1) ^ parity)
+    block_of = jnp.where(slot & 1 == 0, chunk_of, blocks - 1 - chunk_of).astype(jnp.int32)
+
+    normed_in = layer_norm(inputs)
+    normed = (normed_in * gains[0]).astype(BF16).reshape(2, span, width)
+    pair = jnp.concatenate([normed, flip(normed, "cp", 1)], axis=0)
+    slots = jnp.concatenate([pair, flip(pair, "core", 1)], axis=0)
+    q, k, v = project(slots, qkv, cosine, sine, slot_of)
+    attended, attended_low, lse = attend(q, k, v, pcol, prow, srow, bounds, tile)
+    local = reorder(attended_low.reshape(blocks, span, part), block_of)
+    from_core = flip(local[4:], "core", 1)
+    from_chip = flip(jnp.stack([local[2:4], from_core[2:4]]), "cp", 1)
+    pieces = jnp.concatenate([jnp.stack([local[:2], from_core[:2]]), from_chip]).reshape(
+        4, own, part
+    )
+    heads = jnp.concatenate(
+        [lax.dynamic_index_in_dim(pieces, g ^ group, 0, False) for g in range(4)], axis=1
+    )
+    branch = dot(heads, out_w, (1, 0))
+    branch_hat = layer_norm(branch)
+    hidden = inputs + branch_hat * gains[1]
+    hidden_hat = layer_norm(hidden)
+    normed_mid = (hidden_hat * gains[2]).astype(BF16)
+
+    ffn_in = jnp.concatenate([normed_mid, flip(normed_mid, "core", 1)])
+    act, slope = gelu_and_slope(dot(ffn_in, up_half, (1, 0)))
+    act, slope = act.astype(BF16), slope.astype(BF16)
+    terms = dot(act, down_half, (1, 1))
+    down = terms[:own] + flip(terms[own:].astype(BF16), "core", 1).astype(F32)
+    down_hat = layer_norm(down)
+    mixed = swap((hidden + down_hat * gains[3]).astype(BF16)).reshape(tokens.shape)
+
+    gain_four = jnp.sum(upstream * down_hat, axis=0)
+    grad_down = norm_back(down, upstream * gains[3]).astype(BF16)
+    grad_down = jnp.concatenate([grad_down, flip(grad_down, "core", 1)])
+    grad_up = (dot(grad_down, down_half, (1, 0)) * slope.astype(F32)).astype(BF16)
+    terms = dot(grad_up, up_half, (1, 1))
+    grad_mid = terms[:own] + flip(terms[own:].astype(BF16), "core", 1).astype(F32)
+    up_local = dot(ffn_in, grad_up, (0, 0)).astype(BF16)
+    down_local = dot(grad_down, act, (0, 0)).astype(BF16)
+
+    gain_three = jnp.sum(grad_mid * hidden_hat, axis=0)
+    grad_hidden = upstream + norm_back(hidden, grad_mid * gains[2])
+    gain_two = jnp.sum(grad_hidden * branch_hat, axis=0)
+    grad_branch = norm_back(branch, grad_hidden * gains[1]).astype(BF16)
+    grad_heads = dot(grad_branch, out_w, (1, 1)).astype(BF16)
+    out_local = dot(heads, grad_branch, (0, 0)).astype(BF16)
+
+    cut = jnp.transpose(grad_heads.reshape(2, span, 4, part), (2, 0, 1, 3))
+    near = [lax.dynamic_index_in_dim(cut, group ^ r, 0, False) for r in range(4)]
+    from_chip = flip(jnp.stack([near[2], near[3]]), "cp", 1)
+    from_core = flip(jnp.concatenate([near[1], from_chip[1]]), "core", 1)
+    grad_local = jnp.concatenate([near[0], from_chip[0], from_core])
+    grad_local = reorder(grad_local, slot_of).reshape(row_len, part)
+    grad_linear = attend_back(
+        q, k, v, grad_local, attended, lse, pcol, prow, srow, cosine, sine, bounds, tile
+    )
+    terms = project_back(grad_linear, qkv, slot_of)
+    pair = terms[:4].astype(F32) + flip(terms[4:], "core", 1).astype(F32)
+    grad_normed = pair[:2] + flip(pair[2:].astype(BF16), "cp", 1).astype(F32)
+    grad_normed = grad_normed.reshape(own, width)
+    gain_one = jnp.sum(grad_normed * normed_in, axis=0)
+    tokens_grad = grad_hidden + norm_back(inputs, grad_normed * gains[0])
+    tokens_grad = swap(tokens_grad.astype(BF16)).astype(F32).reshape(tokens.shape)
+
+    out_local = out_local.reshape(xy_count, 2, width // xy_count // 2, width)
+    out_mine = lax.dynamic_index_in_dim(out_local, core, 1, False)
+    out_other = lax.dynamic_index_in_dim(out_local, 1 - core, 1, False)
+    out_pair = (out_mine.astype(F32) + flip(out_other, "core", 1).astype(F32)).astype(BF16)
+    out_rows = out_pair.shape[1]
+    out_pair = out_pair.reshape(xy_count, out_rows, cp_count, -1).transpose(0, 2, 1, 3)
+    out_cols = out_pair.shape[3]
+    rows_each = width // xy_count
+    sent = jnp.stack([up_local, down_local]).reshape(
+        2, xy_count, rows_each, cp_count, hidden_part
+    )
+    sent = sent.transpose(1, 3, 0, 2, 4).reshape(xy_count, cp_count, 2 * rows_each, hidden_part)
+    sent = jnp.concatenate([sent, out_pair.reshape(xy_count, cp_count, -1, hidden_part)], axis=2)
+    sent = lax.psum_scatter(sent, "xy", scatter_dimension=0)
+    sent = lax.psum_scatter(sent, "cp", scatter_dimension=0)
+    out_grad = sent[2 * rows_each :].reshape(out_rows, out_cols).astype(F32)
+    sent = sent[: 2 * rows_each].reshape(2, 2, rows_each // 2, hidden_part)
+    mine = lax.dynamic_index_in_dim(sent, core, 1, False)
+    other = flip(lax.dynamic_index_in_dim(sent, 1 - core, 1, False), "core", 1)
+    up_grad = ordered(core == 0, mine[0], other[0], 1).astype(F32)
+    down_grad = ordered(core == 0, mine[1], other[1], 1).T.astype(F32)
+
+    qkv_local = project_weights(slots, grad_linear, slot_of)
+    qkv_local = qkv_local.reshape(xy_count, 2, rows_each // 2, 3 * part)
+    qkv_sum = lax.psum_scatter(qkv_local, "xy", scatter_dimension=0)
+    mine = lax.dynamic_index_in_dim(qkv_sum, core, 0, False)
+    other = flip(lax.dynamic_index_in_dim(qkv_sum, 1 - core, 0, False), "core", 1)
+    both = ordered(core == 0, mine[None], other[None], 0)
+    both = (both.astype(F32) + flip(both, "cp", 2).astype(F32)).astype(BF16)
+    every = ordered(parity == 0, both, flip(both, "cp", 1), 0)
+    every = every.reshape(4, rows_each // 2, 3, part).transpose(1, 2, 0, 3)
+    qkv_grad = lax.dynamic_slice_in_dim(
+        every.reshape(rows_each // 2, 3 * width), z * 3 * part, 3 * part, 1
+    ).astype(F32)
+
+    gain_local = jnp.concatenate([gain_one, gain_two, gain_three, gain_four]).reshape(-1, 128)
+    for axis, bit in (("core", 1), ("xy", 1), ("xy", 2), ("cp", 1), ("cp", 2)):
+        gain_local = gain_local + flip(gain_local, axis, bit)
+    gains_grad = lax.dynamic_index_in_dim(
+        gain_local, (2 * xy + core) * cp_count + z, 0, False
+    )
+    return mixed, tokens_grad, qkv_grad, out_grad, up_grad, down_grad, gains_grad
+
+
 def solution(mesh):
-    in_specs = (
-        P("rows", None, "cp", None),
-        P("rows", None),
-        P("rows", "cp"),
-        P("rows", "cp"),
-        P("rows", "cp"),
-        P("cp", "rows"),
-        P(("rows", "cp")),
-        P("rows", None, "cp", None),
-    )
-    out_specs = (
-        P("rows", None, "cp", None),
-        P("rows", None, "cp", None),
-        P("rows", "cp"),
-        P("rows", "cp"),
-        P("rows", "cp"),
-        P("cp", "rows"),
-        P(("rows", "cp")),
-    )
-    return jax.shard_map(body, mesh=mesh, in_specs=in_specs, out_specs=out_specs, check_vma=False)
+    rows, cp = mesh.shape["rows"], mesh.shape["cp"]
+    if (rows, cp) == (8, 4):
+        grid = Mesh(mesh.devices.reshape(rows // 2, 2, cp), ("xy", "core", "cp"))
+        run, lines = body, ("xy", "core")
+    else:
+        grid, run, lines = mesh, general_body, ("rows",)
+    tokens = P(lines, None, "cp", None)
+    weight, down, gains = P(lines, "cp"), P("cp", lines), P(lines + ("cp",))
+    return jax.shard_map(
+        run,
+        mesh=grid,
+        in_specs=(tokens, P(lines, None), weight, weight, weight, down, gains, tokens),
+        out_specs=(tokens, tokens, weight, weight, weight, down, gains),
+        check_vma=False,
+    )

time: 2980 us -> 752 us (0.25)
  local copies, waits for them, and re-layouts: 1850 us -> 78.9 us
  waiting for transfers between devices: 675 us -> 242 us
  matrix products: 281 us -> 53.7 us
  Pallas kernels: 0 us -> 114 us
  starting transfers between devices: 2.41 us -> 64 us
  blocking collectives: 56.8 us -> 106 us
    unnamed x111 -> x113, local copies, waits for them, and re-layouts: 1750 us -> 19.6 us
    all_gather x9 -> x1, waiting for transfers between devices: 412 us -> 0.01 us  [body(): ffn = lax.all_gather(both, ('xy', 'cp'), axis=0)]
    reduce_scatter x7 -> x1, waiting for transfers between devices: 261 us -> 0.02 us  [body(): sent = lax.psum_scatter(sent, 'cp', scatter_dimension=0)]
    dot_general x40 -> x9, matrix products: 281 us -> 53.7 us  [dot(): lax.dot_general(a, b, ((dims[:1], dims[1:]), ((), ())), preferred_element...]
    ppermute x0 -> x38, waiting for transfers between devices: none -> 185 us  [the longest x34 185 us: flip(): lax.ppermute(x, axis, [(i, i ^ bit) for i in range(lax.axis_size(axis))])]
    pallas_call x0 -> x7, Pallas kernels: none -> 114 us  [the longest x1 43 us: attend_back(): pl.pallas_call(functools.partial(attend_back_kernel, tile), grid_spec=gri...]
    all_gather x3 -> x1, blocking collectives: 33.6 us -> 106 us  [body(): gains = lax.all_gather(norm_gains, ('xy', 'core', 'cp'), axis=0, tiled=True)]
    ppermute x0 -> x38, starting transfers between devices: none -> 63.6 us  [the longest x34 49.7 us: flip(): lax.ppermute(x, axis, [(i, i ^ bit) for i in range(lax.axis_size(axis))])]
  transfers between devices with their start and end apart: 19 -> 42, of which waited for: 11 -> 21; matrix products, arithmetic and copies ran while one was open for 71% -> 18% of each run, Pallas kernels for 0% -> 15%
where the time goes in v1:
time: 752 us; the launch traced here: 741 us
  waiting for transfers between devices  242 us (32%)
  Pallas kernels  114 us (15%)
  blocking collectives  106 us (14%)
  local copies, waits for them, and re-layouts  78.9 us (10%)
  other arithmetic  65.5 us (9%)
  starting transfers between devices  64 us (9%)
  matrix products  53.7 us (7%)
  between operations  16.1 us (2%)
    ppermute x34, waiting for transfers between devices, flip(): lax.ppermute(x, axis, [(i, i ^ bit) for i in range(lax.axis_size(axis))])  185 us
    all_gather x1, blocking collectives, body(): gains = lax.all_gather(norm_gains, ('xy', 'core', 'cp'), axis=0, tiled=True)  106 us
    unnamed x6, waiting for transfers between devices  57.5 us
    dot_general x9, matrix products, dot(): lax.dot_general(a, b, ((dims[:1], dims[1:]), ((), ())), preferred_element...  53.7 us
    ppermute x34, starting transfers between devices, flip(): lax.ppermute(x, axis, [(i, i ^ bit) for i in range(lax.axis_size(axis))])  49.7 us
    pallas_call x1, Pallas kernels, attend_back(): pl.pallas_call(functools.partial(attend_back_kernel, tile), grid_spec=gri...  43 us
    pallas_call x1, Pallas kernels, attend(): pl.pallas_call(functools.partial(attend_kernel, tile), grid_spec=grid_spe...  28.4 us
    another operation x4, local copies, waits for them, and re-layouts, body(): jnp.stack([up_local, down_local])  26.2 us
  transfers between devices with their start and end apart: 42, of which 21 were waited for; matrix products, arithmetic and copies ran while one was open for 18% of the time, Pallas kernels for 15%

profile of v1, /device:TPU:0, one launch (start us, length us, event | category | flops | bytes accessed | tf_op | source)
XLA Modules:
  0.0 740.9 jit_solution(13592196581130877987)
XLA Ops:
  12.0 4.0 collective-permute-start.4
  21.0 106.3 %all-gather.1 = bf16[32,1,128]{2,1,0:T(2,128)(2,1)S(1)} all-gather(bf16[1,1,128]{2,1,0:T(2,128)(2,1)S(1)} %bitcast.289), channel_id=1, replica_groups=mesh['xy'=4,'core'=2,'cp'=4] {'xy','core','cp'}, dimensions={0}, use_global_device_ids=true | all-gather | bytes 8448 | tf_op jit(solution)/shard_map/all_gather | solution.py:722
  131.2 13.3 %collective-permute-done.12 = bf16[128,512]{1,0:T(8,128)(2,1)S(1)} collective-permute-done((bf16[128,512]{1,0:T(8,128)(2,1)S(1)}, bf16[128,512]{1,0:T(8,128)(2,1)S(1)}, u32[]{:S(2)}, u32[]{:S(2)}) %collective-permute-start.12) | collective-permute-done | bytes 131104 | tf_op jit(solution)/shard_map/ppermute | solution.py:674
  148.5 8.3 %collective-permute-done.5 = bf16[2,128,768]{2,1,0:T(8,128)(2,1)S(1)} collective-permute-done((bf16[2,128,768]{2,1,0:T(8,128)(2,1)S(1)}, bf16[2,128,768]{2,1,0:T(8,128)(2,1)S(1)}, u32[]{:S(2)}, u32[]{:S(2)}) %collective-permute-start.5) | collective-permute-done | bytes 393248 | tf_op jit(solution)/shard_map/ppermute | solution.py:674
  159.5 16.8 %collective-permute-done.2 = bf16[2,256,1024]{2,1,0:T(8,128)(2,1)S(1)} collective-permute-done((bf16[2,256,1024]{2,1,0:T(8,128)(2,1)S(1)}, bf16[2,256,1024]{2,1,0:T(8,128)(2,1)S(1)}, u32[]{:S(2)}, u32[]{:S(2)}) %collective-permute-start.2) | collective-permute-done | bytes 1048608 | tf_op jit(solution)/shard_map/ppermute | solution.py:674
  187.2 7.1 collective-permute-done.14
  196.6 14.1 %collective-permute-done.8 = bf16[512,768]{1,0:T(8,128)(2,1)} collective-permute-done((bf16[512,768]{1,0:T(8,128)(2,1)}, bf16[512,768]{1,0:T(8,128)(2,1)}, u32[]{:S(2)}, u32[]{:S(2)}) %collective-permute-start.8) | collective-permute-done | bytes 786464 | tf_op jit(solution)/shard_map/ppermute | solution.py:674
  213.9 3.4 pad_maximum_fusion.2.x_ref
  217.4 10.6 %project.1 = (bf16[2048,256]{1,0:T(8,128)(2,1)}, bf16[2048,256]{1,0:T(8,128)(2,1)}, bf16[2048,256]{1,0:T(8,128)(2,1)}) custom-call(s32[8]{0:T(128)} %convert_add_fusion.4.table, bf16[8,256,1024]{2,1,0:T(8,128)(2,1)} %pad_maximum_fusion.2.x_ref, bf16[1024,768]{1,0:T(8,128)(2,1)} %pad_maximum_fusion.7.w_ref, f32[2048,128]{1,0:T(8,128)} %copy.101.cos_ref, ...), custom_call_target="tpu_custom_call" | custom-call | tf_op jit(solution)/shard_map/project/pallas_call | solution.py:588
  228.0 28.4 %attend.1 = (f32[2048,256]{1,0:T(8,128)}, bf16[2048,256]{1,0:T(8,128)(2,1)}, f32[2,2,2048]{2,1,0:T(2,128)}) custom-call(s32[4,4]{1,0:T(4,128)} %pad_add_fusion.bounds, bf16[2048,256]{1,0:T(8,128)(2,1)} %get-tuple-element.13.q_ref, bf16[2048,256]{1,0:T(8,128)(2,1)} %get-tuple-element.14.k_ref, bf16[2048,256]{1,0:T(8,128)(2,1)} %get-tuple-element.15.v_ref, ...), custom_call_target="tpu_custom_call" | custom-call | tf_op jit(solution)/shard_map/attend/pallas_call | solution.py:417
  256.4 6.0 reorder.2
  267.5 12.2 %collective-permute-done.10 = bf16[2,2,256,256]{3,2,1,0:T(8,128)(2,1)} collective-permute-done((bf16[2,2,256,256]{3,2,1,0:T(8,128)(2,1)S(1)}, bf16[2,2,256,256]{3,2,1,0:T(8,128)(2,1)}, u32[]{:S(2)}, u32[]{:S(2)}) %collective-permute-start.10) | collective-permute-done | bytes 524320 | tf_op jit(solution)/shard_map/ppermute | solution.py:674
  285.7 10.1 %copy.147 = bf16[4,4,2,256,512]{4,1,3,0,2:T(4,128)(2,1)S(1)} copy(bf16[4,4,2,256,512]{4,3,2,1,0:T(8,128)(2,1)} %bitcast.231) | data formatting | bytes 16777216 | tf_op jit(solution)/shard_map/reshape | solution.py:755
  295.8 3.0 fusion.59
  302.3 6.8 fusion.21
  309.1 5.1 fusion.53
  322.1 25.7 %collective-permute-start.21 = (bf16[512,1024]{1,0:T(8,128)(2,1)}, bf16[512,1024]{1,0:T(8,128)(2,1)}, u32[]{:S(2)}, u32[]{:S(2)}) collective-permute-start(bf16[512,1024]{1,0:T(8,128)(2,1)} %add_convert_fusion.2), channel_id=1, source_target_pairs={{0,4},{4,0},{1,5},{5,1},{2,6},{6,2},{3,7},{7,3},{8,12},{12,8},{9,1... | collective-permute-start | bytes 3145736 | tf_op jit(solution)/shard_map/ppermute | solution.py:674
  347.7 2.6 collective-permute-done.21
  350.4 12.2 %multiply_convert_fusion = bf16[1024,2048]{1,0:T(8,128)(2,1)S(1)} fusion(bf16[1024,2048]{1,0:T(8,128)(2,1)} %bitcast.237, f32[1024,2048]{1,0:T(8,128)} %copy-done.48, bf16[512,1024]{1,0:T(8,128)(2,1)} %collective-permute-done.21, bf16[512,1024]{1,0:T(8,128)(2,1)} %add_convert_fusion.2), kind=kOutput, calls=%fused_computation.11 | convolution fusion | flops 4343201792 | bytes 18874368 | tf_op jit(solution)/shard_map/dot_general | solution.py:694
  362.6 4.5 fusion.64
  367.8 10.8 %convolution_convert_fusion = bf16[1024,2048]{1,0:T(8,128)(2,1)} fusion(bf16[512,1024]{1,0:T(8,128)(2,1)} %collective-permute-done.21, bf16[512,1024]{1,0:T(8,128)(2,1)} %add_convert_fusion.2, f32[1024,2048]{1,0:T(8,128)} %copy-done.48), kind=kOutput, calls=%fused_computation.15 | convolution fusion | flops 4320133120 | bytes 14680064 | tf_op jit(solution)/shard_map/dot_general | solution.py:694
  386.6 7.7 %convolution_convert_fusion.1 = bf16[1024,2048]{1,0:T(8,128)(2,1)} fusion(bf16[1024,2048]{1,0:T(8,128)(2,1)S(1)} %multiply_convert_fusion, bf16[512,1024]{1,0:T(8,128)(2,1)} %collective-permute-done.16, bf16[512,1024]{1,0:T(8,128)(2,1)} %multiply_convert_fusion.2), kind=kOutput, calls=%fused_computation.16 | convolution fusion | flops 4301258752 | bytes 10485760 | tf_op jit(solution)/shard_map/dot_general | solution.py:694
  394.3 7.9 %stack.67 = bf16[1,4,256,4,512]{4,3,2,1,0:T(4,128)(2,1)} reshape(bf16[1024,2048]{1,0:T(8,128)(2,1)} %convolution_convert_fusion.1) | data formatting | bytes 8388608 | tf_op jit(solution)/shard_map/stack | solution.py:870
  402.2 5.1 copy.121
  407.3 7.9 %stack.68 = bf16[1,4,256,4,512]{4,3,2,1,0:T(4,128)(2,1)} reshape(bf16[1024,2048]{1,0:T(8,128)(2,1)} %convolution_convert_fusion) | data formatting | bytes 8388608 | tf_op jit(solution)/shard_map/stack | solution.py:870
  415.2 5.4 copy.122
  420.6 6.2 pad_maximum_fusion.1
  429.2 7.4 pad_maximum_fusion
  438.2 3.9 convolution_convert_fusion.3
  444.1 2.2 constant_dynamic-slice_fusion.4
  446.6 14.2 %collective-permute-done.23 = bf16[2,2,256,256]{3,2,1,0:T(8,128)(2,1)S(1)} collective-permute-done((bf16[2,2,256,256]{3,2,1,0:T(8,128)(2,1)S(1)}, bf16[2,2,256,256]{3,2,1,0:T(8,128)(2,1)S(1)}, u32[]{:S(2)}, u32[]{:S(2)}) %collective-permute-start.23) | collective-permute-done | bytes 524320 | tf_op jit(solution)/shard_map/ppermute | solution.py:674
  463.9 5.9 reorder.3
  469.8 43.0 %attend_back.1.g_ref = bf16[3,2048,256]{2,1,0:T(8,128)(2,1)} custom-call(s32[4,4]{1,0:T(4,128)} %pad_add_fusion.bounds, bf16[2048,256]{1,0:T(8,128)(2,1)} %get-tuple-element.13.q_ref, bf16[2048,256]{1,0:T(8,128)(2,1)} %get-tuple-element.14.k_ref, bf16[2048,256]{1,0:T(8,128)(2,1)} %get-tuple-element.15.v_ref, bf16[2048,256]{1,0:T(8,128)(2,1)} %bitcast.241, ...), custom_call_target="tpu_custom_call" | custom-call | tf_op jit(solution)/shard_map/attend_back/pallas_call | solution.py:529
  512.8 10.0 %project_back.1 = bf16[8,256,1024]{2,1,0:T(8,128)(2,1)} custom-call(s32[8]{0:T(128)} %convert_add_fusion.4.table, bf16[3,2048,256]{2,1,0:T(8,128)(2,1)} %attend_back.1.g_ref, bf16[1024,768]{1,0:T(8,128)(2,1)} %pad_maximum_fusion.7.w_ref), custom_call_target="tpu_custom_call" | custom-call | tf_op jit(solution)/shard_map/project_back/pallas_call | solution.py:618
  524.8 10.3 %project_weights.1 = bf16[1024,768]{1,0:T(8,128)(2,1)} custom-call(s32[8]{0:T(128)} %convert_add_fusion.4.table, bf16[8,256,1024]{2,1,0:T(8,128)(2,1)} %pad_maximum_fusion.2.x_ref, bf16[3,2048,256]{2,1,0:T(8,128)(2,1)} %attend_back.1.g_ref), custom_call_target="tpu_custom_call" | custom-call | tf_op jit(solution)/shard_map/project_weights/pallas_call | solution.py:655
  537.0 57.1 %all-reduce.4.cloned.1.call-done = bf16[4,2,128,768]{3,2,1,0:T(8,128)(2,1)} async-done(((bf16[4,2,128,768]{3,2,1,0:T(8,128)(2,1)}), bf16[4,2,128,768]{3,2,1,0:T(8,128)(2,1)}) %all-reduce.4.cloned.1.call-update) | async-done | bytes 1572880
  595.2 3.1 convert_add_fusion
  603.9 2.5 collective-permute-start.29
  608.0 57.1 %collective-permute-done.29 = bf16[2,128,768]{2,1,0:T(8,128)(2,1)S(1)} collective-permute-done((bf16[2,128,768]{2,1,0:T(8,128)(2,1)S(1)}, bf16[2,128,768]{2,1,0:T(8,128)(2,1)S(1)}, u32[]{:S(2)}, u32[]{:S(2)}) %collective-permute-start.29) | collective-permute-done | bytes 393248 | tf_op jit(solution)/shard_map/ppermute | solution.py:674
  666.0 3.7 collective-permute-start.30
  669.6 15.0 %collective-permute-done.26 = bf16[2,256,1024]{2,1,0:T(8,128)(2,1)} collective-permute-done((bf16[2,256,1024]{2,1,0:T(8,128)(2,1)}, bf16[2,256,1024]{2,1,0:T(8,128)(2,1)}, u32[]{:S(2)}, u32[]{:S(2)}) %collective-permute-start.26) | collective-permute-done | bytes 1048608 | tf_op jit(solution)/shard_map/ppermute | solution.py:674
  684.6 2.2 slice_add_fusion
  691.3 9.5 %collective-permute-start.27 = (bf16[512,1024]{1,0:T(8,128)(2,1)}, bf16[512,1024]{1,0:T(8,128)(2,1)}, u32[]{:S(2)}, u32[]{:S(2)}) collective-permute-start(bf16[512,1024]{1,0:T(8,128)(2,1)} %add_convert_fusion), channel_id=1, source_target_pairs={{4,2},{2,4},{0,0},{6,6},{5,3},{3,5},{1,1},{7,7},{12,10},{10,12},{8... | collective-permute-start | bytes 3145736 | tf_op jit(solution)/shard_map/ppermute | solution.py:684
  703.7 2.1 collective-permute-done.34
  710.5 9.8 %collective-permute-done.36 = f32[32,128]{1,0:T(8,128)S(1)} collective-permute-done((f32[32,128]{1,0:T(8,128)S(1)}, f32[32,128]{1,0:T(8,128)S(1)}, u32[]{:S(2)}, u32[]{:S(2)}) %collective-permute-start.36) | collective-permute-done | bytes 16416 | tf_op jit(solution)/shard_map/ppermute | solution.py:674
  721.5 3.4 collective-permute-done.37
  725.4 2.8 convert.16
  731.7 2.3 copy.155
  (311 shorter events, 106.0 us)
Async XLA Ops:
  7.2 278.5 %all-gather.4.cloned.1.call-start = ((), (), s32[]{:S(2)}) async-start(), calls=%async_computation.3 | async-start | bytes 8912896 | tf_op jit(solution)/shard_map/all_gather | solution.py:754
  9.4 1.7 collective-permute-start.17
  12.0 523.5 %reduce-scatter.7.cloned.1.call-start = ((), (), s32[]{:S(2)}) async-start(), calls=%async_computation.5 | async-start | bytes 11796480
  12.0 132.6 %collective-permute-start.4 = (bf16[128,768]{1,0:T(8,128)(2,1)S(1)}, bf16[128,768]{1,0:T(8,128)(2,1)S(1)}, u32[]{:S(2)}, u32[]{:S(2)}) collective-permute-start(bf16[128,768]{1,0:T(8,128)(2,1)S(1)} %copy-done.29), channel_id=1, source_target_pairs={{0,2},{1,3},{2,0},{3,1},{4,6},{5,7},{6,4},{7,5},{8,10},{9,11},{10,... | collective-permute-start | bytes 589832 | tf_op jit(solution)/shard_map/ppermute | solution.py:674
  16.1 113.0 %collective-permute-start.1 = (s32[1,4]{1,0:T(1,128)S(1)}, s32[1,4]{1,0:T(1,128)S(1)}, u32[]{:S(2)}, u32[]{:S(2)}) collective-permute-start(s32[1,4]{1,0:T(1,128)S(1)} %copy-done.45), channel_id=1, source_target_pairs={{0,4},{4,0},{1,5},{5,1},{2,6},{6,2},{3,7},{7,3},{8,12},{12,8},{9,1... | collective-permute-start | bytes 56 | tf_op jit(solution)/shard_map/ppermute | solution.py:674
  16.1 128.7 %collective-permute-start = (bf16[512,1024]{1,0:T(8,128)(2,1)}, bf16[512,1024]{1,0:T(8,128)(2,1)S(1)}, u32[]{:S(2)}, u32[]{:S(2)}) collective-permute-start(bf16[512,1024]{1,0:T(8,128)(2,1)} %bitcast), channel_id=1, source_target_pairs={{4,2},{2,4},{0,0},{6,6},{5,3},{3,5},{1,1},{7,7},{12,10},{10,12},{8... | collective-permute-start | bytes 3145736 | tf_op jit(solution)/shard_map/ppermute | solution.py:684
  17.9 113.1 %collective-permute-start.11 = (bf16[128,256]{1,0:T(8,128)(2,1)S(1)}, bf16[128,256]{1,0:T(8,128)(2,1)S(1)}, u32[]{:S(2)}, u32[]{:S(2)}) collective-permute-start(bf16[128,256]{1,0:T(8,128)(2,1)S(1)} %copy-done.37), channel_id=1, source_target_pairs={{0,1},{1,0},{2,3},{3,2},{4,5},{5,4},{6,7},{7,6},{8,9},{9,8},{10,11... | collective-permute-start | bytes 196616 | tf_op jit(solution)/shard_map/ppermute | solution.py:674
  19.6 125.0 %copy-start.30 = (s32[1,1,8,256]{3,1,2,0:T(1,128)}, s32[1,1,8,256]{3,1,2,0:T(1,128)S(1)}, u32[]{:S(2)}) copy-start(s32[1,1,8,256]{3,1,2,0:T(1,128)S(1)} %copy.136) | copy-start | bytes 24580
  129.1 16.9 %copy-start.32 = (f32[8,1,128]{2,1,0:T(1,128)}, f32[8,1,128]{2,1,0:T(1,128)S(1)}, u32[]{:S(2)}) copy-start(f32[8,1,128]{2,1,0:T(1,128)S(1)} %get-tuple-element.137) | copy-start | bytes 12292
  129.2 15.5 %copy-start.31 = (s32[2048]{0:T(1024)}, s32[2048]{0:T(1024)S(1)}, u32[]{:S(2)}) copy-start(s32[2048]{0:T(1024)S(1)} %get-tuple-element.65) | copy-start | bytes 24580
  131.1 13.5 %collective-permute-start.12 = (bf16[128,512]{1,0:T(8,128)(2,1)S(1)}, bf16[128,512]{1,0:T(8,128)(2,1)S(1)}, u32[]{:S(2)}, u32[]{:S(2)}) collective-permute-start(bf16[128,512]{1,0:T(8,128)(2,1)S(1)} %pad_maximum_fusion.33), channel_id=1, source_target_pairs={{0,2},{1,3},{2,0},{3,1},{4,6},{5,7},{6,4},{7,5},{8,10},{9,11},{10,... | collective-permute-start | bytes 393224 | tf_op jit(solution)/shard_map/ppermute | solution.py:674
  144.7 12.1 %collective-permute-start.5 = (bf16[2,128,768]{2,1,0:T(8,128)(2,1)S(1)}, bf16[2,128,768]{2,1,0:T(8,128)(2,1)S(1)}, u32[]{:S(2)}, u32[]{:S(2)}) collective-permute-start(bf16[2,128,768]{2,1,0:T(8,128)(2,1)S(1)} %pad_maximum_fusion.24), channel_id=1, source_target_pairs={{0,1},{1,0},{2,3},{3,2},{4,5},{5,4},{6,7},{7,6},{8,9},{9,8},{10,11... | collective-permute-start | bytes 1179656 | tf_op jit(solution)/shard_map/ppermute | solution.py:674
  146.4 29.9 %collective-permute-start.2 = (bf16[2,256,1024]{2,1,0:T(8,128)(2,1)S(1)}, bf16[2,256,1024]{2,1,0:T(8,128)(2,1)S(1)}, u32[]{:S(2)}, u32[]{:S(2)}) collective-permute-start(bf16[2,256,1024]{2,1,0:T(8,128)(2,1)S(1)} %bitcast.228), channel_id=1, source_target_pairs={{0,1},{1,0},{2,3},{3,2},{4,5},{5,4},{6,7},{7,6},{8,9},{9,8},{10,11... | collective-permute-start | bytes 3145736 | tf_op jit(solution)/shard_map/ppermute | solution.py:674
  157.1 1.5 collective-permute-start.6
  157.2 21.1 %collective-permute-start.13 = (bf16[1,128,1024]{2,1,0:T(8,128)(2,1)S(1)}, bf16[1,128,1024]{2,1,0:T(8,128)(2,1)S(1)}, u32[]{:S(2)}, u32[]{:S(2)}) collective-permute-start(bf16[1,128,1024]{2,1,0:T(8,128)(2,1)S(1)} %maximum_bitcast_fusion), channel_id=1, source_target_pairs={{0,8},{8,0},{16,24},{24,16},{1,9},{9,1},{17,25},{25,17},{2,10},{10... | collective-permute-start | bytes 786440 | tf_op jit(solution)/shard_map/ppermute | solution.py:674
  158.7 21.9 %collective-permute-start.7 = (bf16[256,768]{1,0:T(8,128)(2,1)S(1)}, bf16[256,768]{1,0:T(8,128)(2,1)S(1)}, u32[]{:S(2)}, u32[]{:S(2)}) collective-permute-start(bf16[256,768]{1,0:T(8,128)(2,1)S(1)} %pad_maximum_fusion.25), channel_id=1, source_target_pairs={{0,8},{8,0},{16,24},{24,16},{1,9},{9,1},{17,25},{25,17},{2,10},{10... | collective-permute-start | bytes 1179656 | tf_op jit(solution)/shard_map/ppermute | solution.py:674
  178.0 35.6 %collective-permute-start.3 = (bf16[4,256,1024]{2,1,0:T(8,128)(2,1)}, bf16[4,256,1024]{2,1,0:T(8,128)(2,1)}, u32[]{:S(2)}, u32[]{:S(2)}) collective-permute-start(bf16[4,256,1024]{2,1,0:T(8,128)(2,1)} %pad_maximum_fusion.3), channel_id=1, source_target_pairs={{0,4},{4,0},{1,5},{5,1},{2,6},{6,2},{3,7},{7,3},{8,12},{12,8},{9,1... | collective-permute-start | bytes 6291464 | tf_op jit(solution)/shard_map/ppermute | solution.py:674
  179.3 15.0 %collective-permute-start.14 = (bf16[2,128,1024]{2,1,0:T(8,128)(2,1)}, bf16[2,128,1024]{2,1,0:T(8,128)(2,1)}, u32[]{:S(2)}, u32[]{:S(2)}) collective-permute-start(bf16[2,128,1024]{2,1,0:T(8,128)(2,1)} %pad_maximum_fusion.20), channel_id=1, source_target_pairs={{0,16},{8,24},{16,0},{24,8},{1,17},{9,25},{17,1},{25,9},{2,18},{10... | collective-permute-start | bytes 1572872 | tf_op jit(solution)/shard_map/ppermute | solution.py:674
  181.7 29.1 %collective-permute-start.8 = (bf16[512,768]{1,0:T(8,128)(2,1)}, bf16[512,768]{1,0:T(8,128)(2,1)}, u32[]{:S(2)}, u32[]{:S(2)}) collective-permute-start(bf16[512,768]{1,0:T(8,128)(2,1)} %pad_maximum_fusion.16), channel_id=1, source_target_pairs={{0,16},{8,24},{16,0},{24,8},{1,17},{9,25},{17,1},{25,9},{2,18},{10... | collective-permute-start | bytes 2359304 | tf_op jit(solution)/shard_map/ppermute | solution.py:674
  187.2 23.6 %copy-start.15 = (bf16[256,768]{1,0:T(8,128)(2,1)S(1)}, bf16[256,768]{1,0:T(8,128)(2,1)}, u32[]{:S(2)}) copy-start(bf16[256,768]{1,0:T(8,128)(2,1)} %copy-done.14) | copy-start | bytes 1179652
  196.6 69.2 %collective-permute-start.15 = (bf16[4,128,1024]{2,1,0:T(8,128)(2,1)}, bf16[4,128,1024]{2,1,0:T(8,128)(2,1)}, u32[]{:S(2)}, u32[]{:S(2)}) collective-permute-start(bf16[4,128,1024]{2,1,0:T(8,128)(2,1)} %pad_maximum_fusion.14), channel_id=1, source_target_pairs={{0,4},{4,0},{1,5},{5,1},{2,6},{6,2},{3,7},{7,3},{8,12},{12,8},{9,1... | collective-permute-start | bytes 3145736 | tf_op jit(solution)/shard_map/ppermute | solution.py:674
  263.5 2.0 collective-permute-start.9
  265.5 14.1 %collective-permute-start.10 = (bf16[2,2,256,256]{3,2,1,0:T(8,128)(2,1)S(1)}, bf16[2,2,256,256]{3,2,1,0:T(8,128)(2,1)}, u32[]{:S(2)}, u32[]{:S(2)}) collective-permute-start(bf16[2,2,256,256]{3,2,1,0:T(8,128)(2,1)S(1)} %pad_maximum_fusion.19), channel_id=1, source_target_pairs={{0,1},{1,0},{2,3},{3,2},{4,5},{5,4},{6,7},{7,6},{8,9},{9,8},{10,11... | collective-permute-start | bytes 1572872 | tf_op jit(solution)/shard_map/ppermute | solution.py:674
  285.7 16.0 %collective-permute-start.16 = (bf16[512,1024]{1,0:T(8,128)(2,1)}, bf16[512,1024]{1,0:T(8,128)(2,1)}, u32[]{:S(2)}, u32[]{:S(2)}) collective-permute-start(bf16[512,1024]{1,0:T(8,128)(2,1)} %multiply_convert_fusion.2), channel_id=1, source_target_pairs={{0,4},{4,0},{1,5},{5,1},{2,6},{6,2},{3,7},{7,3},{8,12},{12,8},{9,1... | collective-permute-start | bytes 3145736 | tf_op jit(solution)/shard_map/ppermute | solution.py:674
  314.3 2.9 collective-permute-start.18
  315.4 2.5 collective-permute-start.20
  322.1 28.3 %collective-permute-start.21 = (bf16[512,1024]{1,0:T(8,128)(2,1)}, bf16[512,1024]{1,0:T(8,128)(2,1)}, u32[]{:S(2)}, u32[]{:S(2)}) collective-permute-start(bf16[512,1024]{1,0:T(8,128)(2,1)} %add_convert_fusion.2), channel_id=1, source_target_pairs={{0,4},{4,0},{1,5},{5,1},{2,6},{6,2},{3,7},{7,3},{8,12},{12,8},{9,1... | collective-permute-start | bytes 3145736 | tf_op jit(solution)/shard_map/ppermute | solution.py:674
  367.3 11.3 %collective-permute-start.22 = (bf16[512,1024]{1,0:T(8,128)(2,1)S(1)}, bf16[512,1024]{1,0:T(8,128)(2,1)S(1)}, u32[]{:S(2)}, u32[]{:S(2)}) collective-permute-start(bf16[512,1024]{1,0:T(8,128)(2,1)S(1)} %slice.196), channel_id=1, source_target_pairs={{0,4},{4,0},{1,5},{5,1},{2,6},{6,2},{3,7},{7,3},{8,12},{12,8},{9,1... | collective-permute-start | bytes 3145736 | tf_op jit(solution)/shard_map/ppermute | solution.py:674
  386.4 40.3 %collective-permute-start.31 = (bf16[4,128,1024]{2,1,0:T(8,128)(2,1)S(1)}, bf16[4,128,1024]{2,1,0:T(8,128)(2,1)}, u32[]{:S(2)}, u32[]{:S(2)}) collective-permute-start(bf16[4,128,1024]{2,1,0:T(8,128)(2,1)S(1)} %dynamic-slice_bitcast_fusion), channel_id=1, source_target_pairs={{0,4},{4,0},{1,5},{5,1},{2,6},{6,2},{3,7},{7,3},{8,12},{12,8},{9,1... | collective-permute-start | bytes 3145736 | tf_op jit(solution)/shard_map/ppermute | solution.py:674
  436.6 157.5 %all-reduce.4.cloned.1.call-start = ((), (), s32[]{:S(2)}) async-start(), calls=%async_computation.4 | async-start | bytes 3145728
  446.5 14.3 %collective-permute-start.23 = (bf16[2,2,256,256]{3,2,1,0:T(8,128)(2,1)S(1)}, bf16[2,2,256,256]{3,2,1,0:T(8,128)(2,1)S(1)}, u32[]{:S(2)}, u32[]{:S(2)}) collective-permute-start(bf16[2,2,256,256]{3,2,1,0:T(8,128)(2,1)S(1)} %pad_maximum_fusion.22), channel_id=1, source_target_pairs={{0,1},{1,0},{2,3},{3,2},{4,5},{5,4},{6,7},{7,6},{8,9},{9,8},{10,11... | collective-permute-start | bytes 1572872 | tf_op jit(solution)/shard_map/ppermute | solution.py:674
  460.8 2.0 collective-permute-start.24
  524.6 70.5 %collective-permute-start.25 = (bf16[4,256,1024]{2,1,0:T(8,128)(2,1)S(1)}, bf16[4,256,1024]{2,1,0:T(8,128)(2,1)}, u32[]{:S(2)}, u32[]{:S(2)}) collective-permute-start(bf16[4,256,1024]{2,1,0:T(8,128)(2,1)S(1)} %slice.157), channel_id=1, source_target_pairs={{0,4},{4,0},{1,5},{5,1},{2,6},{6,2},{3,7},{7,3},{8,12},{12,8},{9,1... | collective-permute-start | bytes 6291464 | tf_op jit(solution)/shard_map/ppermute | solution.py:674
  535.1 185.2 %reduce-scatter.5.cloned.1.call-start = ((), (), s32[]{:S(2)}) async-start(), calls=%async_computation.2 | async-start | bytes 2949120 | tf_op jit(solution)/shard_map/reduce_scatter | solution.py:876
  595.1 7.8 %collective-permute-start.28 = (bf16[128,768]{1,0:T(8,128)(2,1)S(1)}, bf16[128,768]{1,0:T(8,128)(2,1)S(1)}, u32[]{:S(2)}, u32[]{:S(2)}) collective-permute-start(bf16[128,768]{1,0:T(8,128)(2,1)S(1)} %dynamic-slice_bitcast_fusion.6), channel_id=1, source_target_pairs={{0,4},{4,0},{1,5},{5,1},{2,6},{6,2},{3,7},{7,3},{8,12},{12,8},{9,1... | collective-permute-start | bytes 589832 | tf_op jit(solution)/shard_map/ppermute | solution.py:674
  601.4 83.2 %collective-permute-start.26 = (bf16[2,256,1024]{2,1,0:T(8,128)(2,1)}, bf16[2,256,1024]{2,1,0:T(8,128)(2,1)}, u32[]{:S(2)}, u32[]{:S(2)}) collective-permute-start(bf16[2,256,1024]{2,1,0:T(8,128)(2,1)} %slice.195), channel_id=1, source_target_pairs={{0,1},{1,0},{2,3},{3,2},{4,5},{5,4},{6,7},{7,6},{8,9},{9,8},{10,11... | collective-permute-start | bytes 3145736 | tf_op jit(solution)/shard_map/ppermute | solution.py:674
  603.9 61.2 %collective-permute-start.29 = (bf16[2,128,768]{2,1,0:T(8,128)(2,1)S(1)}, bf16[2,128,768]{2,1,0:T(8,128)(2,1)S(1)}, u32[]{:S(2)}, u32[]{:S(2)}) collective-permute-start(bf16[2,128,768]{2,1,0:T(8,128)(2,1)S(1)} %pad_maximum_fusion.26), channel_id=1, source_target_pairs={{0,2},{1,3},{2,0},{3,1},{4,6},{5,7},{6,4},{7,5},{8,10},{9,11},{10,... | collective-permute-start | bytes 1179656 | tf_op jit(solution)/shard_map/ppermute | solution.py:674
  606.4 94.5 %collective-permute-start.19 = (bf16[512,1024]{1,0:T(8,128)(2,1)S(1)}, bf16[512,1024]{1,0:T(8,128)(2,1)}, u32[]{:S(2)}, u32[]{:S(2)}) collective-permute-start(bf16[512,1024]{1,0:T(8,128)(2,1)S(1)} %copy-done.22), channel_id=1, source_target_pairs={{4,2},{2,4},{0,0},{6,6},{5,3},{3,5},{1,1},{7,7},{12,10},{10,12},{8... | collective-permute-start | bytes 3145736 | tf_op jit(solution)/shard_map/ppermute | solution.py:684
  666.0 20.8 %copy-start.33 = (f32[8,1,128]{2,1,0:T(1,128)S(1)}, f32[8,1,128]{2,1,0:T(1,128)}, u32[]{:S(2)}) copy-start(f32[8,1,128]{2,1,0:T(1,128)} %copy-done.32) | copy-start | bytes 12292
  666.0 20.8 %copy-start.35 = (f32[512]{0:T(512)S(1)}, f32[512]{0:T(512)}, u32[]{:S(2)}) copy-start(f32[512]{0:T(512)} %copy-done.34) | copy-start | bytes 6148
  666.0 37.5 %collective-permute-start.30 = (bf16[2,128,768]{2,1,0:T(8,128)(2,1)}, bf16[2,128,768]{2,1,0:T(8,128)(2,1)S(1)}, u32[]{:S(2)}, u32[]{:S(2)}) collective-permute-start(bf16[2,128,768]{2,1,0:T(8,128)(2,1)} %add_convert_fusion.4), channel_id=1, source_target_pairs={{0,1},{1,0},{2,3},{3,2},{4,5},{5,4},{6,7},{7,6},{8,9},{9,8},{10,11... | collective-permute-start | bytes 1179656 | tf_op jit(solution)/shard_map/ppermute | solution.py:674
  691.3 34.1 %collective-permute-start.27 = (bf16[512,1024]{1,0:T(8,128)(2,1)}, bf16[512,1024]{1,0:T(8,128)(2,1)}, u32[]{:S(2)}, u32[]{:S(2)}) collective-permute-start(bf16[512,1024]{1,0:T(8,128)(2,1)} %add_convert_fusion), channel_id=1, source_target_pairs={{4,2},{2,4},{0,0},{6,6},{5,3},{3,5},{1,1},{7,7},{12,10},{10,12},{8... | collective-permute-start | bytes 3145736 | tf_op jit(solution)/shard_map/ppermute | solution.py:684
  700.8 1.2 collective-permute-start.33
  702.0 3.7 collective-permute-start.34
  705.8 3.7 collective-permute-start.35
  709.5 10.7 %collective-permute-start.36 = (f32[32,128]{1,0:T(8,128)S(1)}, f32[32,128]{1,0:T(8,128)S(1)}, u32[]{:S(2)}, u32[]{:S(2)}) collective-permute-start(f32[32,128]{1,0:T(8,128)S(1)} %add.433), channel_id=1, source_target_pairs={{0,1},{1,0},{2,3},{3,2},{4,5},{5,4},{6,7},{7,6},{8,9},{9,8},{10,11... | collective-permute-start | bytes 49160 | tf_op jit(solution)/shard_map/ppermute | solution.py:674
  720.3 4.6 collective-permute-start.37
  721.4 8.3 %collective-permute-start.32 = (bf16[2,128,512]{2,1,0:T(8,128)(2,1)S(1)}, bf16[2,128,512]{2,1,0:T(8,128)(2,1)S(1)}, u32[]{:S(2)}, u32[]{:S(2)}) collective-permute-start(bf16[2,128,512]{2,1,0:T(8,128)(2,1)S(1)} %dynamic-slice_bitcast_fusion.1), channel_id=1, source_target_pairs={{0,4},{4,0},{1,5},{5,1},{2,6},{6,2},{3,7},{7,3},{8,12},{12,8},{9,1... | collective-permute-start | bytes 786440 | tf_op jit(solution)/shard_map/ppermute | solution.py:674
  (43 other events, 153.6 us)
Sparse Core Ops, SparseCore 0:
  12.1 133.7 all-gather.3
  436.8 92.7 reduce-scatter.6
  535.2 58.8 all-reduce.3
  596.4 85.6 reduce-scatter.4

commit v2 on v1

--- a/solution.py
+++ b/solution.py
@@ -5,6 +5,7 @@
 import jax.numpy as jnp
 from jax import lax
 from jax.experimental import pallas as pl
+from jax.experimental.layout import Layout, with_layout_constraint
 from jax.experimental.pallas import tpu as pltpu
 from jax.sharding import Mesh, PartitionSpec as P
 
@@ -332,13 +333,17 @@
     )
 
 
+def work(flops, moved):
+    return pl.CostEstimate(flops=flops, bytes_accessed=moved, transcendentals=0)
+
+
 def turned(x, cosine, sine):
     lane = lax.broadcasted_iota(jnp.int32, x.shape, 1)
     other = jnp.where((lane & 32) == 0, pltpu.roll(x, 96, 1), pltpu.roll(x, 32, 1))
     return x * cosine + other * sine
 
 
-def attend_kernel(tile, bounds, q_ref, k_ref, v_ref, pcol_ref, prow_ref, srow_ref,
+def attend_kernel(tile, bounds, slot_of, q_ref, k_ref, v_ref, pcol_ref, prow_ref, srow_ref,
                   o_ref, ob_ref, lse_ref, vt_ref):
     i = pl.program_id(1)
 
@@ -389,28 +394,32 @@
         parts.append(acc / total)
     out = jnp.concatenate(parts, axis=0).T
     o_ref[...] = out
-    ob_ref[...] = out.astype(BF16)
-
-
-def attend(q, k, v, pcol, prow, srow, bounds, tile):
+    span = ob_ref.shape[1]
+    for b in range(tile // span):
+        ob_ref[slot_of[i * (tile // span) + b]] = out[b * span : (b + 1) * span].astype(BF16)
+
+
+def attend(q, k, v, pcol, prow, srow, bounds, slot_of, tile):
     rows, width = q.shape
+    blocks = slot_of.shape[0]
+    span = rows // blocks
     pairs = width // 128
     count = rows // tile
     grid_spec = pltpu.PrefetchScalarGridSpec(
-        num_scalar_prefetch=1,
+        num_scalar_prefetch=2,
         grid=(pairs, count),
         in_specs=[
-            pl.BlockSpec((tile, 128), lambda p, i, b: (i, p)),
-            pl.BlockSpec((rows, 128), lambda p, i, b: (0, p)),
-            pl.BlockSpec((rows, 128), lambda p, i, b: (0, p)),
-            pl.BlockSpec((rows, 1), lambda p, i, b: (0, 0)),
-            pl.BlockSpec((1, tile), lambda p, i, b: (0, i)),
-            pl.BlockSpec((1, tile), lambda p, i, b: (0, i)),
+            pl.BlockSpec((tile, 128), lambda p, i, b, t: (i, p)),
+            pl.BlockSpec((rows, 128), lambda p, i, b, t: (0, p)),
+            pl.BlockSpec((rows, 128), lambda p, i, b, t: (0, p)),
+            pl.BlockSpec((rows, 1), lambda p, i, b, t: (0, 0)),
+            pl.BlockSpec((1, tile), lambda p, i, b, t: (0, i)),
+            pl.BlockSpec((1, tile), lambda p, i, b, t: (0, i)),
         ],
         out_specs=[
-            pl.BlockSpec((tile, 128), lambda p, i, b: (i, p)),
-            pl.BlockSpec((tile, 128), lambda p, i, b: (i, p)),
-            pl.BlockSpec((1, 2, tile), lambda p, i, b: (p, 0, i)),
+            pl.BlockSpec((tile, 128), lambda p, i, b, t: (i, p)),
+            pl.BlockSpec((blocks, span, 128), lambda p, i, b, t: (0, 0, p)),
+            pl.BlockSpec((1, 2, tile), lambda p, i, b, t: (p, 0, i)),
         ],
         scratch_shapes=[pltpu.VMEM((128, rows), BF16)],
     )
@@ -419,27 +428,32 @@
         grid_spec=grid_spec,
         out_shape=[
             jax.ShapeDtypeStruct((rows, width), F32),
-            jax.ShapeDtypeStruct((rows, width), BF16),
+            jax.ShapeDtypeStruct((blocks, span, width), BF16),
             jax.ShapeDtypeStruct((pairs, 2, rows), F32),
         ],
         compiler_params=params(2),
+        cost_estimate=work(3 * rows * rows * width, 8 * rows * width),
         name="attend",
-    )(bounds, q, k, v, pcol, prow, srow)
-
-
-def attend_back_kernel(tile, bounds, q_ref, k_ref, v_ref, do_ref, o_ref, lse_ref, pcol_ref,
+    )(bounds, slot_of, q, k, v, pcol, prow, srow)
+
+
+def attend_back_kernel(tile, bounds, slot_of, q_ref, k_ref, v_ref, do_ref, o_ref, lse_ref, pcol_ref,
                        prow_ref, srow_ref, cos_ref, sin_ref, g_ref,
                        qm, dom, qtm, dotm, delta, dqt):
     j = pl.program_id(1)
     count = pl.num_programs(1)
     rows = q_ref.shape[0]
 
+    span = do_ref.shape[1]
+
     @pl.when(j == 0)
     def _():
         for t in range(rows // tile):
             part = pl.ds(t * tile, tile)
             q = q_ref[part, :].astype(F32)
-            do = do_ref[part, :].astype(F32)
+            do = jnp.concatenate(
+                [do_ref[slot_of[t * tile // span + b]] for b in range(tile // span)], axis=0
+            ).astype(F32)
             qt, dot = q.T, do.T
             lane = lax.broadcasted_iota(jnp.int32, q.shape, 1)
             row = lax.broadcasted_iota(jnp.int32, qt.shape, 0)
@@ -503,23 +517,25 @@
             g_ref[0, part, :] = unturned(dqt[:, part].T * 0.125, part)
 
 
-def attend_back(q, k, v, do, o, lse, pcol, prow, srow, cosine, sine, bounds, tile):
+def attend_back(pair, q, k, v, do, o, lse, pcol, prow, srow, cosine, sine, bounds, slot_of, tile):
     rows, width = q.shape
-    pairs = width // 128
+    blocks, span, _ = do.shape
     count = rows // tile
-    whole = pl.BlockSpec((rows, 128), lambda p, j, b: (0, p))
-    table = pl.BlockSpec((rows, 128), lambda p, j, b: (0, 0))
-    line = pl.BlockSpec((1, rows), lambda p, j, b: (0, 0))
+    whole = pl.BlockSpec((rows, 128), lambda p, j, b, t: (0, pair))
+    table = pl.BlockSpec((rows, 128), lambda p, j, b, t: (0, 0))
+    line = pl.BlockSpec((1, rows), lambda p, j, b, t: (0, 0))
     grid_spec = pltpu.PrefetchScalarGridSpec(
-        num_scalar_prefetch=1,
-        grid=(pairs, count),
+        num_scalar_prefetch=2,
+        grid=(1, count),
         in_specs=[
-            whole, whole, whole, whole, whole,
-            pl.BlockSpec((1, 2, rows), lambda p, j, b: (p, 0, 0)),
-            pl.BlockSpec((rows, 1), lambda p, j, b: (0, 0)),
+            whole, whole, whole,
+            pl.BlockSpec((blocks, span, 128), lambda p, j, b, t: (0, 0, pair)),
+            whole,
+            pl.BlockSpec((1, 2, rows), lambda p, j, b, t: (pair, 0, 0)),
+            pl.BlockSpec((rows, 1), lambda p, j, b, t: (0, 0)),
             line, line, table, table,
         ],
-        out_specs=pl.BlockSpec((3, rows, 128), lambda p, j, b: (0, 0, p)),
+        out_specs=pl.BlockSpec((3, rows, 128), lambda p, j, b, t: (0, 0, 0)),
         scratch_shapes=[
             pltpu.VMEM((2, rows, 128), BF16), pltpu.VMEM((2, rows, 128), BF16),
             pltpu.VMEM((2, 128, rows), BF16), pltpu.VMEM((2, 128, rows), BF16),
@@ -529,10 +545,11 @@
     return pl.pallas_call(
         functools.partial(attend_back_kernel, tile),
         grid_spec=grid_spec,
-        out_shape=jax.ShapeDtypeStruct((3, rows, width), BF16),
+        out_shape=jax.ShapeDtypeStruct((3, rows, 128), BF16),
         compiler_params=params(2),
+        cost_estimate=work(7 * rows * rows * 128, 18 * rows * 128),
         name="attend_back",
-    )(bounds, q, k, v, do, o, lse, pcol, prow, srow, cosine, sine)
+    )(bounds, slot_of, q, k, v, do, o, lse, pcol, prow, srow, cosine, sine)
 
 
 def tile_bounds(starts_nat, tile):
@@ -548,30 +565,59 @@
     return jnp.stack([lo, mid, full, end]).astype(jnp.int32)
 
 
-def reorder_kernel(table, x_ref, o_ref):
-    o_ref[...] = x_ref[...]
-
-
-def reorder(x, table):
-    count, rows, width = x.shape
-    block = (1, rows, width)
+def normalized(x):
+    centred = x - jnp.mean(x, axis=1, keepdims=True)
+    scale = lax.rsqrt(jnp.mean(centred * centred, axis=1, keepdims=True) + NORM_EPS)
+    return centred * scale, scale
+
+
+def normalized_back(hat, scale, upstream):
+    level = jnp.mean(upstream, axis=1, keepdims=True)
+    slant = jnp.mean(upstream * hat, axis=1, keepdims=True)
+    return scale * (upstream - level - hat * slant)
+
+
+def dot_nt(a, b):
+    return lax.dot_general(a, b, (((1,), (1,)), ((), ())), preferred_element_type=F32)
+
+
+def call(kernel, name, grid, tables, ins, outs, scratch, flops, *arrays):
+    moved = sum(math.prod(a.shape) * a.dtype.itemsize for a in arrays)
+    moved += sum(math.prod(s.shape) * s.dtype.itemsize for s, _ in outs)
     return pl.pallas_call(
-        reorder_kernel,
+        kernel,
         grid_spec=pltpu.PrefetchScalarGridSpec(
-            num_scalar_prefetch=1,
-            grid=(count,),
-            in_specs=[pl.BlockSpec(block, lambda i, t: (t[i], 0, 0))],
-            out_specs=pl.BlockSpec(block, lambda i, t: (i, 0, 0)),
+            num_scalar_prefetch=len(tables),
+            grid=grid,
+            in_specs=ins,
+            out_specs=[spec for _, spec in outs],
+            scratch_shapes=scratch,
         ),
-        out_shape=jax.ShapeDtypeStruct(x.shape, x.dtype),
-        compiler_params=params(1),
-        name="reorder",
-    )(table, x)
-
-
-def project_kernel(table, x_ref, w_ref, cos_ref, sin_ref, q_ref, k_ref, v_ref):
+        out_shape=[shape for shape, _ in outs],
+        compiler_params=params(len(grid)),
+        cost_estimate=work(flops, moved),
+        name=name,
+    )(*tables, *arrays)
+
+
+def shaped(dtype, *shape):
+    return jax.ShapeDtypeStruct(shape, dtype)
+
+
+def fixed(*shape):
+    return pl.BlockSpec(shape, lambda *_: (0,) * len(shape))
+
+
+def project_kernel(slot_of, x0, x1, x2, x3, gain_ref, w_ref, cos_ref, sin_ref,
+                   q_ref, k_ref, v_ref, n_ref):
+    which = slot_of[pl.program_id(0)] >> 1
     width = q_ref.shape[1]
-    linear = jnp.dot(x_ref[0], w_ref[...], preferred_element_type=F32)
+    near = jnp.where(which == 0, x0[0], x1[0])
+    far = jnp.where(which == 2, x2[0], x3[0])
+    x = jnp.where(which < 2, near, far).astype(F32)
+    normed = (normalized(x)[0] * gain_ref[0:1, :]).astype(BF16)
+    n_ref[0] = normed
+    linear = jnp.dot(normed, w_ref[...], preferred_element_type=F32)
     for at in range(0, width, 128):
         q = turned(linear[:, at : at + 128], cos_ref[...], sin_ref[...])
         k = turned(linear[:, width + at : width + at + 128], cos_ref[...], sin_ref[...])
@@ -580,94 +626,218 @@
     v_ref[...] = linear[:, 2 * width :].astype(BF16)
 
 
-def project(x, w, cosine, sine, table):
-    count, rows, depth = x.shape
+def project(parts, gains, w, cosine, sine, slot_of):
+    count = slot_of.shape[0]
+    _, rows, depth = parts[0].shape
     width = w.shape[1] // 3
-    out = pl.BlockSpec((rows, width), lambda i, t: (i, 0))
+    piece = pl.BlockSpec((1, rows, depth), lambda i, t: (t[i] & 1, 0, 0))
     angle = pl.BlockSpec((rows, 128), lambda i, t: (i, 0))
-    return pl.pallas_call(
-        project_kernel,
-        grid_spec=pltpu.PrefetchScalarGridSpec(
-            num_scalar_prefetch=1,
-            grid=(count,),
-            in_specs=[
-                pl.BlockSpec((1, rows, depth), lambda i, t: (t[i], 0, 0)),
-                pl.BlockSpec(w.shape, lambda i, t: (0, 0)),
-                angle, angle,
-            ],
-            out_specs=[out, out, out],
-        ),
-        out_shape=[jax.ShapeDtypeStruct((count * rows, width), BF16)] * 3,
-        compiler_params=params(1),
-        name="project",
-    )(table, x, w, cosine, sine)
-
-
-def project_back_kernel(table, g_ref, w_ref, o_ref):
-    g = jnp.concatenate([g_ref[0], g_ref[1], g_ref[2]], axis=1)
-    o_ref[0] = lax.dot_general(
-        g, w_ref[...], (((1,), (1,)), ((), ())), preferred_element_type=F32
-    ).astype(BF16)
-
-
-def project_back(grads, w, table):
+    out = shaped(BF16, count * rows, width), pl.BlockSpec((rows, width), lambda i, t: (i, 0))
+    normed = (
+        shaped(BF16, count, rows, depth),
+        pl.BlockSpec((1, rows, depth), lambda i, t: (t[i], 0, 0)),
+    )
+    return call(
+        project_kernel, "project", (count,), [slot_of],
+        [piece] * 4 + [fixed(*gains.shape), fixed(*w.shape), angle, angle],
+        [out, out, out, normed], [], 2 * count * rows * depth * 3 * width,
+        *parts, gains, w, cosine, sine,
+    )
+
+
+def side_by_side(first, second):
+    return jnp.concatenate([half[n] for n in range(3) for half in (first, second)], axis=1)
+
+
+def project_back_kernel(table, g0_ref, g1_ref, w_ref, o_ref):
+    g = side_by_side(g0_ref, g1_ref)
+    o_ref[0] = dot_nt(g, w_ref[...]).astype(o_ref.dtype)
+
+
+def project_back(grads, w, table, rows, dtype):
     count = table.shape[0]
-    _, total, width = grads.shape
-    rows = total // count
-    depth = w.shape[0]
-    return pl.pallas_call(
-        project_back_kernel,
-        grid_spec=pltpu.PrefetchScalarGridSpec(
-            num_scalar_prefetch=1,
-            grid=(count,),
-            in_specs=[
-                pl.BlockSpec((3, rows, width), lambda i, t: (0, i, 0)),
-                pl.BlockSpec(w.shape, lambda i, t: (0, 0)),
-            ],
-            out_specs=pl.BlockSpec((1, rows, depth), lambda i, t: (t[i], 0, 0)),
-        ),
-        out_shape=jax.ShapeDtypeStruct((count, rows, depth), BF16),
-        compiler_params=params(1),
-        name="project_back",
-    )(table, grads, w)
-
-
-def project_weights_kernel(table, x_ref, g_ref, o_ref, total):
+    depth, width = w.shape
+    piece = pl.BlockSpec((3, rows, width // 6), lambda i, t: (0, t[i], 0))
+    return call(
+        project_back_kernel, "project_back", (count,), [table],
+        [piece, piece, fixed(*w.shape)],
+        [(shaped(dtype, count, rows, depth), pl.BlockSpec((1, rows, depth), lambda i, t: (i, 0, 0)))],
+        [], 2 * count * rows * depth * width, *grads, w,
+    )[0]
+
+
+def project_weights_kernel(slot_of, place, x_ref, g0_ref, g1_ref, w_ref, ac, as_, bc, bs, gain_ref, total):
     i = pl.program_id(0)
 
     @pl.when(i == 0)
     def _():
         total[...] = jnp.zeros_like(total)
 
-    g = jnp.concatenate([g_ref[0], g_ref[1], g_ref[2]], axis=1)
+    g = side_by_side(g0_ref, g1_ref)
     total[...] += lax.dot_general(
         x_ref[0], g, (((0,), (0,)), ((), ())), preferred_element_type=F32
     )
 
     @pl.when(i == pl.num_programs(0) - 1)
     def _():
-        o_ref[...] = total[...].astype(BF16)
-
-
-def project_weights(x, grads, table):
+        rows, half = ac.shape[1:]
+        for r in range(2):
+            for out, flips in ((ac, 2 * r), (as_, 1 + 2 * r)):
+                at = pl.ds(pl.multiple_of((place[0] ^ flips) * rows, rows), rows)
+                out[r] = total[at, :half].astype(BF16)
+            for out, flips in ((bc, r), (bs, 2 + r)):
+                at = pl.ds(pl.multiple_of((place[0] ^ flips) * rows, rows), rows)
+                out[r] = total[at, half:].astype(BF16)
+        gain_ref[...] = jnp.sum(total[...] * w_ref[...].astype(F32), axis=1, keepdims=True)
+
+
+def project_weights(x, grads, w, slot_of, place):
     count, rows, depth = x.shape
-    width = grads.shape[2]
-    return pl.pallas_call(
-        project_weights_kernel,
-        grid_spec=pltpu.PrefetchScalarGridSpec(
-            num_scalar_prefetch=1,
-            grid=(count,),
-            in_specs=[
-                pl.BlockSpec((1, rows, depth), lambda i, t: (t[i], 0, 0)),
-                pl.BlockSpec((3, rows, width), lambda i, t: (0, i, 0)),
-            ],
-            out_specs=pl.BlockSpec((depth, 3 * width), lambda i, t: (0, 0)),
-            scratch_shapes=[pltpu.VMEM((depth, 3 * width), F32)],
-        ),
-        out_shape=jax.ShapeDtypeStruct((depth, 3 * width), BF16),
-        compiler_params=params(1),
-        name="project_weights",
-    )(table, x, grads)
+    width = w.shape[1]
+    grad = pl.BlockSpec((3, rows, width // 6), lambda i, t, p: (0, i, 0))
+    quarter = depth // 4
+    piece = shaped(BF16, 2, quarter, width // 2), fixed(2, quarter, width // 2)
+    return call(
+        project_weights_kernel, "project_weights", (count,), [slot_of, place],
+        [
+            pl.BlockSpec((1, rows, depth), lambda i, t, p: (t[i], 0, 0)),
+            grad, grad, fixed(*w.shape),
+        ],
+        [piece, piece, piece, piece, (shaped(F32, depth, 1), fixed(depth, 1))],
+        [pltpu.VMEM((depth, width), F32)], 2 * count * rows * depth * width,
+        x, *grads, w,
+    )
+
+
+def mix_kernel(group, own, near, far, both, w_ref, x_ref, gain_ref,
+               heads_ref, hat_ref, scale_ref, hidden_ref, mid_ref):
+    width = own.shape[2]
+    for r, piece in enumerate((own[0], near[0], far[0], both[0])):
+        at = pl.ds(pl.multiple_of((group[0] ^ r) * width, width), width)
+        heads_ref[:, at] = piece
+    branch = jnp.dot(heads_ref[...], w_ref[...], preferred_element_type=F32)
+    hat, scale = normalized(branch)
+    hidden = x_ref[0].astype(F32) + hat * gain_ref[1:2, :]
+    hat_ref[...] = hat
+    scale_ref[...] = scale
+    hidden_ref[...] = hidden
+    mid_ref[...] = (normalized(hidden)[0] * gain_ref[2:3, :]).astype(BF16)
+
+
+def mix(group, local, near, far, both, w, x, gains):
+    _, rows, part = local.shape
+    count, _, width = x.shape
+    block = pl.BlockSpec((1, rows, part), lambda i, g: (i, 0, 0))
+    row = pl.BlockSpec((rows, width), lambda i, g: (i, 0))
+    total = count * rows
+    return call(
+        mix_kernel, "mix", (count,), [group],
+        [
+            block, block, block, block, fixed(*w.shape), pl.BlockSpec((1, rows, width), lambda i, g: (i, 0, 0)),
+            fixed(*gains.shape),
+        ],
+        [
+            (shaped(BF16, total, width), row),
+            (shaped(F32, total, width), row),
+            (shaped(F32, total, 1), pl.BlockSpec((rows, 1), lambda i, g: (i, 0))),
+            (shaped(F32, total, width), row),
+            (shaped(BF16, total, width), row),
+        ],
+        [], 2 * total * width * width, local, near, far, both, w, x, gains,
+    )
+
+
+def finish_kernel(terms_ref, sent_ref, hidden_ref, dy_ref, gain_ref, mixed_ref, grad_ref, sum_ref):
+    down = terms_ref[...] + sent_ref[...].astype(F32)
+    hat, scale = normalized(down)
+    gain = gain_ref[3:4, :]
+    dy = dy_ref[...].astype(F32)
+    mixed_ref[...] = (hidden_ref[...] + hat * gain).astype(BF16)
+    grad_ref[...] = normalized_back(hat, scale, dy * gain).astype(BF16)
+
+    @pl.when(pl.program_id(0) == 0)
+    def _():
+        sum_ref[...] = jnp.zeros_like(sum_ref)
+
+    sum_ref[...] += jnp.sum(dy * hat, axis=0, keepdims=True)
+
+
+def finish(terms, sent, hidden, dy, gains):
+    total, width = terms.shape
+    rows = total // 2
+    row = pl.BlockSpec((rows, width), lambda i: (i, 0))
+    return call(
+        finish_kernel, "finish", (2,), [],
+        [row, row, row, row, fixed(*gains.shape)],
+        [
+            (shaped(BF16, total, width), row), (shaped(BF16, total, width), row),
+            (shaped(F32, 1, width), fixed(1, width)),
+        ],
+        [], 20 * total * width, terms, sent, hidden, dy, gains,
+    )
+
+
+def turn_kernel(group, terms_ref, sent_ref, hidden_ref, dy_ref, hat_ref, scale_ref, w_ref, gain_ref,
+                keep_ref, branch_ref, heads_ref, three_ref, two_ref):
+    upstream = terms_ref[...] + sent_ref[...].astype(F32)
+    hat, scale = normalized(hidden_ref[...])
+
+    @pl.when(pl.program_id(0) == 0)
+    def _():
+        three_ref[...] = jnp.zeros_like(three_ref)
+        two_ref[...] = jnp.zeros_like(two_ref)
+
+    three_ref[...] += jnp.sum(upstream * hat, axis=0, keepdims=True)
+    grad = dy_ref[...].astype(F32) + normalized_back(hat, scale, upstream * gain_ref[2:3, :])
+    keep_ref[...] = grad
+    branch_hat = hat_ref[...]
+    two_ref[...] += jnp.sum(grad * branch_hat, axis=0, keepdims=True)
+    branch = normalized_back(branch_hat, scale_ref[...], grad * gain_ref[1:2, :]).astype(BF16)
+    branch_ref[...] = branch
+    part = heads_ref.shape[3]
+    for r in range(4):
+        at = pl.ds(pl.multiple_of((group[0] ^ r) * part, part), part)
+        heads_ref[r, 0] = dot_nt(branch, w_ref[at, :]).astype(BF16)
+
+
+def turn(group, terms, sent, hidden, dy, hat, scale, w, gains):
+    total, width = terms.shape
+    rows = total // 2
+    part = width // 4
+    row = pl.BlockSpec((rows, width), lambda i, g: (i, 0))
+    return call(
+        turn_kernel, "turn", (2,), [group],
+        [
+            row, row, row, row, row, pl.BlockSpec((rows, 1), lambda i, g: (i, 0)),
+            fixed(*w.shape), fixed(*gains.shape),
+        ],
+        [
+            (shaped(F32, total, width), row), (shaped(BF16, total, width), row),
+            (
+                shaped(BF16, 4, 2, rows, part),
+                pl.BlockSpec((4, 1, rows, part), lambda i, g: (0, i, 0, 0)),
+            ),
+            (shaped(F32, 1, width), fixed(1, width)), (shaped(F32, 1, width), fixed(1, width)),
+        ],
+        [], 2 * total * width * width, terms, sent, hidden, dy, hat, scale, w, gains,
+    )
+
+
+def end_kernel(keep_ref, near_ref, far_ref, x_ref, grad_ref, gain_ref, o_ref):
+    upstream = keep_ref[...] + near_ref[...].astype(F32) + far_ref[...].astype(F32)
+    hat, scale = normalized(x_ref[...].astype(F32))
+    grad = grad_ref[...] + normalized_back(hat, scale, upstream * gain_ref[0:1, :])
+    o_ref[...] = grad.astype(BF16)
+
+
+def end(keep, near, far, x, grad, gains):
+    rows, width = x.shape
+    return call(
+        end_kernel, "end", (1,), [],
+        [fixed(rows, width)] * 5 + [fixed(*gains.shape)],
+        [(shaped(BF16, rows, width), fixed(rows, width))],
+        [], 20 * rows * width, keep, near, far, x, grad, gains,
+    )[0]
 
 
 def flip(x, axis, bit):
@@ -690,17 +860,57 @@
     )
 
 
+def placed(first, mine, other, at):
+    return ordered(first, jnp.expand_dims(mine, at), jnp.expand_dims(other, at), at)
+
+
+def after(x, *others):
+    return lax.optimization_barrier((x, *others))[0]
+
+
+def all_after(group, *others):
+    return lax.optimization_barrier((*group, *others))[: len(group)]
+
+
+def plain(x):
+    return with_layout_constraint(x, Layout(tuple(range(x.ndim))))
+
+
+def total(a, b):
+    return (a.astype(F32) + b.astype(F32)).astype(BF16)
+
+
+def flip_both(x):
+    cp = lax.axis_size("cp")
+    return lax.ppermute(
+        x, ("core", "cp"), [(c * cp + z, (1 - c) * cp + (z ^ 1)) for c in range(2) for z in range(cp)]
+    )
+
+
 def dot(a, b, dims):
     return lax.dot_general(a, b, ((dims[:1], dims[1:]), ((), ())), preferred_element_type=F32)
 
 
 def gelu_and_slope(u):
-    inner = math.sqrt(2.0 / math.pi) * (u + 0.044715 * u * u * u)
-    t = jnp.tanh(inner)
-    slope = 0.5 * (1.0 + t) + 0.5 * u * (1.0 - t * t) * math.sqrt(2.0 / math.pi) * (
-        1.0 + 3.0 * 0.044715 * u * u
-    )
-    return 0.5 * u * (1.0 + t), slope
+    c = math.sqrt(2.0 / math.pi)
+    square = u * u
+    t = jnp.tanh(u * (c + (c * 0.044715) * square))
+    half = 0.5 + 0.5 * t
+    slope = half + (0.5 * u) * (1.0 - t * t) * (c + (3.0 * 0.044715 * c) * square)
+    return lax.optimization_barrier(((u * half).astype(BF16), slope.astype(BF16)))
+
+
+def pick(x, at, axis):
+    return lax.dynamic_index_in_dim(x, at, axis, False)
+
+
+def widened(z, x):
+    other = flip(x, "cp", 1)
+    first, second = jnp.where(z & 1 == 0, x, other), jnp.where(z & 1 == 0, other, x)
+    half = x.shape[1] // 2
+    return jnp.concatenate(
+        [first[:, :half], second[:, :half], first[:, half:], second[:, half:]], axis=1
+    )
 
 
 def body(tokens, doc_starts, qkv_weight, out_weight, up_weight, down_weight, norm_gains, cotangent):
@@ -714,58 +924,79 @@
     group = 2 * parity + core
     part = width // cp_count
     hidden_part = up_weight.shape[1] // 2
-
-    inputs = swap(tokens.reshape(own, width)).astype(F32)
-    upstream = swap(cotangent.reshape(own, width)).astype(F32)
-    other_starts = flip(doc_starts, "core", 1)
-    starts = jnp.where(core == z // (cp_count // 2), doc_starts, other_starts)[0]
-    gains = lax.all_gather(norm_gains, ("xy", "core", "cp"), axis=0, tiled=True)
-    gains = gains.astype(F32).reshape(4, width)
-
-    w = qkv_weight
-    for bit, at in ((2, 0), (1, 1)):
-        other = flip(w, "cp", bit)
-        w = ordered((z & bit) == 0, jnp.expand_dims(w, at), jnp.expand_dims(other, at), at)
+    lines_each = width // xy_count
+    lines = lines_each // 2
+    here = jnp.reshape(xy, (1,)).astype(jnp.int32)
+    group_at = jnp.reshape(group, (1,)).astype(jnp.int32)
+
+    w = jnp.concatenate([qkv_weight, out_weight], axis=1)
+    gain_rows = jnp.zeros((16, w.shape[1]), BF16)
+    gain_rows = lax.dynamic_update_slice(gain_rows, norm_gains[None], (0, 0))
+    w = jnp.concatenate([w, gain_rows])
+    x = tokens[0]
+    w_far = flip(w, "cp", 2)
+    x_half = [swap(x[0]), swap(x[1])]
+
+    up_weight, down_weight = all_after((up_weight, down_weight), w_far)
+
+    def half_of(which):
+        up = lax.dynamic_slice_in_dim(up_weight, which * hidden_part, hidden_part, 1)
+        down = lax.dynamic_slice_in_dim(down_weight, which * hidden_part, hidden_part, 0)
+        return plain(jnp.stack([up, down.T]))
+
+    ffn = ordered(core == 0, half_of(core), flip(half_of(1 - core), "core", 1), 1)
+
+    def paired(mine, other):
+        return jnp.concatenate(
+            [jnp.where(z & 2 == 0, mine, other), jnp.where(z & 2 == 0, other, mine)], axis=1
+        )
+
+    w = placed(z & 2 == 0, w, w_far, 0)
+    w = placed(z & 1 == 0, w, flip(w, "cp", 1), 1)
+    x_half[0] = after(x_half[0], w)
+    z_half = [flip(x_half[0], "cp", 1), flip(x_half[1], "cp", 1)]
+    up_lines = after(ffn[0], x_half[1])
+    up_lines = paired(up_lines, flip(up_lines, "cp", 2))
+
+    gain_rows = jnp.zeros((16, 3 * part), BF16)
+    gain_rows = lax.dynamic_update_slice(
+        gain_rows, w[:, :, lines, : norm_gains.shape[0]].reshape(cp_count, -1), (0, 0)
+    )
+    out_w = jnp.concatenate([w[a, b, :lines, 3 * part :] for a in range(2) for b in range(2)], axis=1)
 
     def columns(of):
         picked = []
         for third in range(3):
             block = third * cp_count + of
-            picked.append(
-                lax.dynamic_slice(
-                    w, (block // 6, (block // 3) & 1, 0, (block % 3) * part), (1, 1, w.shape[2], part)
-                )[0, 0]
-            )
-        return jnp.concatenate(picked, axis=1)
-
-    mine = columns(group)
-    other = flip(columns(group ^ 1), "core", 1)
-    qkv = ordered(core == 0, mine, other, 0)
-    for bit in (1, 2):
-        other = flip(qkv, "xy", bit)
-        qkv = ordered((xy & bit) == 0, qkv, other, 0)
-
-    def half_of(which):
-        up = lax.dynamic_slice_in_dim(up_weight, which * hidden_part, hidden_part, 1)
-        down = lax.dynamic_slice_in_dim(down_weight, which * hidden_part, hidden_part, 0)
-        return jnp.stack([up, down.T])
-
-    both = ordered(core == 0, half_of(core), flip(half_of(1 - core), "core", 1), 1)
-    ffn = lax.all_gather(both, ("xy", "cp"), axis=0)
-    ffn = ffn.reshape(xy_count, cp_count, 2, -1, hidden_part).transpose(2, 0, 3, 1, 4)
-    ffn = ffn.reshape(2, width, cp_count * hidden_part)
-    up_half, down_half = ffn[0], ffn[1]
-
-    out_w = out_weight
-    for bit in (1, 2):
-        other = flip(out_w, "cp", bit)
-        out_w = ordered((z & bit) == 0, out_w, other, 1)
-    out_w = out_w[None]
-    for bit in (1, 2):
-        other = flip(out_w, "xy", bit)
-        out_w = ordered((xy & bit) == 0, out_w, other, 0)
-    other = flip(out_w, "core", 1)
-    out_w = ordered(core == 0, out_w[:, None], other[:, None], 1).reshape(width, width)
+            at = (block // 6, (block // 3) & 1, 0, (block % 3) * part)
+            picked.append(lax.dynamic_slice(w, at, (1, 1, lines, part))[0, 0])
+        return jnp.concatenate([jnp.concatenate(picked, axis=1), gain_rows])
+
+    qkv = placed(core == 0, columns(group), flip(columns(group ^ 1), "core", 1), 0)
+    cut = qkv.shape[2] // 2
+    low, high = qkv[:, :, :cut], qkv[:, :, cut:]
+    low = placed(xy & 1 == 0, low, flip(low, "xy", 1), 0)
+    high = placed(xy & 2 == 0, high, flip(high, "xy", 2), 0)
+    low = placed(xy & 2 == 0, low, flip(low, "xy", 2), 0)
+    high = placed(xy & 1 == 0, high, flip(high, "xy", 1), 1)
+    qkv = jnp.concatenate([low[:, :, :, :lines], high[:, :, :, :lines]], axis=4)
+    qkv = qkv.reshape(width, 3 * part)
+    gains = low[:, :, :, lines : lines + cp_count, : norm_gains.shape[0]]
+    gains = gains.reshape(4, width).astype(F32)
+
+    x = jnp.stack(x_half)
+    x_core = flip(x, "core", 1)
+    x_chip = jnp.stack(z_half)
+    x_both = flip(x_chip, "core", 1)
+    other_starts = flip(after(doc_starts, w_far), "core", 1)
+    starts = jnp.where(core == z // (cp_count // 2), doc_starts, other_starts)[0]
+
+    up_lines = widened(z, after(up_lines, x_chip))
+    up_full = lax.all_gather(after(up_lines, qkv), "xy", axis=0, tiled=True)
+    down_lines = after(ffn[1], x_chip)
+    down_lines = paired(down_lines, flip(down_lines, "cp", 2))
+    out_w = after(out_w, x_chip)[None]
+    out_w = ordered(xy & 1 == 0, out_w, flip(out_w, "xy", 1), 0)
 
     block_id = jnp.arange(blocks, dtype=jnp.int32)[:, None]
     inside = jnp.arange(span, dtype=jnp.int32)[None, :]
@@ -797,109 +1028,190 @@
     chunk_of = 2 * ((relative >> 1) ^ core) + ((relative & 1) ^ parity)
     block_of = jnp.where(slot & 1 == 0, chunk_of, blocks - 1 - chunk_of).astype(jnp.int32)
 
-    normed_in = layer_norm(inputs)
-    normed = (normed_in * gains[0]).astype(BF16).reshape(2, span, width)
-    pair = jnp.concatenate([normed, flip(normed, "cp", 1)], axis=0)
-    slots = jnp.concatenate([pair, flip(pair, "core", 1)], axis=0)
-    q, k, v = project(slots, qkv, cosine, sine, slot_of)
-    attended, attended_low, lse = attend(q, k, v, pcol, prow, srow, bounds, tile)
-    local = reorder(attended_low.reshape(blocks, span, part), block_of)
-    from_core = flip(local[4:], "core", 1)
-    from_chip = flip(jnp.stack([local[2:4], from_core[2:4]]), "cp", 1)
-    pieces = jnp.concatenate([jnp.stack([local[:2], from_core[:2]]), from_chip]).reshape(
-        4, own, part
-    )
-    heads = jnp.concatenate(
-        [lax.dynamic_index_in_dim(pieces, g ^ group, 0, False) for g in range(4)], axis=1
-    )
-    branch = dot(heads, out_w, (1, 0))
-    branch_hat = layer_norm(branch)
-    hidden = inputs + branch_hat * gains[1]
-    hidden_hat = layer_norm(hidden)
-    normed_mid = (hidden_hat * gains[2]).astype(BF16)
-
-    ffn_in = jnp.concatenate([normed_mid, flip(normed_mid, "core", 1)])
-    act, slope = gelu_and_slope(dot(ffn_in, up_half, (1, 0)))
-    act, slope = act.astype(BF16), slope.astype(BF16)
-    terms = dot(act, down_half, (1, 1))
-    down = terms[:own] + flip(terms[own:].astype(BF16), "core", 1).astype(F32)
-    down_hat = layer_norm(down)
-    mixed = swap((hidden + down_hat * gains[3]).astype(BF16)).reshape(tokens.shape)
-
-    gain_four = jnp.sum(upstream * down_hat, axis=0)
-    grad_down = norm_back(down, upstream * gains[3]).astype(BF16)
+    q, k, v, normed = project([x, x_chip, x_core, x_both], gains, qkv, cosine, sine, slot_of)
+    down_lines, out_w = all_after((down_lines, out_w), q)
+    down_lines = widened(z, down_lines)
+    out_w = ordered(xy & 2 == 0, out_w, flip(out_w, "xy", 2), 0)
+    attended, local, lse = attend(q, k, v, pcol, prow, srow, bounds, slot_of, tile)
+    down_lines, out_w, dy = all_after((down_lines, out_w, cotangent), local)
+    down_full = lax.all_gather(down_lines, "xy", axis=0, tiled=True)
+    out_w = placed(core == 0, out_w, flip(out_w, "core", 1), 1).reshape(width, width)
+    heads, branch_hat, branch_scale, hidden, mid = mix(
+        group_at, local[:2], flip(local[4:6], "core", 1), flip(local[2:4], "cp", 1),
+        flip_both(local[6:]), out_w, x, gains,
+    )
+
+    dy = swap(after(dy.reshape(own, width), mid))
+
+    ffn_in = jnp.concatenate([mid, flip(mid, "core", 1)])
+    act, slope = gelu_and_slope(dot(ffn_in, up_full, (1, 0)))
+    sent = flip(dot(act[own:], down_full, (1, 1)).astype(BF16), "core", 1)
+    terms = dot(act[:own], down_full, (1, 1))
+    mixed, grad_down, gain_four = finish(terms, sent, hidden, dy, gains)
     grad_down = jnp.concatenate([grad_down, flip(grad_down, "core", 1)])
-    grad_up = (dot(grad_down, down_half, (1, 0)) * slope.astype(F32)).astype(BF16)
-    terms = dot(grad_up, up_half, (1, 1))
-    grad_mid = terms[:own] + flip(terms[own:].astype(BF16), "core", 1).astype(F32)
-    up_local = dot(ffn_in, grad_up, (0, 0)).astype(BF16)
-    down_local = dot(grad_down, act, (0, 0)).astype(BF16)
-
-    gain_three = jnp.sum(grad_mid * hidden_hat, axis=0)
-    grad_hidden = upstream + norm_back(hidden, grad_mid * gains[2])
-    gain_two = jnp.sum(grad_hidden * branch_hat, axis=0)
-    grad_branch = norm_back(branch, grad_hidden * gains[1]).astype(BF16)
-    grad_heads = dot(grad_branch, out_w, (1, 1)).astype(BF16)
+
+    x_bit, y_bit = xy & 1, xy >> 1
+
+    def cut_first(grads, extra):
+        grads = grads.reshape(2, 2, 2, lines, -1)
+        low, high = grads[:, :, 0], grads[:, :, 1]
+        if extra is not None:
+            extra = extra.reshape(2, 2, 2, -1, extra.shape[-1])
+            low = jnp.concatenate([low, extra[:, :, 0]], axis=2)
+            high = jnp.concatenate([high, extra[:, :, 1]], axis=2)
+        away = pick(low, 1 - x_bit, 1), pick(high, 1 - y_bit, 0)
+        return (pick(low, x_bit, 1), pick(high, y_bit, 0)), away
+
+    def send_first(away):
+        return flip(away[0], "xy", 1), flip(away[1], "xy", 2)
+
+    def cut_second(near, far):
+        away = (
+            total(pick(near[0], 1 - y_bit, 0), pick(far[0], 1 - y_bit, 0)),
+            total(pick(near[1], 1 - x_bit, 0), pick(far[1], 1 - x_bit, 0)),
+        )
+        near = (
+            total(pick(near[0], y_bit, 0), pick(far[0], y_bit, 0)),
+            total(pick(near[1], x_bit, 0), pick(far[1], x_bit, 0)),
+        )
+        return near, away
+
+    def send_second(away):
+        return flip(away[0], "xy", 2), flip(away[1], "xy", 1)
+
+    def cut_third(near, far):
+        sums = jnp.concatenate([total(a, b) for a, b in zip(near, far)])
+        blocks_of = [sums[:, n * hidden_part : (n + 1) * hidden_part] for n in range(cp_count)]
+        odd = jnp.stack([blocks_of[1], blocks_of[3]])
+        even = jnp.stack([blocks_of[0], blocks_of[2]])
+        return jnp.where(parity == 0, even, odd), jnp.where(parity == 0, odd, even)
+
+    def cut_fourth(near, far):
+        return (
+            total(pick(near, z >> 1, 0), pick(far, z >> 1, 0)),
+            total(pick(near, 1 - (z >> 1), 0), pick(far, 1 - (z >> 1), 0)),
+        )
+
+    down_local = plain(dot(grad_down, act, (0, 0)).astype(BF16))
+    down_near, down_away = cut_first(down_local, None)
+    down_far = send_first(down_away)
+    grad_up = dot(after(grad_down, *down_away), down_full, (1, 0)) * slope.astype(F32)
+    grad_up = grad_up.astype(BF16)
+    sent = flip(dot(grad_up[own:], up_full, (1, 1)).astype(BF16), "core", 1)
+    terms = dot(grad_up[:own], up_full, (1, 1))
+    grad_hidden, grad_branch, grad_heads, gain_three, gain_two = turn(
+        group_at, terms, sent, hidden, dy, branch_hat, branch_scale, out_w, gains
+    )
+
+    grad_local = [
+        grad_heads[0], flip(grad_heads[2], "cp", 1), flip(grad_heads[1], "core", 1),
+        flip_both(grad_heads[3]),
+    ]
     out_local = dot(heads, grad_branch, (0, 0)).astype(BF16)
-
-    cut = jnp.transpose(grad_heads.reshape(2, span, 4, part), (2, 0, 1, 3))
-    near = [lax.dynamic_index_in_dim(cut, group ^ r, 0, False) for r in range(4)]
-    from_chip = flip(jnp.stack([near[2], near[3]]), "cp", 1)
-    from_core = flip(jnp.concatenate([near[1], from_chip[1]]), "core", 1)
-    grad_local = jnp.concatenate([near[0], from_chip[0], from_core])
-    grad_local = reorder(grad_local, slot_of).reshape(row_len, part)
-    grad_linear = attend_back(
-        q, k, v, grad_local, attended, lse, pcol, prow, srow, cosine, sine, bounds, tile
-    )
-    terms = project_back(grad_linear, qkv, slot_of)
-    pair = terms[:4].astype(F32) + flip(terms[4:], "core", 1).astype(F32)
-    grad_normed = pair[:2] + flip(pair[2:].astype(BF16), "cp", 1).astype(F32)
-    grad_normed = grad_normed.reshape(own, width)
-    gain_one = jnp.sum(grad_normed * normed_in, axis=0)
-    tokens_grad = grad_hidden + norm_back(inputs, grad_normed * gains[0])
-    tokens_grad = swap(tokens_grad.astype(BF16)).astype(F32).reshape(tokens.shape)
-
-    out_local = out_local.reshape(xy_count, 2, width // xy_count // 2, width)
-    out_mine = lax.dynamic_index_in_dim(out_local, core, 1, False)
-    out_other = lax.dynamic_index_in_dim(out_local, 1 - core, 1, False)
-    out_pair = (out_mine.astype(F32) + flip(out_other, "core", 1).astype(F32)).astype(BF16)
-    out_rows = out_pair.shape[1]
-    out_pair = out_pair.reshape(xy_count, out_rows, cp_count, -1).transpose(0, 2, 1, 3)
-    out_cols = out_pair.shape[3]
-    rows_each = width // xy_count
-    sent = jnp.stack([up_local, down_local]).reshape(
-        2, xy_count, rows_each, cp_count, hidden_part
-    )
-    sent = sent.transpose(1, 3, 0, 2, 4).reshape(xy_count, cp_count, 2 * rows_each, hidden_part)
-    sent = jnp.concatenate([sent, out_pair.reshape(xy_count, cp_count, -1, hidden_part)], axis=2)
-    sent = lax.psum_scatter(sent, "xy", scatter_dimension=0)
-    sent = lax.psum_scatter(sent, "cp", scatter_dimension=0)
-    out_grad = sent[2 * rows_each :].reshape(out_rows, out_cols).astype(F32)
-    sent = sent[: 2 * rows_each].reshape(2, 2, rows_each // 2, hidden_part)
-    mine = lax.dynamic_index_in_dim(sent, core, 1, False)
-    other = flip(lax.dynamic_index_in_dim(sent, 1 - core, 1, False), "core", 1)
+    out_local = out_local.reshape(xy_count, 2, lines, width)
+    out_away = pick(out_local, 1 - core, 1)
+    out_sum = flip(out_away, "core", 1)
+    down_far = all_after(down_far, grad_heads)
+    down_near, down_away = cut_second(down_near, down_far)
+    down_far = send_second(down_away)
+    up_local = plain(dot(after(ffn_in, out_away), grad_up, (0, 0)).astype(BF16))
+    out_sum = total(pick(out_local, core, 1), out_sum)
+    out_sum = out_sum.reshape(xy_count, 2, lines // 2, cp_count, part)
+    out_sum = jnp.concatenate(
+        [out_sum[:, h, :, n] for n in range(cp_count) for h in range(2)], axis=-1
+    )
+    up_near, up_away = cut_first(up_local, out_sum)
+    up_far = send_first(up_away)
+    grad_local = after(jnp.concatenate(grad_local), *up_away, *down_away)
+
+    tables = (pcol, prow, srow, cosine, sine, bounds, slot_of, tile)
+    first = attend_back(0, q, k, v, grad_local, attended, lse, *tables)
+    down_far = all_after(down_far, first)
+    down_near, down_away = cut_third(down_near, down_far)
+    down_far = flip(down_away, "cp", 1)
+    second = attend_back(1, q, k, v, after(grad_local, first, down_away), attended, lse, *tables)
+    send = project_back((first, second), qkv, block_of[4:], span, BF16)
+    sent = flip(send, "core", 1)
+    up_far = all_after(up_far, send)
+    up_near, up_away = cut_second(up_near, up_far)
+    up_far = send_second(up_away)
+    down_far = after(down_far, send)
+    down_near, down_away = cut_fourth(down_near, down_far)
+    down_far = flip(down_away, "cp", 2)
+    keep = project_back((after(first, send, *up_away, down_away), second), qkv, block_of[:4], span, F32)
+    far_away = [total(keep[2 + h], sent[2 + h]) for h in range(2)]
+    far = [flip(a, "cp", 1) for a in far_away]
+    low, low_send, high, high_send, gain_one = project_weights(
+        normed, (after(first, *far_away), second), qkv, slot_of, here
+    )
+    low_far, high_far = flip(low_send, "xy", 1), flip(high_send, "xy", 2)
+    up_far = all_after(up_far, low_send)
+    up_near, up_away = cut_third(up_near, up_far)
+    up_far = flip(up_away, "cp", 1)
+    tokens_grad = []
+    for h in range(2):
+        grad = end(
+            keep[h], sent[h], far[h], x[h], grad_hidden[h * span : (h + 1) * span], gains
+        )
+        tokens_grad.append(grad)
+    ended = tuple(tokens_grad)
+    tokens_grad = [swap(grad) for grad in tokens_grad]
+    tokens_grad = jnp.stack(tokens_grad).astype(F32).reshape(tokens.shape)
+    mixed = swap(after(mixed, send)).reshape(tokens.shape)
+
+    low_send, low = total(low[1], low_far[1]), total(low[0], low_far[0])
+    high_send, high = total(high[1], high_far[1]), total(high[0], high_far[0])
+    low = total(low, flip(low_send, "xy", 2))
+    high = total(high, flip(high_send, "xy", 1))
+    both = jnp.concatenate([low, high], axis=1).reshape(2, lines, 3 * part)
+    mine, other = pick(both, core, 0), flip(pick(both, 1 - core, 0), "core", 1)
+    both = placed(core == 0, mine, other, 0).reshape(2, lines, 3, part).transpose(2, 0, 1, 3)
+    right = z >= 2
+    even = parity == 0
+    send_at = (
+        jnp.where(right, 0, jnp.where(even, 2, 1)), jnp.where(right, jnp.where(even, 1, 0), 2)
+    )
+    keep_at = (
+        jnp.where(right, jnp.where(even, 2, 1), 0), jnp.where(right, 2, jnp.where(even, 1, 0))
+    )
+    sent = flip(jnp.stack([pick(both, at, 0) for at in send_at]), "cp", 2)
+    both = total(jnp.stack([pick(both, at, 0) for at in keep_at]), sent)
+    sent = flip(pick(both, jnp.where(z == 0, 1, 0), 0), "cp", 1)
+
+    def choice(*four):
+        return jnp.where(
+            z == 0, four[0], jnp.where(z == 1, four[1], jnp.where(z == 2, four[2], four[3]))
+        )
+
+    qkv_grad = jnp.concatenate(
+        [
+            choice(both[0, 0], both[0, 1], sent[0], sent[1]),
+            choice(both[0, 1], sent[0], sent[1], both[1, 0]),
+            choice(sent[0], sent[1], both[0, 0], both[1, 1]),
+        ],
+        axis=1,
+    ).astype(F32)
+
+    up_near, up_away = cut_fourth(up_near, up_far)
+    up_sums = total(up_near, flip(up_away, "cp", 2))
+    down_sums = plain(total(down_near, down_far))
+    extra = lines // 4
+    out_grad = jnp.concatenate([up_sums[lines : lines + extra], up_sums[2 * lines + extra :]])
+    out_grad = jnp.concatenate([out_grad[:, :part], out_grad[:, part:]]).astype(F32)
+    both = jnp.stack([
+        jnp.stack([up_sums[:lines], up_sums[lines + extra : 2 * lines + extra]]),
+        down_sums.reshape(2, lines, hidden_part),
+    ], axis=1)
+    mine, other = pick(both, core, 0), flip(pick(both, 1 - core, 0), "core", 1)
     up_grad = ordered(core == 0, mine[0], other[0], 1).astype(F32)
     down_grad = ordered(core == 0, mine[1], other[1], 1).T.astype(F32)
 
-    qkv_local = project_weights(slots, grad_linear, slot_of)
-    qkv_local = qkv_local.reshape(xy_count, 2, rows_each // 2, 3 * part)
-    qkv_sum = lax.psum_scatter(qkv_local, "xy", scatter_dimension=0)
-    mine = lax.dynamic_index_in_dim(qkv_sum, core, 0, False)
-    other = flip(lax.dynamic_index_in_dim(qkv_sum, 1 - core, 0, False), "core", 1)
-    both = ordered(core == 0, mine[None], other[None], 0)
-    both = (both.astype(F32) + flip(both, "cp", 2).astype(F32)).astype(BF16)
-    every = ordered(parity == 0, both, flip(both, "cp", 1), 0)
-    every = every.reshape(4, rows_each // 2, 3, part).transpose(1, 2, 0, 3)
-    qkv_grad = lax.dynamic_slice_in_dim(
-        every.reshape(rows_each // 2, 3 * width), z * 3 * part, 3 * part, 1
-    ).astype(F32)
-
-    gain_local = jnp.concatenate([gain_one, gain_two, gain_three, gain_four]).reshape(-1, 128)
+    gain_one = gain_one.reshape(1, width) / gains[0:1]
+    gain_sum = jnp.concatenate([gain_one, gain_two, gain_three, gain_four]).reshape(-1, 128)
+    gain_sum = after(gain_sum, *ended)
     for axis, bit in (("core", 1), ("xy", 1), ("xy", 2), ("cp", 1), ("cp", 2)):
-        gain_local = gain_local + flip(gain_local, axis, bit)
-    gains_grad = lax.dynamic_index_in_dim(
-        gain_local, (2 * xy + core) * cp_count + z, 0, False
-    )
+        gain_sum = gain_sum + flip(gain_sum, axis, bit)
+    gains_grad = pick(gain_sum, (2 * xy + core) * cp_count + z, 0)
     return mixed, tokens_grad, qkv_grad, out_grad, up_grad, down_grad, gains_grad
 
 

time: 752 us -> 575 us (0.76)
  blocking collectives: 106 us -> 0 us
  waiting for transfers between devices: 242 us -> 185 us
  local copies, waits for them, and re-layouts: 78.9 us -> 41.5 us
  Pallas kernels: 114 us -> 141 us
  starting transfers between devices: 64 us -> 77.7 us
  other arithmetic: 65.5 us -> 56.5 us
    all_gather x1 -> x0, blocking collectives: 106 us -> none  [body(): gains = lax.all_gather(norm_gains, ('xy', 'core', 'cp'), axis=0, tiled=True)]
    unnamed x6 -> x2, waiting for transfers between devices: 57.5 us -> 0.03 us
    another operation x6 -> x8, local copies, waits for them, and re-layouts: 29.4 us -> 1.55 us  [the longest x2 1.02 us: half_of(): return plain(jnp.stack([up, down.T]))]
    ppermute x34 -> x57, waiting for transfers between devices: 185 us -> 161 us  [flip(): lax.ppermute(x, axis, [(i, i ^ bit) for i in range(lax.axis_size(axis))])]
    convert_element_type x8 -> x23, other arithmetic: 8.53 us -> 30.4 us  [the longest x19 26.5 us: total(): return (a.astype(F32) + b.astype(F32)).astype(BF16)]
    pallas_call x5 -> x9, Pallas kernels: 42.8 us -> 64 us  [call(): pl.pallas_call(kernel, grid_spec=pltpu.PrefetchScalarGridSpec(num_scalar_...]
    all_gather x1 -> x2, waiting for transfers between devices: 0.01 us -> 16.5 us  [the longest x1 16.4 us: body(): down_full = lax.all_gather(down_lines, 'xy', axis=0, tiled=True)]
    reshape x4 -> x2, local copies, waits for them, and re-layouts: 12.7 us -> 1.86 us  [the longest x1 1.85 us: body(): out_sum = out_sum.reshape(xy_count, 2, lines // 2, cp_count, part)]
  transfers between devices with their start and end apart: 42 -> 67, of which waited for: 21 -> 29; matrix products, arithmetic and copies ran while one was open for 18% -> 20% of each run, Pallas kernels for 15% -> 19%
where the time goes in v2:
time: 575 us; the launch traced here: 569 us
  waiting for transfers between devices  185 us (32%)
  Pallas kernels  141 us (25%)
  starting transfers between devices  77.7 us (14%)
  other arithmetic  56.5 us (10%)
  matrix products  52.1 us (9%)
  local copies, waits for them, and re-layouts  41.5 us (7%)
  between operations  16 us (3%)
    ppermute x57, waiting for transfers between devices, flip(): lax.ppermute(x, axis, [(i, i ^ bit) for i in range(lax.axis_size(axis))])  161 us
    pallas_call x9, Pallas kernels, call(): pl.pallas_call(kernel, grid_spec=pltpu.PrefetchScalarGridSpec(num_scalar_...  64 us
    ppermute x57, starting transfers between devices, flip(): lax.ppermute(x, axis, [(i, i ^ bit) for i in range(lax.axis_size(axis))])  54.3 us
    dot_general x9, matrix products, dot(): lax.dot_general(a, b, ((dims[:1], dims[1:]), ((), ())), preferred_element...  52.1 us
    pallas_call x2, Pallas kernels, attend_back(): pl.pallas_call(functools.partial(attend_back_kernel, tile), grid_spec=gri...  48 us
    pallas_call x1, Pallas kernels, attend(): pl.pallas_call(functools.partial(attend_kernel, tile), grid_spec=grid_spe...  28.6 us
    convert_element_type x19, other arithmetic, total(): return (a.astype(F32) + b.astype(F32)).astype(BF16)  26.5 us
    ppermute x6, starting transfers between devices, swap(): return lax.ppermute(x, ('core', 'cp'), pairs)  22.3 us
  transfers between devices with their start and end apart: 67, of which 29 were waited for; matrix products, arithmetic and copies ran while one was open for 20% of the time, Pallas kernels for 19%

profile of v2, /device:TPU:0, one launch (start us, length us, event | category | flops | bytes accessed | tf_op | source)
XLA Modules:
  0.0 568.9 jit_solution(7055927834579506944)
XLA Ops:
  8.3 4.1 collective-permute-start
  18.0 18.9 %collective-permute-done = bf16[144,1024]{1,0:T(8,128)(2,1)S(1)} collective-permute-done((bf16[144,1024]{1,0:T(8,128)(2,1)S(1)}, bf16[144,1024]{1,0:T(8,128)(2,1)S(1)}, u32[]{:S(2)}, u32[]{:S(2)}) %collective-permute-start) | collective-permute-done | bytes 294944 | tf_op jit(solution)/shard_map/ppermute | solution.py:844
  42.8 18.1 %collective-permute-done.3 = bf16[2,144,1024]{2,1,0:T(8,128)(2,1)S(1)} collective-permute-done((bf16[2,144,1024]{2,1,0:T(8,128)(2,1)S(1)}, bf16[2,144,1024]{2,1,0:T(8,128)(2,1)S(1)}, u32[]{:S(2)}, u32[]{:S(2)}) %collective-permute-start.3) | collective-permute-done | bytes 589856 | tf_op jit(solution)/shard_map/ppermute | solution.py:844
  67.1 21.9 %collective-permute-done.6 = bf16[256,1024]{1,0:T(8,128)(2,1)S(1)} collective-permute-done((bf16[256,1024]{1,0:T(8,128)(2,1)S(1)}, bf16[256,1024]{1,0:T(8,128)(2,1)S(1)}, u32[]{:S(2)}, u32[]{:S(2)}) %collective-permute-start.6) | collective-permute-done | bytes 524320 | tf_op jit(solution)/shard_map/ppermute | solution.py:844
  93.8 6.1 %collective-permute-done.10 = bf16[2,144,384]{2,1,0:T(8,128)(2,1)S(1)} collective-permute-done((bf16[2,144,384]{2,1,0:T(8,128)(2,1)S(1)}, bf16[2,144,384]{2,1,0:T(8,128)(2,1)S(1)}, u32[]{:S(2)}, u32[]{:S(2)}) %collective-permute-start.10) | collective-permute-done | bytes 221216 | tf_op jit(solution)/shard_map/ppermute | solution.py:844
  101.7 3.1 collective-permute-done.18
  105.8 2.4 collective-permute-done.13
  111.2 7.6 %collective-permute-done.25 = bf16[256,1024]{1,0:T(8,128)(2,1)S(1)} collective-permute-done((bf16[256,1024]{1,0:T(8,128)(2,1)S(1)}, bf16[256,1024]{1,0:T(8,128)(2,1)S(1)}, u32[]{:S(2)}, u32[]{:S(2)}) %collective-permute-start.25) | collective-permute-done | bytes 524320 | tf_op jit(solution)/shard_map/ppermute | solution.py:844
  132.2 8.9 %collective-permute-done.19 = bf16[1,128,1024]{2,1,0:T(8,128)(2,1)} collective-permute-done((bf16[1,128,1024]{2,1,0:T(8,128)(2,1)S(1)}, bf16[1,128,1024]{2,1,0:T(8,128)(2,1)}, u32[]{:S(2)}, u32[]{:S(2)}) %collective-permute-start.19) | collective-permute-done | bytes 262176 | tf_op jit(solution)/shard_map/ppermute | solution.py:844
  142.9 12.9 %project.1 = (bf16[2048,256]{1,0:T(8,128)(2,1)}, bf16[2048,256]{1,0:T(8,128)(2,1)}, bf16[2048,256]{1,0:T(8,128)(2,1)}, bf16[8,256,1024]{2,1,0:T(8,128)(2,1)}) custom-call(s32[8]{0:T(128)} %convert_add_fusion.13.slot_of, bf16[2,256,1024]{2,1,0:T(8,128)(2,1)} %copy-done.4, bf16[2,256,1024]{2,1,0:T(8,128)(2,1)} %pad_maximum_fusion.5.x1, ...), custom_call_target="tpu_custom_call" | custom-call | flops 3221225472 | bytes 15220736 | tf_op jit(solution)/shard_map/project/pallas_call | solution.py:587
  158.4 28.6 %attend.1 = (f32[2048,256]{1,0:T(8,128)}, bf16[8,256,256]{2,1,0:T(8,128)(2,1)}, f32[2,2,2048]{2,1,0:T(2,128)}) custom-call(s32[4,4]{1,0:T(4,128)} %pad_add_fusion.bounds, s32[8]{0:T(128)} %convert_add_fusion.13.slot_of, bf16[2048,256]{1,0:T(8,128)(2,1)} %get-tuple-element.68.q_ref, bf16[2048,256]{1,0:T(8,128)(2,1)} %get-tuple-element.69.k_ref, ...), custom_call_target="tpu_custom_call" | custom-call | flops 3221225472 | bytes 4194304 | tf_op jit(solution)/shard_map/attend/pallas_call | solution.py:426
  193.7 5.2 collective-permute-done.15.far
  198.9 5.0 collective-permute-done.16.both
  204.6 6.4 %mix.1 = (bf16[512,1024]{1,0:T(8,128)(2,1)}, f32[512,1024]{1,0:T(8,128)}, f32[512,1]{1,0:T(8,128)}, f32[512,1024]{1,0:T(8,128)}, bf16[512,1024]{1,0:T(8,128)(2,1)}) custom-call(s32[1]{0:T(128)} %bitcast.group, bf16[2,256,256]{2,1,0:T(8,128)(2,1)} %get-tuple-element.221.own, bf16[2,256,256]{2,1,0:T(8,128)(2,1)} %copy-done.25, ...), custom_call_target="tpu_custom_call" | custom-call | flops 1073741824 | bytes 10504192 | tf_op jit(solution)/shard_map/mix/pallas_call | solution.py:587
  211.5 2.4 collective-permute-start.27
  215.3 13.4 %add_convert_fusion = (bf16[1024,2048]{1,0:T(8,128)(2,1)}, bf16[1024,2048]{1,0:T(8,128)(2,1)}) fusion(bf16[1024,1024]{1,0:T(8,128)(2,1)S(1)} %constant_dynamic-update-slice_fusion, bf16[1024,2048]{1,0:T(8,128)(2,1)} %all-gather.3.cloned.1.call-done), kind=kOutput, calls=%fused_computation.1 | convolution fusion | flops 4330618880 | bytes 14680064 | tf_op jit(solution)/shard_map/dot_general | solution.py:891
  228.8 16.4 %all-gather.5.cloned.1.call-done = bf16[1024,2048]{1,0:T(8,128)(2,1)} async-done(((bf16[256,2048]{1,0:T(8,128)(2,1)}), bf16[1024,2048]{1,0:T(8,128)(2,1)}) %all-gather.5.cloned.1.call-update) | async-done | bytes 4194320 | tf_op jit(solution)/shard_map/all_gather | solution.py:1037
  245.2 5.3 fusion.10
  250.6 3.7 fusion.7.terms_ref
  255.6 4.6 finish.1
  263.3 7.1 %convolution_convert_fusion.1 = bf16[1024,2048]{1,0:T(8,128)(2,1)S(1)} fusion(bf16[1024,1024]{1,0:T(8,128)(2,1)S(1)} %constant_dynamic-update-slice_fusion.2, bf16[1024,2048]{1,0:T(8,128)(2,1)} %get-tuple-element.83), kind=kOutput, calls=%fused_computation.13 | convolution fusion | flops 4297064448 | bytes 10485760 | tf_op jit(solution)/shard_map/dot_general | solution.py:891
  275.4 4.9 multiply_convert_fusion
  280.3 3.4 fusion.13
  286.7 6.5 %fusion.2.terms_ref = f32[512,1024]{1,0:T(8,128)} fusion(bf16[1024,2048]{1,0:T(8,128)(2,1)} %all-gather.3.cloned.1.call-done, bf16[1024,2048]{1,0:T(8,128)(2,1)} %copy-done.41), kind=kOutput, calls=%fused_computation.39 | convolution fusion | flops 2147483648 | bytes 8388608 | tf_op jit(solution)/shard_map/dot_general | solution.py:891
  294.2 8.5 %turn.1 = (f32[512,1024]{1,0:T(8,128)}, bf16[512,1024]{1,0:T(8,128)(2,1)}, bf16[4,2,256,256]{3,2,1,0:T(8,128)(2,1)}, f32[1,1024]{1,0:T(1,128)}, f32[1,1024]{1,0:T(1,128)}) custom-call(s32[1]{0:T(128)} %bitcast.group, f32[512,1024]{1,0:T(8,128)} %fusion.2.terms_ref, bf16[512,1024]{1,0:T(8,128)(2,1)} %copy-done.19, f32[512,1024]{1,0:T(8,128)} %get-tuple-element.85.hidden_ref, ...), custom_call_target="tpu_custom_call" | custom-call | flops 1073741824 | bytes 14706688 | tf_op jit(solution)/shard_map/turn/pallas_call | solution.py:587
  302.7 2.7 convolution_convert_fusion.2
  306.7 3.2 collective-permute-done.35
  311.1 5.1 convolution_convert_fusion
  338.5 23.9 %attend_back.2.g0_ref = bf16[3,2048,128]{2,1,0:T(8,128)(2,1)} custom-call(s32[4,4]{1,0:T(4,128)} %pad_add_fusion.bounds, s32[8]{0:T(128)} %convert_add_fusion.13.slot_of, bf16[2048,256]{1,0:T(8,128)(2,1)} %get-tuple-element.68.q_ref, bf16[2048,256]{1,0:T(8,128)(2,1)} %get-tuple-element.69.k_ref, bf16[2048,256]{1,0:T(8,128)(2,1)} %get-tuple-element.70.v_ref, ...), custom_call_target="tpu_custom_call" | custom-call | flops 3758096384 | bytes 4718592 | tf_op jit(solution)/shard_map/attend_back/pallas_call | solution.py:545
  366.5 24.1 %attend_back.3.g1_ref = bf16[3,2048,128]{2,1,0:T(8,128)(2,1)} custom-call(s32[4,4]{1,0:T(4,128)} %pad_add_fusion.bounds, s32[8]{0:T(128)} %convert_add_fusion.13.slot_of, bf16[2048,256]{1,0:T(8,128)(2,1)} %get-tuple-element.68.q_ref, bf16[2048,256]{1,0:T(8,128)(2,1)} %get-tuple-element.69.k_ref, bf16[2048,256]{1,0:T(8,128)(2,1)} %get-tuple-element.70.v_ref, ...), custom_call_target="tpu_custom_call" | custom-call | flops 3758096384 | bytes 4718592 | tf_op jit(solution)/shard_map/attend_back/pallas_call | solution.py:545
  390.6 6.3 %project_back.2 = bf16[4,256,1024]{2,1,0:T(8,128)(2,1)} custom-call(s32[4]{0:T(128)} %get-tuple-element.296.table, bf16[3,2048,128]{2,1,0:T(8,128)(2,1)} %attend_back.2.g0_ref, bf16[3,2048,128]{2,1,0:T(8,128)(2,1)} %attend_back.3.g1_ref, bf16[1024,768]{1,0:T(8,128)(2,1)} %bitcast.399), custom_call_target="tpu_custom_call" | custom-call | flops 1610612736 | bytes 6815744 | tf_op jit(solution)/shard_map/project_back/pallas_call | solution.py:587
  401.6 9.5 %collective-permute-start.38 = (bf16[512,1024]{1,0:T(8,128)(2,1)}, bf16[512,1024]{1,0:T(8,128)(2,1)}, u32[]{:S(2)}, u32[]{:S(2)}) collective-permute-start(bf16[512,1024]{1,0:T(8,128)(2,1)} %get-tuple-element.106), channel_id=1, source_target_pairs={{4,2},{2,4},{0,0},{6,6},{5,3},{3,5},{1,1},{7,7},{12,10},{10,12},{8... | collective-permute-start | bytes 3145736 | tf_op jit(solution)/shard_map/ppermute | solution.py:854
  411.1 10.5 %collective-permute-done.41 = bf16[2,256,512]{2,1,0:T(8,128)(2,1)} collective-permute-done((bf16[2,256,512]{2,1,0:T(8,128)(2,1)}, bf16[2,256,512]{2,1,0:T(8,128)(2,1)}, u32[]{:S(2)}, u32[]{:S(2)}) %collective-permute-start.41) | collective-permute-done | bytes 524320 | tf_op jit(solution)/shard_map/ppermute | solution.py:844
  423.3 3.3 fusion.109
  426.6 14.9 %collective-permute-done.58 = bf16[256,512]{1,0:T(8,128)(2,1)S(1)} collective-permute-done((bf16[256,512]{1,0:T(8,128)(2,1)S(1)}, bf16[256,512]{1,0:T(8,128)(2,1)S(1)}, u32[]{:S(2)}, u32[]{:S(2)}) %collective-permute-start.58) | collective-permute-done | bytes 262176 | tf_op jit(solution)/shard_map/ppermute | solution.py:844
  446.5 6.8 %project_back.3 = f32[4,256,1024]{2,1,0:T(8,128)} custom-call(s32[4]{0:T(128)} %get-tuple-element.295.table, bf16[3,2048,128]{2,1,0:T(8,128)(2,1)} %attend_back.2.g0_ref, bf16[3,2048,128]{2,1,0:T(8,128)(2,1)} %attend_back.3.g1_ref, bf16[1024,768]{1,0:T(8,128)(2,1)} %bitcast.400), custom_call_target="tpu_custom_call" | custom-call | flops 1610612736 | bytes 8912896 | tf_op jit(solution)/shard_map/project_back/pallas_call | solution.py:587
  453.3 4.5 fusion.40
  459.9 11.3 %project_weights.1 = (bf16[2,256,384]{2,1,0:T(8,128)(2,1)}, bf16[2,256,384]{2,1,0:T(8,128)(2,1)}, bf16[2,256,384]{2,1,0:T(8,128)(2,1)}, bf16[2,256,384]{2,1,0:T(8,128)(2,1)}, f32[1024,1]{1,0:T(8,128)}) custom-call(s32[8]{0:T(128)} %convert_add_fusion.13.slot_of, s32[1]{0:T(128)} %bitcast.98.place, bf16[8,256,1024]{2,1,0:T(8,128)(2,1)} %get-tuple-element.112.x_ref, ...), custom_call_target="tpu_custom_call" | custom-call | flops 3221225472 | bytes 10489856 | tf_op jit(solution)/shard_map/project_weights/pallas_call | solution.py:587
  482.3 3.6 end.2
  486.0 3.6 end.3
  499.2 5.4 collective-permute-start.46
  507.9 3.3 collective-permute-done.63
  511.2 6.9 %collective-permute-start.64 = (f32[32,128]{1,0:T(8,128)S(1)}, f32[32,128]{1,0:T(8,128)S(1)}, u32[]{:S(2)}, u32[]{:S(2)}) collective-permute-start(f32[32,128]{1,0:T(8,128)S(1)} %add.561), channel_id=1, source_target_pairs={{0,2},{1,3},{2,0},{3,1},{4,6},{5,7},{6,4},{7,5},{8,10},{9,11},{10,... | collective-permute-start | bytes 49160 | tf_op jit(solution)/shard_map/ppermute | solution.py:844
  518.5 14.3 %collective-permute-done.64 = f32[32,128]{1,0:T(8,128)S(1)} collective-permute-done((f32[32,128]{1,0:T(8,128)S(1)}, f32[32,128]{1,0:T(8,128)S(1)}, u32[]{:S(2)}, u32[]{:S(2)}) %collective-permute-start.64) | collective-permute-done | bytes 16416 | tf_op jit(solution)/shard_map/ppermute | solution.py:844
  535.6 2.9 collective-permute-start.52
  538.7 9.2 %collective-permute-done.57 = bf16[320,512]{1,0:T(8,128)(2,1)S(1)} collective-permute-done((bf16[320,512]{1,0:T(8,128)(2,1)S(1)}, bf16[320,512]{1,0:T(8,128)(2,1)S(1)}, u32[]{:S(2)}, u32[]{:S(2)}) %collective-permute-start.57) | collective-permute-done | bytes 327712 | tf_op jit(solution)/shard_map/ppermute | solution.py:844
  552.0 2.5 maximum_convert_fusion
  554.5 2.4 collective-permute-done.53
  (369 shorter events, 147.4 us)
Async XLA Ops:
  7.2 208.1 %all-gather.3.cloned.1.call-start = ((), (), s32[]{:S(2)}) async-start(), calls=%async_computation | async-start | bytes 5242880 | tf_op jit(solution)/shard_map/all_gather | solution.py:995
  8.3 28.7 %collective-permute-start = (bf16[144,1024]{1,0:T(8,128)(2,1)S(1)}, bf16[144,1024]{1,0:T(8,128)(2,1)S(1)}, u32[]{:S(2)}, u32[]{:S(2)}) collective-permute-start(bf16[144,1024]{1,0:T(8,128)(2,1)S(1)} %fusion.55), channel_id=1, source_target_pairs={{0,2},{1,3},{2,0},{3,1},{4,6},{5,7},{6,4},{7,5},{8,10},{9,11},{10,... | collective-permute-start | bytes 884744 | tf_op jit(solution)/shard_map/ppermute | solution.py:844
  14.7 26.3 %collective-permute-start.4 = (bf16[256,1024]{1,0:T(8,128)(2,1)}, bf16[256,1024]{1,0:T(8,128)(2,1)S(1)}, u32[]{:S(2)}, u32[]{:S(2)}) collective-permute-start(bf16[256,1024]{1,0:T(8,128)(2,1)} %get-tuple-element.227), channel_id=1, source_target_pairs={{4,2},{2,4},{0,0},{6,6},{5,3},{3,5},{1,1},{7,7},{12,10},{10,12},{8... | collective-permute-start | bytes 1572872 | tf_op jit(solution)/shard_map/ppermute | solution.py:854
  16.4 23.4 %collective-permute-start.2 = (bf16[256,1024]{1,0:T(8,128)(2,1)}, bf16[256,1024]{1,0:T(8,128)(2,1)S(1)}, u32[]{:S(2)}, u32[]{:S(2)}) collective-permute-start(bf16[256,1024]{1,0:T(8,128)(2,1)} %get-tuple-element.226), channel_id=1, source_target_pairs={{4,2},{2,4},{0,0},{6,6},{5,3},{3,5},{1,1},{7,7},{12,10},{10,12},{8... | collective-permute-start | bytes 1572872 | tf_op jit(solution)/shard_map/ppermute | solution.py:854
  37.2 23.8 %collective-permute-start.3 = (bf16[2,144,1024]{2,1,0:T(8,128)(2,1)S(1)}, bf16[2,144,1024]{2,1,0:T(8,128)(2,1)S(1)}, u32[]{:S(2)}, u32[]{:S(2)}) collective-permute-start(bf16[2,144,1024]{2,1,0:T(8,128)(2,1)S(1)} %pad_maximum_fusion.12), channel_id=1, source_target_pairs={{0,1},{1,0},{2,3},{3,2},{4,5},{5,4},{6,7},{7,6},{8,9},{9,8},{10,11... | collective-permute-start | bytes 1769480 | tf_op jit(solution)/shard_map/ppermute | solution.py:844
  39.7 49.2 %collective-permute-start.5 = (bf16[256,1024]{1,0:T(8,128)(2,1)S(1)}, bf16[256,1024]{1,0:T(8,128)(2,1)S(1)}, u32[]{:S(2)}, u32[]{:S(2)}) collective-permute-start(bf16[256,1024]{1,0:T(8,128)(2,1)S(1)} %collective-permute-done.2.x_ref), channel_id=1, source_target_pairs={{0,1},{1,0},{2,3},{3,2},{4,5},{5,4},{6,7},{7,6},{8,9},{9,8},{10,11... | collective-permute-start | bytes 1572872 | tf_op jit(solution)/shard_map/ppermute | solution.py:844
  41.0 47.9 %collective-permute-start.6 = (bf16[256,1024]{1,0:T(8,128)(2,1)S(1)}, bf16[256,1024]{1,0:T(8,128)(2,1)S(1)}, u32[]{:S(2)}, u32[]{:S(2)}) collective-permute-start(bf16[256,1024]{1,0:T(8,128)(2,1)S(1)} %collective-permute-done.4.x_ref), channel_id=1, source_target_pairs={{0,1},{1,0},{2,3},{3,2},{4,5},{5,4},{6,7},{7,6},{8,9},{9,8},{10,11... | collective-permute-start | bytes 1572872 | tf_op jit(solution)/shard_map/ppermute | solution.py:844
  63.8 29.4 %collective-permute-start.12 = (bf16[2,144,384]{2,1,0:T(8,128)(2,1)S(1)}, bf16[2,144,384]{2,1,0:T(8,128)(2,1)S(1)}, u32[]{:S(2)}, u32[]{:S(2)}) collective-permute-start(bf16[2,144,384]{2,1,0:T(8,128)(2,1)S(1)} %get-tuple-element.263), channel_id=1, source_target_pairs={{0,16},{8,24},{16,0},{24,8},{1,17},{9,25},{17,1},{25,9},{2,18},{10... | collective-permute-start | bytes 663560 | tf_op jit(solution)/shard_map/ppermute | solution.py:844
  65.5 36.2 %collective-permute-start.24 = (bf16[256,512]{1,0:T(8,128)(2,1)S(1)}, bf16[256,512]{1,0:T(8,128)(2,1)S(1)}, u32[]{:S(2)}, u32[]{:S(2)}) collective-permute-start(bf16[256,512]{1,0:T(8,128)(2,1)S(1)} %get-tuple-element.80), channel_id=1, source_target_pairs={{0,2},{1,3},{2,0},{3,1},{4,6},{5,7},{6,4},{7,5},{8,10},{9,11},{10,... | collective-permute-start | bytes 786440 | tf_op jit(solution)/shard_map/ppermute | solution.py:844
  90.0 14.7 %collective-permute-start.18 = (bf16[256,512]{1,0:T(8,128)(2,1)S(1)}, bf16[256,512]{1,0:T(8,128)(2,1)S(1)}, u32[]{:S(2)}, u32[]{:S(2)}) collective-permute-start(bf16[256,512]{1,0:T(8,128)(2,1)S(1)} %get-tuple-element.74), channel_id=1, source_target_pairs={{0,2},{1,3},{2,0},{3,1},{4,6},{5,7},{6,4},{7,5},{8,10},{9,11},{10,... | collective-permute-start | bytes 786440 | tf_op jit(solution)/shard_map/ppermute | solution.py:844
  93.2 14.9 %collective-permute-start.13 = (bf16[2,2,144,384]{3,2,1,0:T(8,128)(2,1)S(1)}, bf16[2,2,144,384]{3,2,1,0:T(8,128)(2,1)S(1)}, u32[]{:S(2)}, u32[]{:S(2)}) collective-permute-start(bf16[2,2,144,384]{3,2,1,0:T(8,128)(2,1)S(1)} %pad_maximum_fusion.20), channel_id=1, source_target_pairs={{0,8},{8,0},{16,24},{24,16},{1,9},{9,1},{17,25},{25,17},{2,10},{10... | collective-permute-start | bytes 1327112 | tf_op jit(solution)/shard_map/ppermute | solution.py:844
  100.1 9.7 %collective-permute-start.11 = (bf16[2,2,144,384]{3,2,1,0:T(8,128)(2,1)S(1)}, bf16[2,2,144,384]{3,2,1,0:T(8,128)(2,1)S(1)}, u32[]{:S(2)}, u32[]{:S(2)}) collective-permute-start(bf16[2,2,144,384]{3,2,1,0:T(8,128)(2,1)S(1)} %pad_maximum_fusion.19), channel_id=1, source_target_pairs={{0,16},{8,24},{16,0},{24,8},{1,17},{9,25},{17,1},{25,9},{2,18},{10... | collective-permute-start | bytes 1327112 | tf_op jit(solution)/shard_map/ppermute | solution.py:844
  105.7 13.1 %collective-permute-start.25 = (bf16[256,1024]{1,0:T(8,128)(2,1)S(1)}, bf16[256,1024]{1,0:T(8,128)(2,1)S(1)}, u32[]{:S(2)}, u32[]{:S(2)}) collective-permute-start(bf16[256,1024]{1,0:T(8,128)(2,1)S(1)} %pad_maximum_fusion.16), channel_id=1, source_target_pairs={{0,1},{1,0},{2,3},{3,2},{4,5},{5,4},{6,7},{7,6},{8,9},{9,8},{10,11... | collective-permute-start | bytes 1572872 | tf_op jit(solution)/shard_map/ppermute | solution.py:844
  120.1 125.1 %all-gather.5.cloned.1.call-start = ((), (), s32[]{:S(2)}) async-start(), calls=%async_computation.1 | async-start | bytes 5242880 | tf_op jit(solution)/shard_map/all_gather | solution.py:1037
  125.1 17.7 %collective-permute-start.7 = (bf16[2,256,1024]{2,1,0:T(8,128)(2,1)S(1)}, bf16[2,256,1024]{2,1,0:T(8,128)(2,1)}, u32[]{:S(2)}, u32[]{:S(2)}) collective-permute-start(bf16[2,256,1024]{2,1,0:T(8,128)(2,1)S(1)} %pad_maximum_fusion.4.x0.x_ref), channel_id=1, source_target_pairs={{0,4},{4,0},{1,5},{5,1},{2,6},{6,2},{3,7},{7,3},{8,12},{12,8},{9,1... | collective-permute-start | bytes 3145736 | tf_op jit(solution)/shard_map/ppermute | solution.py:844
  126.3 16.5 %collective-permute-start.8 = (bf16[2,256,1024]{2,1,0:T(8,128)(2,1)}, bf16[2,256,1024]{2,1,0:T(8,128)(2,1)}, u32[]{:S(2)}, u32[]{:S(2)}) collective-permute-start(bf16[2,256,1024]{2,1,0:T(8,128)(2,1)} %pad_maximum_fusion.5.x1), channel_id=1, source_target_pairs={{0,4},{4,0},{1,5},{5,1},{2,6},{6,2},{3,7},{7,3},{8,12},{12,8},{9,1... | collective-permute-start | bytes 3145736 | tf_op jit(solution)/shard_map/ppermute | solution.py:844
  127.5 13.6 %collective-permute-start.19 = (bf16[1,128,1024]{2,1,0:T(8,128)(2,1)S(1)}, bf16[1,128,1024]{2,1,0:T(8,128)(2,1)}, u32[]{:S(2)}, u32[]{:S(2)}) collective-permute-start(bf16[1,128,1024]{2,1,0:T(8,128)(2,1)S(1)} %bitcast.416), channel_id=1, source_target_pairs={{0,8},{8,0},{16,24},{24,16},{1,9},{9,1},{17,25},{25,17},{2,10},{10... | collective-permute-start | bytes 786440 | tf_op jit(solution)/shard_map/ppermute | solution.py:844
  155.8 31.1 %collective-permute-start.21 = (bf16[2,128,1024]{2,1,0:T(8,128)(2,1)S(1)}, bf16[2,128,1024]{2,1,0:T(8,128)(2,1)S(1)}, u32[]{:S(2)}, u32[]{:S(2)}) collective-permute-start(bf16[2,128,1024]{2,1,0:T(8,128)(2,1)S(1)} %pad_maximum_fusion.15), channel_id=1, source_target_pairs={{0,16},{8,24},{16,0},{24,8},{1,17},{9,25},{17,1},{25,9},{2,18},{10... | collective-permute-start | bytes 1572872 | tf_op jit(solution)/shard_map/ppermute | solution.py:844
  158.4 28.8 %collective-permute-start.20 = (bf16[256,1024]{1,0:T(8,128)(2,1)S(1)}, bf16[256,1024]{1,0:T(8,128)(2,1)S(1)}, u32[]{:S(2)}, u32[]{:S(2)}) collective-permute-start(bf16[256,1024]{1,0:T(8,128)(2,1)S(1)} %pad_maximum_fusion.14), channel_id=1, source_target_pairs={{0,1},{1,0},{2,3},{3,2},{4,5},{5,4},{6,7},{7,6},{8,9},{9,8},{10,11... | collective-permute-start | bytes 1572872 | tf_op jit(solution)/shard_map/ppermute | solution.py:844
  191.8 12.1 %collective-permute-start.16 = (bf16[2,256,256]{2,1,0:T(8,128)(2,1)S(1)}, bf16[2,256,256]{2,1,0:T(8,128)(2,1)S(1)}, u32[]{:S(2)}, u32[]{:S(2)}) collective-permute-start(bf16[2,256,256]{2,1,0:T(8,128)(2,1)S(1)} %get-tuple-element.218), channel_id=1, source_target_pairs={{0,5},{1,4},{2,7},{3,6},{4,1},{5,0},{6,3},{7,2},{8,13},{9,12},{10,... | collective-permute-start | bytes 786440 | tf_op jit(solution)/shard_map/ppermute | solution.py:885
  211.5 42.8 %collective-permute-start.27 = (bf16[512,1024]{1,0:T(8,128)(2,1)}, bf16[512,1024]{1,0:T(8,128)(2,1)S(1)}, u32[]{:S(2)}, u32[]{:S(2)}) collective-permute-start(bf16[512,1024]{1,0:T(8,128)(2,1)} %bitcast.54), channel_id=1, source_target_pairs={{4,2},{2,4},{0,0},{6,6},{5,3},{3,5},{1,1},{7,7},{12,10},{10,12},{8... | collective-permute-start | bytes 3145736 | tf_op jit(solution)/shard_map/ppermute | solution.py:854
  284.7 25.2 %collective-permute-start.35 = (bf16[2,128,2048]{2,1,0:T(8,128)(2,1)S(1)}, bf16[2,128,2048]{2,1,0:T(8,128)(2,1)S(1)}, u32[]{:S(2)}, u32[]{:S(2)}) collective-permute-start(bf16[2,128,2048]{2,1,0:T(8,128)(2,1)S(1)} %dynamic-slice_bitcast_fusion.1), channel_id=1, source_target_pairs={{0,16},{8,24},{16,0},{24,8},{1,17},{9,25},{17,1},{25,9},{2,18},{10... | collective-permute-start | bytes 3145736 | tf_op jit(solution)/shard_map/ppermute | solution.py:844
  286.1 24.9 %collective-permute-start.34 = (bf16[2,128,2048]{2,1,0:T(8,128)(2,1)S(1)}, bf16[2,128,2048]{2,1,0:T(8,128)(2,1)S(1)}, u32[]{:S(2)}, u32[]{:S(2)}) collective-permute-start(bf16[2,128,2048]{2,1,0:T(8,128)(2,1)S(1)} %dynamic-slice_bitcast_fusion.2), channel_id=1, source_target_pairs={{0,8},{8,0},{16,24},{24,16},{1,9},{9,1},{17,25},{25,17},{2,10},{10... | collective-permute-start | bytes 3145736 | tf_op jit(solution)/shard_map/ppermute | solution.py:844
  305.5 23.7 %collective-permute-start.33 = (bf16[4,128,1024]{2,1,0:T(8,128)(2,1)S(1)}, bf16[4,128,1024]{2,1,0:T(8,128)(2,1)S(1)}, u32[]{:S(2)}, u32[]{:S(2)}) collective-permute-start(bf16[4,128,1024]{2,1,0:T(8,128)(2,1)S(1)} %dynamic-slice_bitcast_fusion), channel_id=1, source_target_pairs={{0,4},{4,0},{1,5},{5,1},{2,6},{6,2},{3,7},{7,3},{8,12},{12,8},{9,1... | collective-permute-start | bytes 3145736 | tf_op jit(solution)/shard_map/ppermute | solution.py:844
  317.8 10.3 %collective-permute-start.32 = (bf16[2,256,256]{2,1,0:T(8,128)(2,1)S(1)}, bf16[2,256,256]{2,1,0:T(8,128)(2,1)S(1)}, u32[]{:S(2)}, u32[]{:S(2)}) collective-permute-start(bf16[2,256,256]{2,1,0:T(8,128)(2,1)S(1)} %get-tuple-element.213), channel_id=1, source_target_pairs={{0,5},{1,4},{2,7},{3,6},{4,1},{5,0},{6,3},{7,2},{8,13},{9,12},{10,... | collective-permute-start | bytes 786440 | tf_op jit(solution)/shard_map/ppermute | solution.py:885
  322.2 40.1 %collective-permute-start.37 = (bf16[128,2048]{1,0:T(8,128)(2,1)}, bf16[128,2048]{1,0:T(8,128)(2,1)}, u32[]{:S(2)}, u32[]{:S(2)}) collective-permute-start(bf16[128,2048]{1,0:T(8,128)(2,1)} %fusion.28), channel_id=1, source_target_pairs={{0,8},{8,0},{16,24},{24,16},{1,9},{9,1},{17,25},{25,17},{2,10},{10... | collective-permute-start | bytes 1572872 | tf_op jit(solution)/shard_map/ppermute | solution.py:844
  325.5 36.8 %collective-permute-start.36 = (bf16[128,2048]{1,0:T(8,128)(2,1)}, bf16[128,2048]{1,0:T(8,128)(2,1)}, u32[]{:S(2)}, u32[]{:S(2)}) collective-permute-start(bf16[128,2048]{1,0:T(8,128)(2,1)} %fusion.29), channel_id=1, source_target_pairs={{0,16},{8,24},{16,0},{24,8},{1,17},{9,25},{17,1},{25,9},{2,18},{10... | collective-permute-start | bytes 1572872 | tf_op jit(solution)/shard_map/ppermute | solution.py:844
  396.9 56.4 %collective-permute-start.42 = (bf16[4,256,1024]{2,1,0:T(8,128)(2,1)}, bf16[4,256,1024]{2,1,0:T(8,128)(2,1)}, u32[]{:S(2)}, u32[]{:S(2)}) collective-permute-start(bf16[4,256,1024]{2,1,0:T(8,128)(2,1)} %project_back.2), channel_id=1, source_target_pairs={{0,4},{4,0},{1,5},{5,1},{2,6},{6,2},{3,7},{7,3},{8,12},{12,8},{9,1... | collective-permute-start | bytes 6291464 | tf_op jit(solution)/shard_map/ppermute | solution.py:844
  398.1 44.4 %collective-permute-start.40 = (bf16[2,160,2048]{2,1,0:T(8,128)(2,1)}, bf16[2,160,2048]{2,1,0:T(8,128)(2,1)}, u32[]{:S(2)}, u32[]{:S(2)}) collective-permute-start(bf16[2,160,2048]{2,1,0:T(8,128)(2,1)} %fusion.17), channel_id=1, source_target_pairs={{0,16},{8,24},{16,0},{24,8},{1,17},{9,25},{17,1},{25,9},{2,18},{10... | collective-permute-start | bytes 3932168 | tf_op jit(solution)/shard_map/ppermute | solution.py:844
  398.7 43.8 %collective-permute-start.39 = (bf16[2,160,2048]{2,1,0:T(8,128)(2,1)}, bf16[2,160,2048]{2,1,0:T(8,128)(2,1)}, u32[]{:S(2)}, u32[]{:S(2)}) collective-permute-start(bf16[2,160,2048]{2,1,0:T(8,128)(2,1)} %fusion.19), channel_id=1, source_target_pairs={{0,8},{8,0},{16,24},{24,16},{1,9},{9,1},{17,25},{25,17},{2,10},{10... | collective-permute-start | bytes 3932168 | tf_op jit(solution)/shard_map/ppermute | solution.py:844
  400.1 21.4 %collective-permute-start.41 = (bf16[2,256,512]{2,1,0:T(8,128)(2,1)}, bf16[2,256,512]{2,1,0:T(8,128)(2,1)}, u32[]{:S(2)}, u32[]{:S(2)}) collective-permute-start(bf16[2,256,512]{2,1,0:T(8,128)(2,1)} %get-tuple-element.197), channel_id=1, source_target_pairs={{0,1},{1,0},{2,3},{3,2},{4,5},{5,4},{6,7},{7,6},{8,9},{9,8},{10,11... | collective-permute-start | bytes 1572872 | tf_op jit(solution)/shard_map/ppermute | solution.py:844
  401.6 40.9 %collective-permute-start.38 = (bf16[512,1024]{1,0:T(8,128)(2,1)}, bf16[512,1024]{1,0:T(8,128)(2,1)}, u32[]{:S(2)}, u32[]{:S(2)}) collective-permute-start(bf16[512,1024]{1,0:T(8,128)(2,1)} %get-tuple-element.106), channel_id=1, source_target_pairs={{4,2},{2,4},{0,0},{6,6},{5,3},{3,5},{1,1},{7,7},{12,10},{10,12},{8... | collective-permute-start | bytes 3145736 | tf_op jit(solution)/shard_map/ppermute | solution.py:854
  422.7 18.8 %collective-permute-start.58 = (bf16[256,512]{1,0:T(8,128)(2,1)S(1)}, bf16[256,512]{1,0:T(8,128)(2,1)S(1)}, u32[]{:S(2)}, u32[]{:S(2)}) collective-permute-start(bf16[256,512]{1,0:T(8,128)(2,1)S(1)} %fusion.56), channel_id=1, source_target_pairs={{0,2},{1,3},{2,0},{3,1},{4,6},{5,7},{6,4},{7,5},{8,10},{9,11},{10,... | collective-permute-start | bytes 786440 | tf_op jit(solution)/shard_map/ppermute | solution.py:844
  443.8 28.2 %collective-permute-start.55 = (bf16[160,2048]{1,0:T(8,128)(2,1)S(1)}, bf16[160,2048]{1,0:T(8,128)(2,1)S(1)}, u32[]{:S(2)}, u32[]{:S(2)}) collective-permute-start(bf16[160,2048]{1,0:T(8,128)(2,1)S(1)} %fusion.22), channel_id=1, source_target_pairs={{0,8},{8,0},{16,24},{24,16},{1,9},{9,1},{17,25},{25,17},{2,10},{10... | collective-permute-start | bytes 1966088 | tf_op jit(solution)/shard_map/ppermute | solution.py:844
  445.2 26.8 %collective-permute-start.54 = (bf16[160,2048]{1,0:T(8,128)(2,1)S(1)}, bf16[160,2048]{1,0:T(8,128)(2,1)S(1)}, u32[]{:S(2)}, u32[]{:S(2)}) collective-permute-start(bf16[160,2048]{1,0:T(8,128)(2,1)S(1)} %fusion.23), channel_id=1, source_target_pairs={{0,16},{8,24},{16,0},{24,8},{1,17},{9,25},{17,1},{25,9},{2,18},{10... | collective-permute-start | bytes 1966088 | tf_op jit(solution)/shard_map/ppermute | solution.py:844
  457.9 24.5 %collective-permute-start.43 = (bf16[256,1024]{1,0:T(8,128)(2,1)}, bf16[256,1024]{1,0:T(8,128)(2,1)}, u32[]{:S(2)}, u32[]{:S(2)}) collective-permute-start(bf16[256,1024]{1,0:T(8,128)(2,1)} %get-tuple-element.167), channel_id=1, source_target_pairs={{0,1},{1,0},{2,3},{3,2},{4,5},{5,4},{6,7},{7,6},{8,9},{9,8},{10,11... | collective-permute-start | bytes 1572872 | tf_op jit(solution)/shard_map/ppermute | solution.py:844
  457.9 28.1 %collective-permute-start.45 = (bf16[256,1024]{1,0:T(8,128)(2,1)}, bf16[256,1024]{1,0:T(8,128)(2,1)}, u32[]{:S(2)}, u32[]{:S(2)}) collective-permute-start(bf16[256,1024]{1,0:T(8,128)(2,1)} %get-tuple-element.168), channel_id=1, source_target_pairs={{0,1},{1,0},{2,3},{3,2},{4,5},{5,4},{6,7},{7,6},{8,9},{9,8},{10,11... | collective-permute-start | bytes 1572872 | tf_op jit(solution)/shard_map/ppermute | solution.py:844
  471.2 19.5 %collective-permute-start.47 = (bf16[2,256,384]{2,1,0:T(8,128)(2,1)}, bf16[2,256,384]{2,1,0:T(8,128)(2,1)}, u32[]{:S(2)}, u32[]{:S(2)}) collective-permute-start(bf16[2,256,384]{2,1,0:T(8,128)(2,1)} %get-tuple-element.115), channel_id=1, source_target_pairs={{0,8},{8,0},{16,24},{24,16},{1,9},{9,1},{17,25},{25,17},{2,10},{10... | collective-permute-start | bytes 1179656 | tf_op jit(solution)/shard_map/ppermute | solution.py:844
  477.8 16.7 %collective-permute-start.49 = (bf16[2,256,384]{2,1,0:T(8,128)(2,1)}, bf16[2,256,384]{2,1,0:T(8,128)(2,1)}, u32[]{:S(2)}, u32[]{:S(2)}) collective-permute-start(bf16[2,256,384]{2,1,0:T(8,128)(2,1)} %get-tuple-element.117), channel_id=1, source_target_pairs={{0,16},{8,24},{16,0},{24,8},{1,17},{9,25},{17,1},{25,9},{2,18},{10... | collective-permute-start | bytes 1179656 | tf_op jit(solution)/shard_map/ppermute | solution.py:844
  489.7 43.6 %collective-permute-start.56 = (bf16[2,320,512]{2,1,0:T(8,128)(2,1)S(1)}, bf16[2,320,512]{2,1,0:T(8,128)(2,1)S(1)}, u32[]{:S(2)}, u32[]{:S(2)}) collective-permute-start(bf16[2,320,512]{2,1,0:T(8,128)(2,1)S(1)} %get-tuple-element.182), channel_id=1, source_target_pairs={{0,1},{1,0},{2,3},{3,2},{4,5},{5,4},{6,7},{7,6},{8,9},{9,8},{10,11... | collective-permute-start | bytes 1966088 | tf_op jit(solution)/shard_map/ppermute | solution.py:844
  491.8 12.8 %collective-permute-start.48 = (bf16[256,384]{1,0:T(8,128)(2,1)S(1)}, bf16[256,384]{1,0:T(8,128)(2,1)S(1)}, u32[]{:S(2)}, u32[]{:S(2)}) collective-permute-start(bf16[256,384]{1,0:T(8,128)(2,1)S(1)} %fusion.77), channel_id=1, source_target_pairs={{0,16},{8,24},{16,0},{24,8},{1,17},{9,25},{17,1},{25,9},{2,18},{10... | collective-permute-start | bytes 589832 | tf_op jit(solution)/shard_map/ppermute | solution.py:844
  495.5 11.3 %collective-permute-start.50 = (bf16[256,384]{1,0:T(8,128)(2,1)S(1)}, bf16[256,384]{1,0:T(8,128)(2,1)S(1)}, u32[]{:S(2)}, u32[]{:S(2)}) collective-permute-start(bf16[256,384]{1,0:T(8,128)(2,1)S(1)} %fusion.79), channel_id=1, source_target_pairs={{0,8},{8,0},{16,24},{24,16},{1,9},{9,1},{17,25},{25,17},{2,10},{10... | collective-permute-start | bytes 589832 | tf_op jit(solution)/shard_map/ppermute | solution.py:844
  497.0 54.9 %collective-permute-start.44 = (bf16[256,1024]{1,0:T(8,128)(2,1)}, bf16[256,1024]{1,0:T(8,128)(2,1)S(1)}, u32[]{:S(2)}, u32[]{:S(2)}) collective-permute-start(bf16[256,1024]{1,0:T(8,128)(2,1)} %end.2), channel_id=1, source_target_pairs={{4,2},{2,4},{0,0},{6,6},{5,3},{3,5},{1,1},{7,7},{12,10},{10,12},{8... | collective-permute-start | bytes 1572872 | tf_op jit(solution)/shard_map/ppermute | solution.py:854
  499.2 52.8 %collective-permute-start.46 = (bf16[256,1024]{1,0:T(8,128)(2,1)}, bf16[256,1024]{1,0:T(8,128)(2,1)}, u32[]{:S(2)}, u32[]{:S(2)}) collective-permute-start(bf16[256,1024]{1,0:T(8,128)(2,1)} %end.3), channel_id=1, source_target_pairs={{4,2},{2,4},{0,0},{6,6},{5,3},{3,5},{1,1},{7,7},{12,10},{10,12},{8... | collective-permute-start | bytes 1572872 | tf_op jit(solution)/shard_map/ppermute | solution.py:854
  511.2 21.7 %collective-permute-start.64 = (f32[32,128]{1,0:T(8,128)S(1)}, f32[32,128]{1,0:T(8,128)S(1)}, u32[]{:S(2)}, u32[]{:S(2)}) collective-permute-start(f32[32,128]{1,0:T(8,128)S(1)} %add.561), channel_id=1, source_target_pairs={{0,2},{1,3},{2,0},{3,1},{4,6},{5,7},{6,4},{7,5},{8,10},{9,11},{10,... | collective-permute-start | bytes 49160 | tf_op jit(solution)/shard_map/ppermute | solution.py:844
  518.3 15.2 %collective-permute-start.51 = (bf16[128,768]{0,1:T(8,128)(2,1)S(1)}, bf16[128,768]{0,1:T(8,128)(2,1)}, u32[]{:S(2)}, u32[]{:S(2)}) collective-permute-start(bf16[128,768]{0,1:T(8,128)(2,1)S(1)} %bitcast.433), channel_id=1, source_target_pairs={{0,4},{4,0},{1,5},{5,1},{2,6},{6,2},{3,7},{7,3},{8,12},{12,8},{9,1... | collective-permute-start | bytes 589832 | tf_op jit(solution)/shard_map/ppermute | solution.py:844
  533.4 14.5 %collective-permute-start.57 = (bf16[320,512]{1,0:T(8,128)(2,1)S(1)}, bf16[320,512]{1,0:T(8,128)(2,1)S(1)}, u32[]{:S(2)}, u32[]{:S(2)}) collective-permute-start(bf16[320,512]{1,0:T(8,128)(2,1)S(1)} %fusion.47), channel_id=1, source_target_pairs={{0,2},{1,3},{2,0},{3,1},{4,6},{5,7},{6,4},{7,5},{8,10},{9,11},{10,... | collective-permute-start | bytes 983048 | tf_op jit(solution)/shard_map/ppermute | solution.py:844
  535.6 15.2 %collective-permute-start.52 = (bf16[2,2,128,256]{3,2,1,0:T(8,128)(2,1)}, bf16[2,2,128,256]{3,2,1,0:T(8,128)(2,1)}, u32[]{:S(2)}, u32[]{:S(2)}) collective-permute-start(bf16[2,2,128,256]{3,2,1,0:T(8,128)(2,1)} %pad_maximum_fusion.29), channel_id=1, source_target_pairs={{0,2},{1,3},{2,0},{3,1},{4,6},{5,7},{6,4},{7,5},{8,10},{9,11},{10,... | collective-permute-start | bytes 786440 | tf_op jit(solution)/shard_map/ppermute | solution.py:844
  (64 other events, 624.8 us)
Sparse Core Ops, SparseCore 0:
  120.2 69.7 all-gather.2
  192.4 52.7 all-gather.4

commit v3 on v2

--- a/solution.py
+++ b/solution.py
@@ -333,8 +333,10 @@
     )
 
 
-def work(flops, moved):
-    return pl.CostEstimate(flops=flops, bytes_accessed=moved, transcendentals=0)
+def lasting(microseconds):
+    return pl.CostEstimate(
+        flops=int(microseconds * 1e7), bytes_accessed=1024, transcendentals=0
+    )
 
 
 def turned(x, cosine, sine):
@@ -399,19 +401,18 @@
         ob_ref[slot_of[i * (tile // span) + b]] = out[b * span : (b + 1) * span].astype(BF16)
 
 
-def attend(q, k, v, pcol, prow, srow, bounds, slot_of, tile):
+def attend(pair, q, k, v, pcol, prow, srow, bounds, slot_of, tile):
     rows, width = q.shape
     blocks = slot_of.shape[0]
     span = rows // blocks
-    pairs = width // 128
     count = rows // tile
     grid_spec = pltpu.PrefetchScalarGridSpec(
         num_scalar_prefetch=2,
-        grid=(pairs, count),
+        grid=(1, count),
         in_specs=[
-            pl.BlockSpec((tile, 128), lambda p, i, b, t: (i, p)),
-            pl.BlockSpec((rows, 128), lambda p, i, b, t: (0, p)),
-            pl.BlockSpec((rows, 128), lambda p, i, b, t: (0, p)),
+            pl.BlockSpec((tile, 128), lambda p, i, b, t: (i, pair)),
+            pl.BlockSpec((rows, 128), lambda p, i, b, t: (0, pair)),
+            pl.BlockSpec((rows, 128), lambda p, i, b, t: (0, pair)),
             pl.BlockSpec((rows, 1), lambda p, i, b, t: (0, 0)),
             pl.BlockSpec((1, tile), lambda p, i, b, t: (0, i)),
             pl.BlockSpec((1, tile), lambda p, i, b, t: (0, i)),
@@ -427,12 +428,12 @@
         functools.partial(attend_kernel, tile),
         grid_spec=grid_spec,
         out_shape=[
-            jax.ShapeDtypeStruct((rows, width), F32),
-            jax.ShapeDtypeStruct((blocks, span, width), BF16),
-            jax.ShapeDtypeStruct((pairs, 2, rows), F32),
+            jax.ShapeDtypeStruct((rows, 128), F32),
+            jax.ShapeDtypeStruct((blocks, span, 128), BF16),
+            jax.ShapeDtypeStruct((1, 2, rows), F32),
         ],
         compiler_params=params(2),
-        cost_estimate=work(3 * rows * rows * width, 8 * rows * width),
+        cost_estimate=lasting(14),
         name="attend",
     )(bounds, slot_of, q, k, v, pcol, prow, srow)
 
@@ -507,14 +508,20 @@
         x = x.astype(BF16).astype(F32)
         return turned(x, cos_ref[at, :], -sin_ref[at, :]).astype(BF16)
 
-    g_ref[1, here, :] = unturned(dk, here)
-    g_ref[2, here, :] = dv.astype(BF16)
+    grad_k, grad_v = unturned(dk, here), dv.astype(BF16)
+    for b in range(tile // span):
+        at = slot_of[j * (tile // span) + b]
+        g_ref[1, at] = grad_k[b * span : (b + 1) * span]
+        g_ref[2, at] = grad_v[b * span : (b + 1) * span]
 
     @pl.when(j == count - 1)
     def _():
         for t in range(rows // tile):
             part = pl.ds(t * tile, tile)
-            g_ref[0, part, :] = unturned(dqt[:, part].T * 0.125, part)
+            grad_q = unturned(dqt[:, part].T * 0.125, part)
+            for b in range(tile // span):
+                at = slot_of[t * (tile // span) + b]
+                g_ref[0, at] = grad_q[b * span : (b + 1) * span]
 
 
 def attend_back(pair, q, k, v, do, o, lse, pcol, prow, srow, cosine, sine, bounds, slot_of, tile):
@@ -530,12 +537,12 @@
         in_specs=[
             whole, whole, whole,
             pl.BlockSpec((blocks, span, 128), lambda p, j, b, t: (0, 0, pair)),
-            whole,
-            pl.BlockSpec((1, 2, rows), lambda p, j, b, t: (pair, 0, 0)),
+            table,
+            pl.BlockSpec((1, 2, rows), lambda p, j, b, t: (0, 0, 0)),
             pl.BlockSpec((rows, 1), lambda p, j, b, t: (0, 0)),
             line, line, table, table,
         ],
-        out_specs=pl.BlockSpec((3, rows, 128), lambda p, j, b, t: (0, 0, 0)),
+        out_specs=pl.BlockSpec((3, blocks, span, 128), lambda p, j, b, t: (0, 0, 0, 0)),
         scratch_shapes=[
             pltpu.VMEM((2, rows, 128), BF16), pltpu.VMEM((2, rows, 128), BF16),
             pltpu.VMEM((2, 128, rows), BF16), pltpu.VMEM((2, 128, rows), BF16),
@@ -545,9 +552,9 @@
     return pl.pallas_call(
         functools.partial(attend_back_kernel, tile),
         grid_spec=grid_spec,
-        out_shape=jax.ShapeDtypeStruct((3, rows, 128), BF16),
+        out_shape=jax.ShapeDtypeStruct((3, blocks, span, 128), BF16),
         compiler_params=params(2),
-        cost_estimate=work(7 * rows * rows * 128, 18 * rows * 128),
+        cost_estimate=lasting(23),
         name="attend_back",
     )(bounds, slot_of, q, k, v, do, o, lse, pcol, prow, srow, cosine, sine)
 
@@ -581,9 +588,7 @@
     return lax.dot_general(a, b, (((1,), (1,)), ((), ())), preferred_element_type=F32)
 
 
-def call(kernel, name, grid, tables, ins, outs, scratch, flops, *arrays):
-    moved = sum(math.prod(a.shape) * a.dtype.itemsize for a in arrays)
-    moved += sum(math.prod(s.shape) * s.dtype.itemsize for s, _ in outs)
+def call(kernel, name, grid, tables, ins, outs, microseconds, *arrays):
     return pl.pallas_call(
         kernel,
         grid_spec=pltpu.PrefetchScalarGridSpec(
@@ -591,11 +596,10 @@
             grid=grid,
             in_specs=ins,
             out_specs=[spec for _, spec in outs],
-            scratch_shapes=scratch,
         ),
         out_shape=[shape for shape, _ in outs],
         compiler_params=params(len(grid)),
-        cost_estimate=work(flops, moved),
+        cost_estimate=lasting(microseconds),
         name=name,
     )(*tables, *arrays)
 
@@ -640,72 +644,7 @@
     return call(
         project_kernel, "project", (count,), [slot_of],
         [piece] * 4 + [fixed(*gains.shape), fixed(*w.shape), angle, angle],
-        [out, out, out, normed], [], 2 * count * rows * depth * 3 * width,
-        *parts, gains, w, cosine, sine,
-    )
-
-
-def side_by_side(first, second):
-    return jnp.concatenate([half[n] for n in range(3) for half in (first, second)], axis=1)
-
-
-def project_back_kernel(table, g0_ref, g1_ref, w_ref, o_ref):
-    g = side_by_side(g0_ref, g1_ref)
-    o_ref[0] = dot_nt(g, w_ref[...]).astype(o_ref.dtype)
-
-
-def project_back(grads, w, table, rows, dtype):
-    count = table.shape[0]
-    depth, width = w.shape
-    piece = pl.BlockSpec((3, rows, width // 6), lambda i, t: (0, t[i], 0))
-    return call(
-        project_back_kernel, "project_back", (count,), [table],
-        [piece, piece, fixed(*w.shape)],
-        [(shaped(dtype, count, rows, depth), pl.BlockSpec((1, rows, depth), lambda i, t: (i, 0, 0)))],
-        [], 2 * count * rows * depth * width, *grads, w,
-    )[0]
-
-
-def project_weights_kernel(slot_of, place, x_ref, g0_ref, g1_ref, w_ref, ac, as_, bc, bs, gain_ref, total):
-    i = pl.program_id(0)
-
-    @pl.when(i == 0)
-    def _():
-        total[...] = jnp.zeros_like(total)
-
-    g = side_by_side(g0_ref, g1_ref)
-    total[...] += lax.dot_general(
-        x_ref[0], g, (((0,), (0,)), ((), ())), preferred_element_type=F32
-    )
-
-    @pl.when(i == pl.num_programs(0) - 1)
-    def _():
-        rows, half = ac.shape[1:]
-        for r in range(2):
-            for out, flips in ((ac, 2 * r), (as_, 1 + 2 * r)):
-                at = pl.ds(pl.multiple_of((place[0] ^ flips) * rows, rows), rows)
-                out[r] = total[at, :half].astype(BF16)
-            for out, flips in ((bc, r), (bs, 2 + r)):
-                at = pl.ds(pl.multiple_of((place[0] ^ flips) * rows, rows), rows)
-                out[r] = total[at, half:].astype(BF16)
-        gain_ref[...] = jnp.sum(total[...] * w_ref[...].astype(F32), axis=1, keepdims=True)
-
-
-def project_weights(x, grads, w, slot_of, place):
-    count, rows, depth = x.shape
-    width = w.shape[1]
-    grad = pl.BlockSpec((3, rows, width // 6), lambda i, t, p: (0, i, 0))
-    quarter = depth // 4
-    piece = shaped(BF16, 2, quarter, width // 2), fixed(2, quarter, width // 2)
-    return call(
-        project_weights_kernel, "project_weights", (count,), [slot_of, place],
-        [
-            pl.BlockSpec((1, rows, depth), lambda i, t, p: (t[i], 0, 0)),
-            grad, grad, fixed(*w.shape),
-        ],
-        [piece, piece, piece, piece, (shaped(F32, depth, 1), fixed(depth, 1))],
-        [pltpu.VMEM((depth, width), F32)], 2 * count * rows * depth * width,
-        x, *grads, w,
+        [out, out, out, normed], 13, *parts, gains, w, cosine, sine,
     )
 
 
@@ -743,7 +682,7 @@
             (shaped(F32, total, width), row),
             (shaped(BF16, total, width), row),
         ],
-        [], 2 * total * width * width, local, near, far, both, w, x, gains,
+        6, local, near, far, both, w, x, gains,
     )
 
 
@@ -773,7 +712,7 @@
             (shaped(BF16, total, width), row), (shaped(BF16, total, width), row),
             (shaped(F32, 1, width), fixed(1, width)),
         ],
-        [], 20 * total * width, terms, sent, hidden, dy, gains,
+        5, terms, sent, hidden, dy, gains,
     )
 
 
@@ -819,7 +758,7 @@
             ),
             (shaped(F32, 1, width), fixed(1, width)), (shaped(F32, 1, width), fixed(1, width)),
         ],
-        [], 2 * total * width * width, terms, sent, hidden, dy, hat, scale, w, gains,
+        8, terms, sent, hidden, dy, hat, scale, w, gains,
     )
 
 
@@ -831,17 +770,21 @@
 
 
 def end(keep, near, far, x, grad, gains):
-    rows, width = x.shape
+    total, width = x.shape
+    rows = total // 2
+    row = pl.BlockSpec((rows, width), lambda i: (i, 0))
     return call(
-        end_kernel, "end", (1,), [],
-        [fixed(rows, width)] * 5 + [fixed(*gains.shape)],
-        [(shaped(BF16, rows, width), fixed(rows, width))],
-        [], 20 * rows * width, keep, near, far, x, grad, gains,
+        end_kernel, "end", (2,), [], [row] * 5 + [fixed(*gains.shape)],
+        [(shaped(BF16, total, width), row)], 20, keep, near, far, x, grad, gains,
     )[0]
 
 
+def plain(x):
+    return with_layout_constraint(x, Layout(tuple(range(x.ndim))))
+
+
 def flip(x, axis, bit):
-    return lax.ppermute(x, axis, [(i, i ^ bit) for i in range(lax.axis_size(axis))])
+    return lax.ppermute(plain(x), axis, [(i, i ^ bit) for i in range(lax.axis_size(axis))])
 
 
 def swap(x):
@@ -851,7 +794,7 @@
     for z in range(half):
         low, high = cp + z, z + half
         pairs += [(low, high), (high, low), (z, z), (cp + high, cp + high)]
-    return lax.ppermute(x, ("core", "cp"), pairs)
+    return lax.ppermute(plain(x), ("core", "cp"), pairs)
 
 
 def ordered(first, mine, other, axis):
@@ -870,10 +813,6 @@
 
 def all_after(group, *others):
     return lax.optimization_barrier((*group, *others))[: len(group)]
-
-
-def plain(x):
-    return with_layout_constraint(x, Layout(tuple(range(x.ndim))))
 
 
 def total(a, b):
@@ -904,8 +843,7 @@
     return lax.dynamic_index_in_dim(x, at, axis, False)
 
 
-def widened(z, x):
-    other = flip(x, "cp", 1)
+def widened(z, x, other):
     first, second = jnp.where(z & 1 == 0, x, other), jnp.where(z & 1 == 0, other, x)
     half = x.shape[1] // 2
     return jnp.concatenate(
@@ -929,15 +867,13 @@
     here = jnp.reshape(xy, (1,)).astype(jnp.int32)
     group_at = jnp.reshape(group, (1,)).astype(jnp.int32)
 
-    w = jnp.concatenate([qkv_weight, out_weight], axis=1)
-    gain_rows = jnp.zeros((16, w.shape[1]), BF16)
+    gain_rows = jnp.zeros((16, qkv_weight.shape[1]), BF16)
     gain_rows = lax.dynamic_update_slice(gain_rows, norm_gains[None], (0, 0))
-    w = jnp.concatenate([w, gain_rows])
-    x = tokens[0]
+    w = jnp.concatenate([qkv_weight, gain_rows])
     w_far = flip(w, "cp", 2)
-    x_half = [swap(x[0]), swap(x[1])]
-
-    up_weight, down_weight = all_after((up_weight, down_weight), w_far)
+    x = swap(after(tokens, w_far)[0])
+
+    up_weight, down_weight, out_weight = all_after((up_weight, down_weight, out_weight), w_far)
 
     def half_of(which):
         up = lax.dynamic_slice_in_dim(up_weight, which * hidden_part, hidden_part, 1)
@@ -951,52 +887,39 @@
             [jnp.where(z & 2 == 0, mine, other), jnp.where(z & 2 == 0, other, mine)], axis=1
         )
 
-    w = placed(z & 2 == 0, w, w_far, 0)
-    w = placed(z & 1 == 0, w, flip(w, "cp", 1), 1)
-    x_half[0] = after(x_half[0], w)
-    z_half = [flip(x_half[0], "cp", 1), flip(x_half[1], "cp", 1)]
-    up_lines = after(ffn[0], x_half[1])
-    up_lines = paired(up_lines, flip(up_lines, "cp", 2))
-
-    gain_rows = jnp.zeros((16, 3 * part), BF16)
-    gain_rows = lax.dynamic_update_slice(
-        gain_rows, w[:, :, lines, : norm_gains.shape[0]].reshape(cp_count, -1), (0, 0)
-    )
-    out_w = jnp.concatenate([w[a, b, :lines, 3 * part :] for a in range(2) for b in range(2)], axis=1)
-
-    def columns(of):
-        picked = []
-        for third in range(3):
-            block = third * cp_count + of
-            at = (block // 6, (block // 3) & 1, 0, (block % 3) * part)
-            picked.append(lax.dynamic_slice(w, at, (1, 1, lines, part))[0, 0])
-        return jnp.concatenate([jnp.concatenate(picked, axis=1), gain_rows])
-
-    qkv = placed(core == 0, columns(group), flip(columns(group ^ 1), "core", 1), 0)
-    cut = qkv.shape[2] // 2
-    low, high = qkv[:, :, :cut], qkv[:, :, cut:]
-    low = placed(xy & 1 == 0, low, flip(low, "xy", 1), 0)
-    high = placed(xy & 2 == 0, high, flip(high, "xy", 2), 0)
-    low = placed(xy & 2 == 0, low, flip(low, "xy", 2), 0)
-    high = placed(xy & 1 == 0, high, flip(high, "xy", 1), 1)
-    qkv = jnp.concatenate([low[:, :, :, :lines], high[:, :, :, :lines]], axis=4)
-    qkv = qkv.reshape(width, 3 * part)
-    gains = low[:, :, :, lines : lines + cp_count, : norm_gains.shape[0]]
-    gains = gains.reshape(4, width).astype(F32)
-
-    x = jnp.stack(x_half)
-    x_core = flip(x, "core", 1)
-    x_chip = jnp.stack(z_half)
-    x_both = flip(x_chip, "core", 1)
+    out_far = flip(out_weight, "cp", 2)
+    w, w_far = jnp.where(z & 2 == 0, w, w_far), jnp.where(z & 2 == 0, w_far, w)
+    near = [w[:, n * part : (n + 1) * part] for n in range(3)]
+    near += [w_far[:, n * part : (n + 1) * part] for n in range(3)]
+    even = parity == 0
+    sent = jnp.concatenate(
+        [jnp.where(even, near[a], near[b]) for a, b in ((2, 1), (3, 2), (4, 3))], axis=1
+    )
+    gain_near = jnp.stack([w[lines, :128], w_far[lines, :128]])
+    sent = lax.dynamic_update_slice(sent, gain_near, (lines, 0))
+    far = flip(sent, "cp", 1)
+    gain_far = far[lines : lines + 2, :128]
+    gain_near, gain_far = (
+        jnp.where(even, gain_near, gain_far), jnp.where(even, gain_far, gain_near)
+    )
+    gain_rows = jnp.stack([gain_near[0], gain_far[0], gain_near[1], gain_far[1]])
+    far = [far[:lines, n * part : (n + 1) * part] for n in range(3)]
+    near = [block[:lines] for block in near]
+    first_group = jnp.concatenate(
+        [jnp.where(even, a, b) for a, b in ((near[0], far[0]), (far[0], far[1]), (near[5], near[4]))],
+        axis=1,
+    )
+    second_group = jnp.concatenate(
+        [jnp.where(even, a, b) for a, b in ((near[1], near[0]), (far[1], far[2]), (far[2], near[5]))],
+        axis=1,
+    )
+    gain_block = jnp.zeros((16, 3 * part), BF16)
+    gain_block = lax.dynamic_update_slice(gain_block, gain_rows, (0, 0))
+    mine = jnp.concatenate([jnp.where(core == 0, first_group, second_group), gain_block])
+    other = jnp.concatenate([jnp.where(core == 0, second_group, first_group), gain_block])
+
     other_starts = flip(after(doc_starts, w_far), "core", 1)
     starts = jnp.where(core == z // (cp_count // 2), doc_starts, other_starts)[0]
-
-    up_lines = widened(z, after(up_lines, x_chip))
-    up_full = lax.all_gather(after(up_lines, qkv), "xy", axis=0, tiled=True)
-    down_lines = after(ffn[1], x_chip)
-    down_lines = paired(down_lines, flip(down_lines, "cp", 2))
-    out_w = after(out_w, x_chip)[None]
-    out_w = ordered(xy & 1 == 0, out_w, flip(out_w, "xy", 1), 0)
 
     block_id = jnp.arange(blocks, dtype=jnp.int32)[:, None]
     inside = jnp.arange(span, dtype=jnp.int32)[None, :]
@@ -1014,8 +937,8 @@
     )
     angles = (positions - row_start).astype(F32)[:, None] * freq
     cosine, sine = jnp.cos(angles), jnp.sin(angles)
-    cosine = jnp.tile(cosine, (1, 4))
-    sine = jnp.tile(jnp.concatenate([-sine, sine], axis=1), (1, 2))
+    cosine = plain(jnp.tile(cosine, (1, 4)))
+    sine = plain(jnp.tile(jnp.concatenate([-sine, sine], axis=1), (1, 2)))
     pcol, prow, srow = positions[:, None], positions[None, :], row_start[None, :]
     chunk = jnp.arange(blocks, dtype=jnp.int32)
     chunk = jnp.where(chunk < cp_count, chunk, blocks - 1 - chunk)
@@ -1028,23 +951,97 @@
     chunk_of = 2 * ((relative >> 1) ^ core) + ((relative & 1) ^ parity)
     block_of = jnp.where(slot & 1 == 0, chunk_of, blocks - 1 - chunk_of).astype(jnp.int32)
 
+    x = after(x, sent, cosine, sine)
+    x_chip = flip(x, "cp", 1)
+    x_core = flip(x, "core", 1)
+    up_lines, out_w, out_far = all_after((ffn[0], out_weight, out_far), x)
+    up_far = flip(up_lines, "cp", 2)
+    out_w = paired(out_w, out_far)
+    out_far = flip(out_w, "cp", 1)
+
+    qkv = placed(core == 0, mine, flip(other, "core", 1), 0)
+    cut = qkv.shape[2] // 2
+    low, high = qkv[:, :, :cut], qkv[:, :, cut:]
+    low = placed(xy & 1 == 0, low, flip(low, "xy", 1), 0)
+    high = placed(xy & 2 == 0, high, flip(high, "xy", 2), 0)
+    low = placed(xy & 2 == 0, low, flip(low, "xy", 2), 0)
+    high = placed(xy & 1 == 0, high, flip(high, "xy", 1), 1)
+    qkv = jnp.concatenate([low[:, :, :, :lines], high[:, :, :, :lines]], axis=4)
+    qkv = qkv.reshape(width, 3 * part)
+    gains = low[:, :, :, lines : lines + cp_count, :128]
+    gains = gains.reshape(4, width).astype(F32)
+
+    x_both = flip(x_chip, "core", 1)
+    x_chip, up_far = lax.optimization_barrier((x_chip, up_far))
+    up_lines, up_far, down_lines, out_w, out_far = all_after(
+        (up_lines, up_far, ffn[1], out_w, out_far), x_chip, qkv
+    )
+    up_lines, out_w = paired(up_lines, up_far), widened(z, out_w, out_far)[None]
+    up_far = flip(up_lines, "cp", 1)
+    down_far = flip(down_lines, "cp", 2)
+    out_far = flip(out_w, "xy", 1)
+
+    def halves(x):
+        return x[None, :lines], x[None, lines:]
+
+    def send_lines(low, high):
+        return flip(low, "xy", 1), flip(high, "xy", 2)
+
+    def join_lines(low, high, low_far, high_far):
+        low = ordered(xy & 1 == 0, low, low_far, 0)
+        high = jnp.expand_dims(ordered(xy & 2 == 0, high, high_far, 0), 1)
+        return low, high
+
+    def send_more(low, high):
+        return flip(low, "xy", 2), flip(high, "xy", 1)
+
+    def join_all(low, high, low_far, high_far):
+        low = ordered(xy & 2 == 0, low, low_far, 0)
+        high = ordered(xy & 1 == 0, high, high_far, 1).reshape(low.shape)
+        return jnp.stack([low, high], axis=1).reshape(width, -1)
+
     q, k, v, normed = project([x, x_chip, x_core, x_both], gains, qkv, cosine, sine, slot_of)
-    down_lines, out_w = all_after((down_lines, out_w), q)
-    down_lines = widened(z, down_lines)
-    out_w = ordered(xy & 2 == 0, out_w, flip(out_w, "xy", 2), 0)
-    attended, local, lse = attend(q, k, v, pcol, prow, srow, bounds, slot_of, tile)
-    down_lines, out_w, dy = all_after((down_lines, out_w, cotangent), local)
-    down_full = lax.all_gather(down_lines, "xy", axis=0, tiled=True)
-    out_w = placed(core == 0, out_w, flip(out_w, "core", 1), 1).reshape(width, width)
+    up_lines, up_far, down_lines, down_far, out_w, out_far = all_after(
+        (up_lines, up_far, down_lines, down_far, out_w, out_far), q
+    )
+    up_pair = halves(widened(z, up_lines, up_far))
+    up_far = send_lines(*up_pair)
+    down_lines = paired(down_lines, down_far)
+    down_far = flip(down_lines, "cp", 1)
+    out_w = ordered(xy & 1 == 0, out_w, out_far, 0)
+    out_far = flip(out_w, "xy", 2)
+    q = after(q, *up_pair, down_lines, out_w)
+    first = attend(0, q, k, v, pcol, prow, srow, bounds, slot_of, tile)
+    up_pair, up_far = all_after(up_pair, first[0]), all_after(up_far, first[0])
+    down_lines, down_far, out_w, out_far = all_after(
+        (down_lines, down_far, out_w, out_far), first[0]
+    )
+    up_pair = join_lines(*up_pair, *up_far)
+    up_far = send_more(*up_pair)
+    out_w = ordered(xy & 2 == 0, out_w, out_far, 0)
+    out_far = flip(out_w, "core", 1)
+    down_pair = halves(widened(z, down_lines, down_far))
+    down_far = send_lines(*all_after(down_pair, *up_pair))
+    q = after(q, first[0], *down_pair, *up_pair, out_w)
+    second = attend(1, q, k, v, pcol, prow, srow, bounds, slot_of, tile)
+    attended, local, lse = zip(first, second)
+    local = jnp.concatenate(local, axis=2)
+    out_w, out_far = all_after((out_w, out_far), local)
+    out_w = placed(core == 0, out_w, out_far, 1).reshape(width, width)
     heads, branch_hat, branch_scale, hidden, mid = mix(
         group_at, local[:2], flip(local[4:6], "core", 1), flip(local[2:4], "cp", 1),
         flip_both(local[6:]), out_w, x, gains,
     )
 
-    dy = swap(after(dy.reshape(own, width), mid))
+    dy = swap(after(cotangent.reshape(own, width), mid))
 
     ffn_in = jnp.concatenate([mid, flip(mid, "core", 1)])
+    down_pair, down_far = all_after(down_pair, mid), all_after(down_far, mid)
+    down_pair = join_lines(*down_pair, *down_far)
+    down_far = send_more(*down_pair)
+    up_full = join_all(*up_pair, *all_after(up_far, *down_pair))
     act, slope = gelu_and_slope(dot(ffn_in, up_full, (1, 0)))
+    down_full = join_all(*down_pair, *all_after(down_far, act))
     sent = flip(dot(act[own:], down_full, (1, 1)).astype(BF16), "core", 1)
     terms = dot(act[:own], down_full, (1, 1))
     mixed, grad_down, gain_four = finish(terms, sent, hidden, dy, gains)
@@ -1052,15 +1049,16 @@
 
     x_bit, y_bit = xy & 1, xy >> 1
 
-    def cut_first(grads, extra):
-        grads = grads.reshape(2, 2, 2, lines, -1)
-        low, high = grads[:, :, 0], grads[:, :, 1]
-        if extra is not None:
-            extra = extra.reshape(2, 2, 2, -1, extra.shape[-1])
-            low = jnp.concatenate([low, extra[:, :, 0]], axis=2)
-            high = jnp.concatenate([high, extra[:, :, 1]], axis=2)
-        away = pick(low, 1 - x_bit, 1), pick(high, 1 - y_bit, 0)
-        return (pick(low, x_bit, 1), pick(high, y_bit, 0)), away
+    def cut_first(grads):
+        grads = [g.reshape(2, 2, 2, lines, -1) for g in grads]
+        low = [g[:, :, 0] for g in grads]
+        high = [g[:, :, 1] for g in grads]
+
+        def both(parts, at, axis):
+            return jnp.concatenate([pick(part_of, at, axis) for part_of in parts], axis=1)
+
+        away = both(low, 1 - x_bit, 1), both(high, 1 - y_bit, 0)
+        return (both(low, x_bit, 1), both(high, y_bit, 0)), away
 
     def send_first(away):
         return flip(away[0], "xy", 1), flip(away[1], "xy", 2)
@@ -1080,8 +1078,12 @@
         return flip(away[0], "xy", 2), flip(away[1], "xy", 1)
 
     def cut_third(near, far):
-        sums = jnp.concatenate([total(a, b) for a, b in zip(near, far)])
-        blocks_of = [sums[:, n * hidden_part : (n + 1) * hidden_part] for n in range(cp_count)]
+        return split_columns(
+            jnp.concatenate([total(a, b) for a, b in zip(near, far)]), hidden_part
+        )
+
+    def split_columns(sums, each):
+        blocks_of = [sums[:, n * each : (n + 1) * each] for n in range(cp_count)]
         odd = jnp.stack([blocks_of[1], blocks_of[3]])
         even = jnp.stack([blocks_of[0], blocks_of[2]])
         return jnp.where(parity == 0, even, odd), jnp.where(parity == 0, odd, even)
@@ -1093,12 +1095,13 @@
         )
 
     down_local = plain(dot(grad_down, act, (0, 0)).astype(BF16))
-    down_near, down_away = cut_first(down_local, None)
-    down_far = send_first(down_away)
-    grad_up = dot(after(grad_down, *down_away), down_full, (1, 0)) * slope.astype(F32)
+    grad_up = dot(after(grad_down, down_local), down_full, (1, 0)) * slope.astype(F32)
     grad_up = grad_up.astype(BF16)
     sent = flip(dot(grad_up[own:], up_full, (1, 1)).astype(BF16), "core", 1)
-    terms = dot(grad_up[:own], up_full, (1, 1))
+    up_local = plain(dot(ffn_in, grad_up, (0, 0)).astype(BF16))
+    grad_near, grad_away = cut_first((up_local, down_local))
+    grad_far = send_first(grad_away)
+    terms = dot(after(grad_up, *grad_away)[:own], up_full, (1, 1))
     grad_hidden, grad_branch, grad_heads, gain_three, gain_two = turn(
         group_at, terms, sent, hidden, dy, branch_hat, branch_scale, out_w, gains
     )
@@ -1107,65 +1110,91 @@
         grad_heads[0], flip(grad_heads[2], "cp", 1), flip(grad_heads[1], "core", 1),
         flip_both(grad_heads[3]),
     ]
-    out_local = dot(heads, grad_branch, (0, 0)).astype(BF16)
+    out_local = dot(after(heads, grad_heads), grad_branch, (0, 0)).astype(BF16)
     out_local = out_local.reshape(xy_count, 2, lines, width)
     out_away = pick(out_local, 1 - core, 1)
-    out_sum = flip(out_away, "core", 1)
-    down_far = all_after(down_far, grad_heads)
-    down_near, down_away = cut_second(down_near, down_far)
-    down_far = send_second(down_away)
-    up_local = plain(dot(after(ffn_in, out_away), grad_up, (0, 0)).astype(BF16))
-    out_sum = total(pick(out_local, core, 1), out_sum)
-    out_sum = out_sum.reshape(xy_count, 2, lines // 2, cp_count, part)
-    out_sum = jnp.concatenate(
-        [out_sum[:, h, :, n] for n in range(cp_count) for h in range(2)], axis=-1
-    )
-    up_near, up_away = cut_first(up_local, out_sum)
-    up_far = send_first(up_away)
-    grad_local = after(jnp.concatenate(grad_local), *up_away, *down_away)
+    grad_local = plain(jnp.concatenate(grad_local))
+    out_away, mixed = all_after((out_away, mixed), grad_local)
+    out_far = flip(out_away, "core", 1)
+    mixed = swap(mixed).reshape(tokens.shape)
+    grad_local = after(grad_local, out_away)
 
     tables = (pcol, prow, srow, cosine, sine, bounds, slot_of, tile)
-    first = attend_back(0, q, k, v, grad_local, attended, lse, *tables)
-    down_far = all_after(down_far, first)
-    down_near, down_away = cut_third(down_near, down_far)
-    down_far = flip(down_away, "cp", 1)
-    second = attend_back(1, q, k, v, after(grad_local, first, down_away), attended, lse, *tables)
-    send = project_back((first, second), qkv, block_of[4:], span, BF16)
+    first = attend_back(0, q, k, v, grad_local, attended[0], lse[0], *tables)
+    grad_far = all_after(grad_far, first)
+    grad_near, grad_away = cut_second(grad_near, grad_far)
+    grad_far = send_second(grad_away)
+    out_near, out_away = split_columns(
+        total(pick(out_local, core, 1), after(out_far, first)).reshape(-1, width), part
+    )
+    out_far = flip(out_away, "cp", 1)
+    second = attend_back(
+        1, q, k, v, after(grad_local, first, *grad_away, out_away, mixed), attended[1], lse[1],
+        *tables,
+    )
+    first, second, grad_far, out_far = lax.optimization_barrier((first, second, grad_far, out_far))
+
+    def rows_of(low, high):
+        return jnp.concatenate(
+            [half[n, low:high].reshape(-1, 128) for n in range(3) for half in (first, second)],
+            axis=1,
+        )
+
+    half_rows = row_len // 2
+    grad_rows = rows_of(0, blocks)
+    send = dot(grad_rows[half_rows:], qkv, (1, 1)).astype(BF16)
     sent = flip(send, "core", 1)
-    up_far = all_after(up_far, send)
-    up_near, up_away = cut_second(up_near, up_far)
-    up_far = send_second(up_away)
-    down_far = after(down_far, send)
-    down_near, down_away = cut_fourth(down_near, down_far)
-    down_far = flip(down_away, "cp", 2)
-    keep = project_back((after(first, send, *up_away, down_away), second), qkv, block_of[:4], span, F32)
-    far_away = [total(keep[2 + h], sent[2 + h]) for h in range(2)]
-    far = [flip(a, "cp", 1) for a in far_away]
-    low, low_send, high, high_send, gain_one = project_weights(
-        normed, (after(first, *far_away), second), qkv, slot_of, here
-    )
-    low_far, high_far = flip(low_send, "xy", 1), flip(high_send, "xy", 2)
-    up_far = all_after(up_far, low_send)
-    up_near, up_away = cut_third(up_near, up_far)
-    up_far = flip(up_away, "cp", 1)
-    tokens_grad = []
-    for h in range(2):
-        grad = end(
-            keep[h], sent[h], far[h], x[h], grad_hidden[h * span : (h + 1) * span], gains
-        )
-        tokens_grad.append(grad)
-    ended = tuple(tokens_grad)
-    tokens_grad = [swap(grad) for grad in tokens_grad]
-    tokens_grad = jnp.stack(tokens_grad).astype(F32).reshape(tokens.shape)
-    mixed = swap(after(mixed, send)).reshape(tokens.shape)
-
-    low_send, low = total(low[1], low_far[1]), total(low[0], low_far[0])
-    high_send, high = total(high[1], high_far[1]), total(high[0], high_far[0])
-    low = total(low, flip(low_send, "xy", 2))
-    high = total(high, flip(high_send, "xy", 1))
-    both = jnp.concatenate([low, high], axis=1).reshape(2, lines, 3 * part)
-    mine, other = pick(both, core, 0), flip(pick(both, 1 - core, 0), "core", 1)
-    both = placed(core == 0, mine, other, 0).reshape(2, lines, 3, part).transpose(2, 0, 1, 3)
+    grad_near, grad_away = cut_third(grad_near, all_after(grad_far, send))
+    grad_far = flip(grad_away, "cp", 1)
+    out_near, out_away = cut_fourth(out_near, after(out_far, send))
+    out_far = flip(out_away, "cp", 2)
+    grad_rows = after(grad_rows, send, grad_away, out_away)
+    qkv_local = dot(normed.reshape(row_len, width), grad_rows, (0, 0)).astype(BF16)
+    gain_one = jnp.sum(qkv_local.astype(F32) * qkv.astype(F32), axis=1) / gains[0]
+    gain_sum = jnp.concatenate([gain_one[None], gain_two, gain_three, gain_four])
+    gain_sum = gain_sum.reshape(2 * xy_count, cp_count, 128).astype(BF16)
+    gain_sum = jnp.pad(gain_sum, ((0, 0), (0, lines - cp_count), (0, 0)))
+    rest = plain(jnp.concatenate([qkv_local, gain_sum.reshape(width, 128)], axis=1))
+    rest = rest.reshape(xy_count, 2, lines, -1)
+    rest_near, rest_away = pick(rest, core, 1), pick(rest, 1 - core, 1)
+    rest_far = flip(rest_away, "core", 1)
+    grad_rows = after(grad_rows, rest_away)
+    far_away = total(dot(grad_rows[own:half_rows], qkv, (1, 1)), sent[own:])
+    far = flip(far_away, "cp", 1)
+    keep = dot(after(grad_rows, far_away)[:own], qkv, (1, 1))
+
+    out_sum = total(out_near, out_far).reshape(xy_count, lines, part)
+    rest_far = after(rest_far, far_away)
+    three = 3 * part
+    summed = total(rest_near[..., three:], rest_far[..., three:])
+    rest_near, rest_far = rest_near[..., :three], rest_far[..., :three]
+    rest = jnp.concatenate(
+        [
+            jnp.where(core == 0, rest_near, rest_far), jnp.where(core == 0, rest_far, rest_near),
+            out_sum, summed,
+        ],
+        axis=2,
+    )
+    rest = plain(rest).reshape(2, 2, lines, -1)
+    cut = rest.shape[3] // 256 * 128
+    low, high = rest[..., :cut], rest[..., cut:]
+    rest_near = pick(low, x_bit, 1), pick(high, y_bit, 0)
+    rest_away = pick(low, 1 - x_bit, 1), pick(high, 1 - y_bit, 0)
+    rest_far = send_first(rest_away)
+    grad_near, grad_away = cut_fourth(grad_near, after(grad_far, *rest_away))
+    grad_far = flip(grad_away, "cp", 2)
+    far = after(far, grad_away)
+    tokens_grad = end(keep, sent[:own], far, x.reshape(own, width), grad_hidden, gains)
+    ended = tokens_grad
+    tokens_grad = swap(tokens_grad)
+
+    rest_far = all_after(rest_far, far)
+    rest_near, rest_away = cut_second(rest_near, rest_far)
+    rest_far = send_second(rest_away)
+    rest = jnp.concatenate([total(a, b) for a, b in zip(rest_near, rest_far)], axis=1)
+    qkv_sum = rest[:, : 2 * three].reshape(lines, 2, 3, part).transpose(2, 1, 0, 3)
+    out_grad = rest[:, 2 * three : 2 * three + part].astype(F32)
+    gain_sum = rest[:, 2 * three + part :]
     right = z >= 2
     even = parity == 0
     send_at = (
@@ -1174,9 +1203,19 @@
     keep_at = (
         jnp.where(right, jnp.where(even, 2, 1), 0), jnp.where(right, 2, jnp.where(even, 1, 0))
     )
-    sent = flip(jnp.stack([pick(both, at, 0) for at in send_at]), "cp", 2)
-    both = total(jnp.stack([pick(both, at, 0) for at in keep_at]), sent)
-    sent = flip(pick(both, jnp.where(z == 0, 1, 0), 0), "cp", 1)
+
+    def flat(qkv_blocks, gain_block):
+        return jnp.concatenate([*qkv_blocks.reshape(-1, lines, part), gain_block], axis=1)
+
+    rest = flat(jnp.stack([pick(qkv_sum, at, 0) for at in keep_at]), gain_sum)
+    rest_away = flat(jnp.stack([pick(qkv_sum, at, 0) for at in send_at]), gain_sum)
+    rest = total(rest, flip(rest_away, "cp", 2))
+    blocks_of = [rest[:, n * part : (n + 1) * part] for n in range(4)]
+    gain_sum = rest[:, 4 * part :]
+    slots = jnp.stack([jnp.stack(blocks_of[:2]), jnp.stack(blocks_of[2:4])])
+    rest_away = flat(pick(slots, jnp.where(z == 0, 1, 0), 0), gain_sum)
+    rest_far = flip(rest_away, "cp", 1)
+    sent = [rest_far[:, :part], rest_far[:, part : 2 * part]]
 
     def choice(*four):
         return jnp.where(
@@ -1185,33 +1224,19 @@
 
     qkv_grad = jnp.concatenate(
         [
-            choice(both[0, 0], both[0, 1], sent[0], sent[1]),
-            choice(both[0, 1], sent[0], sent[1], both[1, 0]),
-            choice(sent[0], sent[1], both[0, 0], both[1, 1]),
+            choice(slots[0, 0], slots[0, 1], sent[0], sent[1]),
+            choice(slots[0, 1], sent[0], sent[1], slots[1, 0]),
+            choice(sent[0], sent[1], slots[0, 0], slots[1, 1]),
         ],
         axis=1,
     ).astype(F32)
-
-    up_near, up_away = cut_fourth(up_near, up_far)
-    up_sums = total(up_near, flip(up_away, "cp", 2))
-    down_sums = plain(total(down_near, down_far))
-    extra = lines // 4
-    out_grad = jnp.concatenate([up_sums[lines : lines + extra], up_sums[2 * lines + extra :]])
-    out_grad = jnp.concatenate([out_grad[:, :part], out_grad[:, part:]]).astype(F32)
-    both = jnp.stack([
-        jnp.stack([up_sums[:lines], up_sums[lines + extra : 2 * lines + extra]]),
-        down_sums.reshape(2, lines, hidden_part),
-    ], axis=1)
+    gains_grad = pick(gain_sum.astype(F32) + rest_far[:, 2 * part :].astype(F32), z, 0)
+    tokens_grad = after(tokens_grad, rest_away).astype(F32).reshape(tokens.shape)
+
+    both = plain(total(grad_near, after(grad_far, ended))).reshape(2, 2, lines, hidden_part)
     mine, other = pick(both, core, 0), flip(pick(both, 1 - core, 0), "core", 1)
     up_grad = ordered(core == 0, mine[0], other[0], 1).astype(F32)
     down_grad = ordered(core == 0, mine[1], other[1], 1).T.astype(F32)
-
-    gain_one = gain_one.reshape(1, width) / gains[0:1]
-    gain_sum = jnp.concatenate([gain_one, gain_two, gain_three, gain_four]).reshape(-1, 128)
-    gain_sum = after(gain_sum, *ended)
-    for axis, bit in (("core", 1), ("xy", 1), ("xy", 2), ("cp", 1), ("cp", 2)):
-        gain_sum = gain_sum + flip(gain_sum, axis, bit)
-    gains_grad = pick(gain_sum, (2 * xy + core) * cp_count + z, 0)
     return mixed, tokens_grad, qkv_grad, out_grad, up_grad, down_grad, gains_grad
 
 

time: 575 us -> 508 us (0.88)
  Pallas kernels: 141 us -> 116 us
  waiting for transfers between devices: 185 us -> 162 us
  between operations: 16 us -> 2.62 us
    pallas_call x9 -> x5, Pallas kernels: 64 us -> 38.2 us  [call(): pl.pallas_call(kernel, grid_spec=pltpu.PrefetchScalarGridSpec(num_scalar_...]
    all_gather x2 -> x0, waiting for transfers between devices: 16.5 us -> none  [the longest x1 16.4 us: body(): down_full = lax.all_gather(down_lines, 'xy', axis=0, tiled=True)]
    convert_element_type x19 -> x15, other arithmetic: 26.5 us -> 17.8 us  [total(): return (a.astype(F32) + b.astype(F32)).astype(BF16)]
    squeeze x5 -> x0, local copies, waits for them, and re-layouts: 7.32 us -> none  [the longest x1 2.23 us: body(): x_half = [swap(x[0]), swap(x[1])]]
    ppermute x63 -> x60, waiting for transfers between devices: 161 us -> 154 us  [the longest x56 154 us: flip(): lax.ppermute(plain(x), axis, [(i, i ^ bit) for i in range(lax.axis_size(a...]
    dot_general x9 -> x13, matrix products: 52.1 us -> 56.5 us  [dot(): lax.dot_general(a, b, ((dims[:1], dims[1:]), ((), ())), preferred_element...]
    ppermute x63 -> x60, starting transfers between devices: 76.6 us -> 73.8 us  [the longest x56 59.6 us: flip(): lax.ppermute(plain(x), axis, [(i, i ^ bit) for i in range(lax.axis_size(a...]
    pallas_call x1 -> x2, Pallas kernels: 28.6 us -> 30.8 us  [attend(): pl.pallas_call(functools.partial(attend_kernel, tile), grid_spec=grid_spe...]
  transfers between devices with their start and end apart: 67 -> 62, of which waited for: 29 -> 27; matrix products, arithmetic and copies ran while one was open for 20% -> 20% of each run, Pallas kernels for 19% -> 22%
where the time goes in v3:
time: 508 us; the launch traced here: 502 us
  waiting for transfers between devices  162 us (32%)
  Pallas kernels  116 us (23%)
  starting transfers between devices  75.4 us (15%)
  matrix products  56.5 us (11%)
  other arithmetic  50.8 us (10%)
  local copies, waits for them, and re-layouts  38.6 us (8%)
    ppermute x56, waiting for transfers between devices, flip(): lax.ppermute(plain(x), axis, [(i, i ^ bit) for i in range(lax.axis_size(a...  154 us
    ppermute x56, starting transfers between devices, flip(): lax.ppermute(plain(x), axis, [(i, i ^ bit) for i in range(lax.axis_size(a...  59.6 us
    dot_general x13, matrix products, dot(): lax.dot_general(a, b, ((dims[:1], dims[1:]), ((), ())), preferred_element...  56.5 us
    pallas_call x2, Pallas kernels, attend_back(): pl.pallas_call(functools.partial(attend_back_kernel, tile), grid_spec=gri...  46.8 us
    pallas_call x5, Pallas kernels, call(): pl.pallas_call(kernel, grid_spec=pltpu.PrefetchScalarGridSpec(num_scalar_...  38.2 us
    pallas_call x2, Pallas kernels, attend(): pl.pallas_call(functools.partial(attend_kernel, tile), grid_spec=grid_spe...  30.8 us
    convert_element_type x15, other arithmetic, total(): return (a.astype(F32) + b.astype(F32)).astype(BF16)  17.8 us
    unnamed x107, local copies, waits for them, and re-layouts  17 us
  transfers between devices with their start and end apart: 62, of which 27 were waited for; matrix products, arithmetic and copies ran while one was open for 20% of the time, Pallas kernels for 22%

profile of v3, /device:TPU:0, one launch (start us, length us, event | category | flops | bytes accessed | tf_op | source)
XLA Modules:
  0.0 502.2 jit_solution(4038095541043816951)
XLA Ops:
  1.7 4.1 collective-permute-start
  7.9 8.1 %collective-permute-done = bf16[144,768]{1,0:T(8,128)(2,1)S(1)} collective-permute-done((bf16[144,768]{1,0:T(8,128)(2,1)S(1)}, bf16[144,768]{1,0:T(8,128)(2,1)S(1)}, u32[]{:S(2)}, u32[]{:S(2)}) %collective-permute-start) | collective-permute-done | bytes 221216 | tf_op jit(solution)/shard_map/ppermute | solution.py:787
  21.2 2.6 collective-permute-start.5
  30.7 4.3 collective-permute-done.9
  36.9 2.7 collective-permute-start.10
  45.0 3.5 collective-permute-done.11
  57.7 2.7 collective-permute-done.12
  66.1 16.2 %collective-permute-done.6 = bf16[256,512]{1,0:T(8,128)(2,1)S(1)} collective-permute-done((bf16[256,512]{1,0:T(8,128)(2,1)S(1)}, bf16[256,512]{1,0:T(8,128)(2,1)S(1)}, u32[]{:S(2)}, u32[]{:S(2)}) %collective-permute-start.6) | collective-permute-done | bytes 262176 | tf_op jit(solution)/shard_map/ppermute | solution.py:787
  84.5 2.6 collective-permute-start.16
  91.5 13.2 %project.1 = (bf16[2048,256]{1,0:T(8,128)(2,1)}, bf16[2048,256]{1,0:T(8,128)(2,1)}, bf16[2048,256]{1,0:T(8,128)(2,1)}, bf16[8,256,1024]{2,1,0:T(8,128)(2,1)}) custom-call(s32[8]{0:T(128)} %convert_add_fusion.9.slot_of, bf16[2,256,1024]{2,1,0:T(8,128)(2,1)} %copy-done.2, bf16[2,256,1024]{2,1,0:T(8,128)(2,1)} %copy-done.15, ...), custom_call_target="tpu_custom_call" | custom-call | flops 130000000 | bytes 1024 | tf_op jit(solution)/shard_map/project/pallas_call | solution.py:592
  112.2 15.4 %attend.2 = (f32[2048,128]{1,0:T(8,128)}, bf16[8,256,128]{2,1,0:T(8,128)(2,1)}, f32[1,2,2048]{2,1,0:T(2,128)}) custom-call(s32[4,4]{1,0:T(4,128)} %pad_add_fusion.bounds, s32[8]{0:T(128)} %convert_add_fusion.9.slot_of, bf16[2048,256]{1,0:T(8,128)(2,1)} %get-tuple-element.141.q_ref, bf16[2048,256]{1,0:T(8,128)(2,1)} %get-tuple-element.129.k_ref, ...), custom_call_target="tpu_custom_call" | custom-call | flops 140000000 | bytes 1024 | tf_op jit(solution)/shard_map/attend/pallas_call | solution.py:427
  129.0 4.9 collective-permute-done.22
  138.2 15.4 %attend.3 = (f32[2048,128]{1,0:T(8,128)}, bf16[8,256,128]{2,1,0:T(8,128)(2,1)}, f32[1,2,2048]{2,1,0:T(2,128)}) custom-call(s32[4,4]{1,0:T(4,128)} %pad_add_fusion.bounds, s32[8]{0:T(128)} %convert_add_fusion.9.slot_of, bf16[2048,256]{1,0:T(8,128)(2,1)} %get-tuple-element.141.q_ref, bf16[2048,256]{1,0:T(8,128)(2,1)} %get-tuple-element.129.k_ref, ...), custom_call_target="tpu_custom_call" | custom-call | flops 140000000 | bytes 1024 | tf_op jit(solution)/shard_map/attend/pallas_call | solution.py:427
  159.3 5.4 %collective-permute-done.24.far = bf16[2,256,256]{2,1,0:T(8,128)(2,1)S(1)} collective-permute-done((bf16[2,256,256]{2,1,0:T(8,128)(2,1)S(1)}, bf16[2,256,256]{2,1,0:T(8,128)(2,1)S(1)}, u32[]{:S(2)}, u32[]{:S(2)}) %collective-permute-start.24) | collective-permute-done | bytes 262176 | tf_op jit(solution)/shard_map/ppermute | solution.py:787
  165.4 4.1 collective-permute-done.25.both
  170.2 6.9 %mix.1 = (bf16[512,1024]{1,0:T(8,128)(2,1)}, f32[512,1024]{1,0:T(8,128)}, f32[512,1]{1,0:T(8,128)}, f32[512,1024]{1,0:T(8,128)}, bf16[512,1024]{1,0:T(8,128)(2,1)}) custom-call(s32[1]{0:T(128)} %bitcast.group, bf16[2,256,256]{2,1,0:T(8,128)(2,1)} %get-tuple-element.293.own, bf16[2,256,256]{2,1,0:T(8,128)(2,1)} %copy-done.25, ...), custom_call_target="tpu_custom_call" | custom-call | flops 60000000 | bytes 1024 | tf_op jit(solution)/shard_map/mix/pallas_call | solution.py:592
  181.2 4.1 collective-permute-done.28
  185.3 5.5 %collective-permute-done.29 = bf16[2,1,128,2048]{3,2,1,0:T(8,128)(2,1)S(1)} collective-permute-done((bf16[2,1,128,2048]{3,2,1,0:T(8,128)(2,1)S(1)}, bf16[2,1,128,2048]{3,2,1,0:T(8,128)(2,1)S(1)}, u32[]{:S(2)}, u32[]{:S(2)}) %collective-permute-start.29) | collective-permute-done | bytes 1048608 | tf_op jit(solution)/shard_map/ppermute | solution.py:787
  194.5 9.5 %add_convert_fusion = (bf16[1024,2048]{1,0:T(8,128)(2,1)}, bf16[1024,2048]{1,0:T(8,128)(2,1)S(1)}) fusion(bf16[1024,1024]{1,0:T(8,128)(2,1)S(1)} %constant_dynamic-update-slice_fusion.2, bf16[1024,2048]{1,0:T(8,128)(2,1)S(1)} %bitcast.416), kind=kOutput, calls=%fused_computation.1 | convolution fusion | flops 4330618880 | bytes 14680064 | tf_op jit(solution)/shard_map/dot_general | solution.py:830
  204.1 3.1 collective-permute-done.32
  207.1 4.4 collective-permute-done.33
  215.7 3.7 fusion.9.terms_ref
  220.8 4.6 finish.1
  228.5 7.4 %convolution_convert_fusion.1 = bf16[1024,2048]{1,0:T(8,128)(2,1)S(1)} fusion(bf16[1024,1024]{1,0:T(8,128)(2,1)S(1)} %constant_dynamic-update-slice_fusion.4, bf16[1024,2048]{1,0:T(8,128)(2,1)} %copy-done.40), kind=kOutput, calls=%fused_computation.9 | convolution fusion | flops 4297064448 | bytes 10485760 | tf_op jit(solution)/shard_map/dot_general | solution.py:830
  235.9 4.7 multiply_convert_fusion
  240.7 4.9 convolution_convert_fusion
  245.6 3.4 fusion.16
  257.3 6.5 %fusion.5.terms_ref = f32[512,1024]{1,0:T(8,128)} fusion(bf16[1024,2048]{1,0:T(8,128)(2,1)} %bitcast.417, bf16[1024,2048]{1,0:T(8,128)(2,1)} %copy-done.41), kind=kOutput, calls=%fused_computation.45 | convolution fusion | flops 2147483648 | bytes 8388608 | tf_op jit(solution)/shard_map/dot_general | solution.py:830
  263.8 8.8 %turn.1 = (f32[512,1024]{1,0:T(8,128)}, bf16[512,1024]{1,0:T(8,128)(2,1)}, bf16[4,2,256,256]{3,2,1,0:T(8,128)(2,1)}, f32[1,1024]{1,0:T(1,128)}, f32[1,1024]{1,0:T(1,128)}) custom-call(s32[1]{0:T(128)} %bitcast.group, f32[512,1024]{1,0:T(8,128)} %fusion.5.terms_ref, bf16[512,1024]{1,0:T(8,128)(2,1)} %collective-permute-done.37.sent_ref, ...), custom_call_target="tpu_custom_call" | custom-call | flops 80000000 | bytes 1024 | tf_op jit(solution)/shard_map/turn/pallas_call | solution.py:592
  278.7 4.0 collective-permute-done.40
  282.7 5.1 %collective-permute-done.38 = bf16[2,256,256]{2,1,0:T(8,128)(2,1)S(1)} collective-permute-done((bf16[2,256,256]{2,1,0:T(8,128)(2,1)S(1)}, bf16[2,256,256]{2,1,0:T(8,128)(2,1)S(1)}, u32[]{:S(2)}, u32[]{:S(2)}) %collective-permute-start.38) | collective-permute-done | bytes 262176 | tf_op jit(solution)/shard_map/ppermute | solution.py:787
  289.5 9.5 %collective-permute-start.41 = (bf16[512,1024]{1,0:T(8,128)(2,1)}, bf16[512,1024]{1,0:T(8,128)(2,1)}, u32[]{:S(2)}, u32[]{:S(2)}) collective-permute-start(bf16[512,1024]{1,0:T(8,128)(2,1)} %get-tuple-element.170), channel_id=1, source_target_pairs={{4,2},{2,4},{0,0},{6,6},{5,3},{3,5},{1,1},{7,7},{12,10},{10,12},{8... | collective-permute-start | bytes 3145736 | tf_op jit(solution)/shard_map/ppermute | solution.py:797
  299.0 23.3 %attend_back.2 = bf16[3,8,256,128]{3,2,1,0:T(8,128)(2,1)} custom-call(s32[4,4]{1,0:T(4,128)} %pad_add_fusion.bounds, s32[8]{0:T(128)} %convert_add_fusion.9.slot_of, bf16[2048,256]{1,0:T(8,128)(2,1)} %get-tuple-element.141.q_ref, bf16[2048,256]{1,0:T(8,128)(2,1)} %get-tuple-element.129.k_ref, bf16[2048,256]{1,0:T(8,128)(2,1)} %get-tuple-element.130.v_ref, ...), custom_call_target="tpu_custom_call" | custom-call | flops 230000000 | bytes 1024 | tf_op jit(solution)/shard_map/attend_back/pallas_call | solution.py:552
  322.3 2.7 fusion.19
  325.0 2.8 fusion.20
  333.5 23.6 %attend_back.3 = bf16[3,8,256,128]{3,2,1,0:T(8,128)(2,1)} custom-call(s32[4,4]{1,0:T(4,128)} %pad_add_fusion.bounds, s32[8]{0:T(128)} %convert_add_fusion.9.slot_of, bf16[2048,256]{1,0:T(8,128)(2,1)} %get-tuple-element.141.q_ref, bf16[2048,256]{1,0:T(8,128)(2,1)} %get-tuple-element.129.k_ref, bf16[2048,256]{1,0:T(8,128)(2,1)} %get-tuple-element.130.v_ref, ...), custom_call_target="tpu_custom_call" | custom-call | flops 230000000 | bytes 1024 | tf_op jit(solution)/shard_map/attend_back/pallas_call | solution.py:552
  360.1 3.1 convolution_convert_fusion.3
  372.8 3.6 multiply_reduce_fusion
  381.3 13.0 %collective-permute-done.52 = bf16[512,256]{1,0:T(8,128)(2,1)} collective-permute-done((bf16[512,256]{1,0:T(8,128)(2,1)}, bf16[512,256]{1,0:T(8,128)(2,1)}, u32[]{:S(2)}, u32[]{:S(2)}) %collective-permute-start.52) | collective-permute-done | bytes 262176 | tf_op jit(solution)/shard_map/ppermute | solution.py:787
  395.5 2.5 add_convert_fusion.1
  403.6 8.0 %collective-permute-done.50 = bf16[2,512,512]{2,1,0:T(8,128)(2,1)S(1)} collective-permute-done((bf16[2,512,512]{2,1,0:T(8,128)(2,1)}, bf16[2,512,512]{2,1,0:T(8,128)(2,1)S(1)}, u32[]{:S(2)}, u32[]{:S(2)}) %collective-permute-start.50) | collective-permute-done | bytes 1048608 | tf_op jit(solution)/shard_map/ppermute | solution.py:787
  416.0 3.5 fusion.28.keep_ref
  419.4 25.2 %collective-permute-done.49.far_ref = bf16[512,1024]{1,0:T(8,128)(2,1)S(1)} collective-permute-done((bf16[512,1024]{1,0:T(8,128)(2,1)S(1)}, bf16[512,1024]{1,0:T(8,128)(2,1)S(1)}, u32[]{:S(2)}, u32[]{:S(2)}) %collective-permute-start.49) | collective-permute-done | bytes 1048608 | tf_op jit(solution)/shard_map/ppermute | solution.py:787
  445.6 4.8 end.1
  452.6 2.8 collective-permute-start.57
  456.9 6.2 %collective-permute-done.56 = bf16[128,896]{1,0:T(8,128)(2,1)S(1)} collective-permute-done((bf16[128,896]{1,0:T(8,128)(2,1)S(1)}, bf16[128,896]{1,0:T(8,128)(2,1)S(1)}, u32[]{:S(2)}, u32[]{:S(2)}) %collective-permute-start.56) | collective-permute-done | bytes 229408 | tf_op jit(solution)/shard_map/ppermute | solution.py:787
  467.2 23.9 %collective-permute-done.58 = bf16[128,1152]{1,0:T(8,128)(2,1)S(1)} collective-permute-done((bf16[128,1152]{1,0:T(8,128)(2,1)S(1)}, bf16[128,1152]{1,0:T(8,128)(2,1)S(1)}, u32[]{:S(2)}, u32[]{:S(2)}) %collective-permute-start.58) | collective-permute-done | bytes 294944 | tf_op jit(solution)/shard_map/ppermute | solution.py:787
  493.4 3.4 collective-permute-done.59
  (384 shorter events, 145.9 us)
Async XLA Ops:
  1.7 14.3 %collective-permute-start = (bf16[144,768]{1,0:T(8,128)(2,1)S(1)}, bf16[144,768]{1,0:T(8,128)(2,1)S(1)}, u32[]{:S(2)}, u32[]{:S(2)}) collective-permute-start(bf16[144,768]{1,0:T(8,128)(2,1)S(1)} %fusion.54), channel_id=1, source_target_pairs={{0,2},{1,3},{2,0},{3,1},{4,6},{5,7},{6,4},{7,5},{8,10},{9,11},{10,... | collective-permute-start | bytes 663560 | tf_op jit(solution)/shard_map/ppermute | solution.py:787
  17.1 33.9 %collective-permute-start.2 = (bf16[2,256,1024]{2,1,0:T(8,128)(2,1)}, bf16[2,256,1024]{2,1,0:T(8,128)(2,1)S(1)}, u32[]{:S(2)}, u32[]{:S(2)}) collective-permute-start(bf16[2,256,1024]{2,1,0:T(8,128)(2,1)} %bitcast.465), channel_id=1, source_target_pairs={{4,2},{2,4},{0,0},{6,6},{5,3},{3,5},{1,1},{7,7},{12,10},{10,12},{8... | collective-permute-start | bytes 3145736 | tf_op jit(solution)/shard_map/ppermute | solution.py:797
  20.6 21.8 %collective-permute-start.4 = (bf16[2,128,512]{2,1,0:T(8,128)(2,1)}, bf16[2,128,512]{2,1,0:T(8,128)(2,1)}, u32[]{:S(2)}, u32[]{:S(2)}) collective-permute-start(bf16[2,128,512]{2,1,0:T(8,128)(2,1)} %pad_maximum_fusion.33), channel_id=1, source_target_pairs={{0,4},{4,0},{1,5},{5,1},{2,6},{6,2},{3,7},{7,3},{8,12},{12,8},{9,1... | collective-permute-start | bytes 786440 | tf_op jit(solution)/shard_map/ppermute | solution.py:787
  21.2 33.3 %collective-permute-start.5 = (bf16[128,256]{1,0:T(8,128)(2,1)S(1)}, bf16[128,256]{1,0:T(8,128)(2,1)}, u32[]{:S(2)}, u32[]{:S(2)}) collective-permute-start(bf16[128,256]{1,0:T(8,128)(2,1)S(1)} %copy-done.31), channel_id=1, source_target_pairs={{0,2},{1,3},{2,0},{3,1},{4,6},{5,7},{6,4},{7,5},{8,10},{9,11},{10,... | collective-permute-start | bytes 196616 | tf_op jit(solution)/shard_map/ppermute | solution.py:787
  48.7 11.7 %collective-permute-start.12 = (bf16[2,2,144,384]{3,2,1,0:T(8,128)(2,1)S(1)}, bf16[2,2,144,384]{3,2,1,0:T(8,128)(2,1)S(1)}, u32[]{:S(2)}, u32[]{:S(2)}) collective-permute-start(bf16[2,2,144,384]{3,2,1,0:T(8,128)(2,1)S(1)} %pad_maximum_fusion.26), channel_id=1, source_target_pairs={{0,16},{8,24},{16,0},{24,8},{1,17},{9,25},{17,1},{25,9},{2,18},{10... | collective-permute-start | bytes 1327112 | tf_op jit(solution)/shard_map/ppermute | solution.py:787
  51.0 32.0 %collective-permute-start.3 = (bf16[2,256,1024]{2,1,0:T(8,128)(2,1)S(1)}, bf16[2,256,1024]{2,1,0:T(8,128)(2,1)S(1)}, u32[]{:S(2)}, u32[]{:S(2)}) collective-permute-start(bf16[2,256,1024]{2,1,0:T(8,128)(2,1)S(1)} %collective-permute-done.2.x0.x_ref), channel_id=1, source_target_pairs={{0,1},{1,0},{2,3},{3,2},{4,5},{5,4},{6,7},{7,6},{8,9},{9,8},{10,11... | collective-permute-start | bytes 3145736 | tf_op jit(solution)/shard_map/ppermute | solution.py:787
  53.5 11.1 %collective-permute-start.14 = (bf16[2,2,144,384]{3,2,1,0:T(8,128)(2,1)S(1)}, bf16[2,2,144,384]{3,2,1,0:T(8,128)(2,1)S(1)}, u32[]{:S(2)}, u32[]{:S(2)}) collective-permute-start(bf16[2,2,144,384]{3,2,1,0:T(8,128)(2,1)S(1)} %pad_maximum_fusion.27), channel_id=1, source_target_pairs={{0,8},{8,0},{16,24},{24,16},{1,9},{9,1},{17,25},{25,17},{2,10},{10... | collective-permute-start | bytes 1327112 | tf_op jit(solution)/shard_map/ppermute | solution.py:787
  54.4 36.9 %collective-permute-start.7 = (bf16[2,256,1024]{2,1,0:T(8,128)(2,1)S(1)}, bf16[2,256,1024]{2,1,0:T(8,128)(2,1)}, u32[]{:S(2)}, u32[]{:S(2)}) collective-permute-start(bf16[2,256,1024]{2,1,0:T(8,128)(2,1)S(1)} %collective-permute-done.2.x0.x_ref), channel_id=1, source_target_pairs={{0,4},{4,0},{1,5},{5,1},{2,6},{6,2},{3,7},{7,3},{8,12},{12,8},{9,1... | collective-permute-start | bytes 3145736 | tf_op jit(solution)/shard_map/ppermute | solution.py:787
  54.4 27.8 %collective-permute-start.6 = (bf16[256,512]{1,0:T(8,128)(2,1)S(1)}, bf16[256,512]{1,0:T(8,128)(2,1)S(1)}, u32[]{:S(2)}, u32[]{:S(2)}) collective-permute-start(bf16[256,512]{1,0:T(8,128)(2,1)S(1)} %get-tuple-element.117), channel_id=1, source_target_pairs={{0,2},{1,3},{2,0},{3,1},{4,6},{5,7},{6,4},{7,5},{8,10},{9,11},{10,... | collective-permute-start | bytes 786440 | tf_op jit(solution)/shard_map/ppermute | solution.py:787
  60.4 24.0 %collective-permute-start.15 = (bf16[128,512]{1,0:T(8,128)(2,1)S(1)}, bf16[128,512]{1,0:T(8,128)(2,1)S(1)}, u32[]{:S(2)}, u32[]{:S(2)}) collective-permute-start(bf16[128,512]{1,0:T(8,128)(2,1)S(1)} %pad_maximum_fusion.41), channel_id=1, source_target_pairs={{0,1},{1,0},{2,3},{3,2},{4,5},{5,4},{6,7},{7,6},{8,9},{9,8},{10,11... | collective-permute-start | bytes 393224 | tf_op jit(solution)/shard_map/ppermute | solution.py:787
  84.5 20.2 %collective-permute-start.16 = (bf16[256,1024]{1,0:T(8,128)(2,1)S(1)}, bf16[256,1024]{1,0:T(8,128)(2,1)}, u32[]{:S(2)}, u32[]{:S(2)}) collective-permute-start(bf16[256,1024]{1,0:T(8,128)(2,1)S(1)} %pad_maximum_fusion.21), channel_id=1, source_target_pairs={{0,1},{1,0},{2,3},{3,2},{4,5},{5,4},{6,7},{7,6},{8,9},{9,8},{10,11... | collective-permute-start | bytes 1572872 | tf_op jit(solution)/shard_map/ppermute | solution.py:787
  87.1 17.6 %collective-permute-start.17 = (bf16[256,512]{1,0:T(8,128)(2,1)S(1)}, bf16[256,512]{1,0:T(8,128)(2,1)S(1)}, u32[]{:S(2)}, u32[]{:S(2)}) collective-permute-start(bf16[256,512]{1,0:T(8,128)(2,1)S(1)} %get-tuple-element.124), channel_id=1, source_target_pairs={{0,2},{1,3},{2,0},{3,1},{4,6},{5,7},{6,4},{7,5},{8,10},{9,11},{10,... | collective-permute-start | bytes 786440 | tf_op jit(solution)/shard_map/ppermute | solution.py:787
  88.8 15.9 %collective-permute-start.18 = (bf16[1,128,1024]{2,1,0:T(8,128)(2,1)S(1)}, bf16[1,128,1024]{2,1,0:T(8,128)(2,1)}, u32[]{:S(2)}, u32[]{:S(2)}) collective-permute-start(bf16[1,128,1024]{2,1,0:T(8,128)(2,1)S(1)} %maximum_bitcast_fusion.4), channel_id=1, source_target_pairs={{0,8},{8,0},{16,24},{24,16},{1,9},{9,1},{17,25},{25,17},{2,10},{10... | collective-permute-start | bytes 786440 | tf_op jit(solution)/shard_map/ppermute | solution.py:787
  106.0 22.7 %collective-permute-start.19 = (bf16[256,1024]{1,0:T(8,128)(2,1)S(1)}, bf16[256,1024]{1,0:T(8,128)(2,1)S(1)}, u32[]{:S(2)}, u32[]{:S(2)}) collective-permute-start(bf16[256,1024]{1,0:T(8,128)(2,1)S(1)} %pad_maximum_fusion.22), channel_id=1, source_target_pairs={{0,1},{1,0},{2,3},{3,2},{4,5},{5,4},{6,7},{7,6},{8,9},{9,8},{10,11... | collective-permute-start | bytes 1572872 | tf_op jit(solution)/shard_map/ppermute | solution.py:787
  108.9 19.9 %collective-permute-start.20 = (bf16[2,128,1024]{2,1,0:T(8,128)(2,1)S(1)}, bf16[2,128,1024]{2,1,0:T(8,128)(2,1)S(1)}, u32[]{:S(2)}, u32[]{:S(2)}) collective-permute-start(bf16[2,128,1024]{2,1,0:T(8,128)(2,1)S(1)} %pad_maximum_fusion.23), channel_id=1, source_target_pairs={{0,16},{8,24},{16,0},{24,8},{1,17},{9,25},{17,1},{25,9},{2,18},{10... | collective-permute-start | bytes 1572872 | tf_op jit(solution)/shard_map/ppermute | solution.py:787
  110.7 18.2 %collective-permute-start.21 = (bf16[1,128,2048]{2,1,0:T(8,128)(2,1)S(1)}, bf16[1,128,2048]{2,1,0:T(8,128)(2,1)S(1)}, u32[]{:S(2)}, u32[]{:S(2)}) collective-permute-start(bf16[1,128,2048]{2,1,0:T(8,128)(2,1)S(1)} %get-tuple-element.135), channel_id=1, source_target_pairs={{0,8},{8,0},{16,24},{24,16},{1,9},{9,1},{17,25},{25,17},{2,10},{10... | collective-permute-start | bytes 1572872 | tf_op jit(solution)/shard_map/ppermute | solution.py:787
  111.7 22.2 %collective-permute-start.22 = (bf16[1,128,2048]{2,1,0:T(8,128)(2,1)S(1)}, bf16[1,128,2048]{2,1,0:T(8,128)(2,1)S(1)}, u32[]{:S(2)}, u32[]{:S(2)}) collective-permute-start(bf16[1,128,2048]{2,1,0:T(8,128)(2,1)S(1)} %get-tuple-element.137), channel_id=1, source_target_pairs={{0,16},{8,24},{16,0},{24,8},{1,17},{9,25},{17,1},{25,9},{2,18},{10... | collective-permute-start | bytes 1572872 | tf_op jit(solution)/shard_map/ppermute | solution.py:787
  134.1 21.8 %collective-permute-start.26 = (bf16[4,128,1024]{2,1,0:T(8,128)(2,1)S(1)}, bf16[4,128,1024]{2,1,0:T(8,128)(2,1)S(1)}, u32[]{:S(2)}, u32[]{:S(2)}) collective-permute-start(bf16[4,128,1024]{2,1,0:T(8,128)(2,1)S(1)} %pad_maximum_fusion.14), channel_id=1, source_target_pairs={{0,4},{4,0},{1,5},{5,1},{2,6},{6,2},{3,7},{7,3},{8,12},{12,8},{9,1... | collective-permute-start | bytes 3145736 | tf_op jit(solution)/shard_map/ppermute | solution.py:787
  135.7 42.0 %collective-permute-start.30 = (bf16[1,128,2048]{2,1,0:T(8,128)(2,1)S(1)}, bf16[1,128,2048]{2,1,0:T(8,128)(2,1)}, u32[]{:S(2)}, u32[]{:S(2)}) collective-permute-start(bf16[1,128,2048]{2,1,0:T(8,128)(2,1)S(1)} %get-tuple-element.148), channel_id=1, source_target_pairs={{0,8},{8,0},{16,24},{24,16},{1,9},{9,1},{17,25},{25,17},{2,10},{10... | collective-permute-start | bytes 1572872 | tf_op jit(solution)/shard_map/ppermute | solution.py:787
  136.7 41.0 %collective-permute-start.31 = (bf16[1,128,2048]{2,1,0:T(8,128)(2,1)S(1)}, bf16[1,128,2048]{2,1,0:T(8,128)(2,1)S(1)}, u32[]{:S(2)}, u32[]{:S(2)}) collective-permute-start(bf16[1,128,2048]{2,1,0:T(8,128)(2,1)S(1)} %get-tuple-element.151), channel_id=1, source_target_pairs={{0,16},{8,24},{16,0},{24,8},{1,17},{9,25},{17,1},{25,9},{2,18},{10... | collective-permute-start | bytes 1572872 | tf_op jit(solution)/shard_map/ppermute | solution.py:787
  155.9 13.6 %collective-permute-start.25 = (bf16[2,256,256]{2,1,0:T(8,128)(2,1)S(1)}, bf16[2,256,256]{2,1,0:T(8,128)(2,1)S(1)}, u32[]{:S(2)}, u32[]{:S(2)}) collective-permute-start(bf16[2,256,256]{2,1,0:T(8,128)(2,1)S(1)} %get-tuple-element.290), channel_id=1, source_target_pairs={{0,5},{1,4},{2,7},{3,6},{4,1},{5,0},{6,3},{7,2},{8,13},{9,12},{10,... | collective-permute-start | bytes 786440 | tf_op jit(solution)/shard_map/ppermute | solution.py:824
  159.3 26.0 %collective-permute-start.28 = (bf16[2,128,2048]{2,1,0:T(8,128)(2,1)S(1)}, bf16[2,128,2048]{2,1,0:T(8,128)(2,1)S(1)}, u32[]{:S(2)}, u32[]{:S(2)}) collective-permute-start(bf16[2,128,2048]{2,1,0:T(8,128)(2,1)S(1)} %pad_maximum_fusion.13), channel_id=1, source_target_pairs={{0,16},{8,24},{16,0},{24,8},{1,17},{9,25},{17,1},{25,9},{2,18},{10... | collective-permute-start | bytes 3145736 | tf_op jit(solution)/shard_map/ppermute | solution.py:787
  164.7 26.1 %collective-permute-start.29 = (bf16[2,1,128,2048]{3,2,1,0:T(8,128)(2,1)S(1)}, bf16[2,1,128,2048]{3,2,1,0:T(8,128)(2,1)S(1)}, u32[]{:S(2)}, u32[]{:S(2)}) collective-permute-start(bf16[2,1,128,2048]{3,2,1,0:T(8,128)(2,1)S(1)} %copy-done.18), channel_id=1, source_target_pairs={{0,8},{8,0},{16,24},{24,16},{1,9},{9,1},{17,25},{25,17},{2,10},{10... | collective-permute-start | bytes 3145736 | tf_op jit(solution)/shard_map/ppermute | solution.py:787
  177.1 16.8 %collective-permute-start.27 = (bf16[512,1024]{1,0:T(8,128)(2,1)}, bf16[512,1024]{1,0:T(8,128)(2,1)S(1)}, u32[]{:S(2)}, u32[]{:S(2)}) collective-permute-start(bf16[512,1024]{1,0:T(8,128)(2,1)} %get-tuple-element.146), channel_id=1, source_target_pairs={{0,4},{4,0},{1,5},{5,1},{2,6},{6,2},{3,7},{7,3},{8,12},{12,8},{9,1... | collective-permute-start | bytes 3145736 | tf_op jit(solution)/shard_map/ppermute | solution.py:787
  178.9 28.2 %collective-permute-start.32 = (bf16[2,128,2048]{2,1,0:T(8,128)(2,1)S(1)}, bf16[2,128,2048]{2,1,0:T(8,128)(2,1)S(1)}, u32[]{:S(2)}, u32[]{:S(2)}) collective-permute-start(bf16[2,128,2048]{2,1,0:T(8,128)(2,1)S(1)} %pad_maximum_fusion.15), channel_id=1, source_target_pairs={{0,16},{8,24},{16,0},{24,8},{1,17},{9,25},{17,1},{25,9},{2,18},{10... | collective-permute-start | bytes 3145736 | tf_op jit(solution)/shard_map/ppermute | solution.py:787
  179.2 32.4 %collective-permute-start.33 = (bf16[2,1,128,2048]{3,2,1,0:T(8,128)(2,1)S(1)}, bf16[2,1,128,2048]{3,2,1,0:T(8,128)(2,1)S(1)}, u32[]{:S(2)}, u32[]{:S(2)}) collective-permute-start(bf16[2,1,128,2048]{3,2,1,0:T(8,128)(2,1)S(1)} %maximum_bitcast_fusion.3), channel_id=1, source_target_pairs={{0,8},{8,0},{16,24},{24,16},{1,9},{9,1},{17,25},{25,17},{2,10},{10... | collective-permute-start | bytes 3145736 | tf_op jit(solution)/shard_map/ppermute | solution.py:787
  193.1 26.4 %collective-permute-start.35 = (bf16[512,1024]{1,0:T(8,128)(2,1)S(1)}, bf16[512,1024]{1,0:T(8,128)(2,1)S(1)}, u32[]{:S(2)}, u32[]{:S(2)}) collective-permute-start(bf16[512,1024]{1,0:T(8,128)(2,1)S(1)} %bitcast.466), channel_id=1, source_target_pairs={{4,2},{2,4},{0,0},{6,6},{5,3},{3,5},{1,1},{7,7},{12,10},{10,12},{8... | collective-permute-start | bytes 3145736 | tf_op jit(solution)/shard_map/ppermute | solution.py:797
  251.8 12.0 %collective-permute-start.37 = (bf16[512,1024]{1,0:T(8,128)(2,1)}, bf16[512,1024]{1,0:T(8,128)(2,1)}, u32[]{:S(2)}, u32[]{:S(2)}) collective-permute-start(bf16[512,1024]{1,0:T(8,128)(2,1)} %fusion.16), channel_id=1, source_target_pairs={{0,4},{4,0},{1,5},{5,1},{2,6},{6,2},{3,7},{7,3},{8,12},{12,8},{9,1... | collective-permute-start | bytes 3145736 | tf_op jit(solution)/shard_map/ppermute | solution.py:787
  253.7 68.6 %collective-permute-start.42 = (bf16[2,256,2048]{2,1,0:T(8,128)(2,1)}, bf16[2,256,2048]{2,1,0:T(8,128)(2,1)}, u32[]{:S(2)}, u32[]{:S(2)}) collective-permute-start(bf16[2,256,2048]{2,1,0:T(8,128)(2,1)} %pad_maximum_fusion.5), channel_id=1, source_target_pairs={{0,8},{8,0},{16,24},{24,16},{1,9},{9,1},{17,25},{25,17},{2,10},{10... | collective-permute-start | bytes 6291464 | tf_op jit(solution)/shard_map/ppermute | solution.py:787
  255.7 66.6 %collective-permute-start.43 = (bf16[2,256,2048]{2,1,0:T(8,128)(2,1)}, bf16[2,256,2048]{2,1,0:T(8,128)(2,1)}, u32[]{:S(2)}, u32[]{:S(2)}) collective-permute-start(bf16[2,256,2048]{2,1,0:T(8,128)(2,1)} %pad_maximum_fusion.6), channel_id=1, source_target_pairs={{0,16},{8,24},{16,0},{24,8},{1,17},{9,25},{17,1},{25,9},{2,18},{10... | collective-permute-start | bytes 6291464 | tf_op jit(solution)/shard_map/ppermute | solution.py:787
  274.5 13.3 %collective-permute-start.38 = (bf16[2,256,256]{2,1,0:T(8,128)(2,1)S(1)}, bf16[2,256,256]{2,1,0:T(8,128)(2,1)S(1)}, u32[]{:S(2)}, u32[]{:S(2)}) collective-permute-start(bf16[2,256,256]{2,1,0:T(8,128)(2,1)S(1)} %get-tuple-element.285), channel_id=1, source_target_pairs={{0,1},{1,0},{2,3},{3,2},{4,5},{5,4},{6,7},{7,6},{8,9},{9,8},{10,11... | collective-permute-start | bytes 786440 | tf_op jit(solution)/shard_map/ppermute | solution.py:787
  289.0 41.2 %collective-permute-start.44 = (bf16[4,128,1024]{2,1,0:T(8,128)(2,1)}, bf16[4,128,1024]{2,1,0:T(8,128)(2,1)}, u32[]{:S(2)}, u32[]{:S(2)}) collective-permute-start(bf16[4,128,1024]{2,1,0:T(8,128)(2,1)} %dynamic-slice_bitcast_fusion.4), channel_id=1, source_target_pairs={{0,4},{4,0},{1,5},{5,1},{2,6},{6,2},{3,7},{7,3},{8,12},{12,8},{9,1... | collective-permute-start | bytes 3145736 | tf_op jit(solution)/shard_map/ppermute | solution.py:787
  289.5 44.0 %collective-permute-start.41 = (bf16[512,1024]{1,0:T(8,128)(2,1)}, bf16[512,1024]{1,0:T(8,128)(2,1)}, u32[]{:S(2)}, u32[]{:S(2)}) collective-permute-start(bf16[512,1024]{1,0:T(8,128)(2,1)} %get-tuple-element.170), channel_id=1, source_target_pairs={{4,2},{2,4},{0,0},{6,6},{5,3},{3,5},{1,1},{7,7},{12,10},{10,12},{8... | collective-permute-start | bytes 3145736 | tf_op jit(solution)/shard_map/ppermute | solution.py:797
  325.0 32.0 %collective-permute-start.45 = (bf16[256,2048]{1,0:T(8,128)(2,1)}, bf16[256,2048]{1,0:T(8,128)(2,1)}, u32[]{:S(2)}, u32[]{:S(2)}) collective-permute-start(bf16[256,2048]{1,0:T(8,128)(2,1)} %fusion.19), channel_id=1, source_target_pairs={{0,16},{8,24},{16,0},{24,8},{1,17},{9,25},{17,1},{25,9},{2,18},{10... | collective-permute-start | bytes 3145736 | tf_op jit(solution)/shard_map/ppermute | solution.py:787
  327.8 29.3 %collective-permute-start.46 = (bf16[256,2048]{1,0:T(8,128)(2,1)}, bf16[256,2048]{1,0:T(8,128)(2,1)}, u32[]{:S(2)}, u32[]{:S(2)}) collective-permute-start(bf16[256,2048]{1,0:T(8,128)(2,1)} %fusion.20), channel_id=1, source_target_pairs={{0,8},{8,0},{16,24},{24,16},{1,9},{9,1},{17,25},{25,17},{2,10},{10... | collective-permute-start | bytes 3145736 | tf_op jit(solution)/shard_map/ppermute | solution.py:787
  333.1 24.0 %collective-permute-start.47 = (bf16[2,512,256]{2,1,0:T(8,128)(2,1)}, bf16[2,512,256]{2,1,0:T(8,128)(2,1)}, u32[]{:S(2)}, u32[]{:S(2)}) collective-permute-start(bf16[2,512,256]{2,1,0:T(8,128)(2,1)} %get-tuple-element.277), channel_id=1, source_target_pairs={{0,1},{1,0},{2,3},{3,2},{4,5},{5,4},{6,7},{7,6},{8,9},{9,8},{10,11... | collective-permute-start | bytes 1572872 | tf_op jit(solution)/shard_map/ppermute | solution.py:787
  363.3 32.2 %collective-permute-start.48 = (bf16[1024,1024]{1,0:T(8,128)(2,1)}, bf16[1024,1024]{1,0:T(8,128)(2,1)}, u32[]{:S(2)}, u32[]{:S(2)}) collective-permute-start(bf16[1024,1024]{1,0:T(8,128)(2,1)} %convolution_convert_fusion.3), channel_id=1, source_target_pairs={{0,4},{4,0},{1,5},{5,1},{2,6},{6,2},{3,7},{7,3},{8,12},{12,8},{9,1... | collective-permute-start | bytes 6291464 | tf_op jit(solution)/shard_map/ppermute | solution.py:787
  378.6 19.5 %collective-permute-start.51 = (bf16[4,128,896]{2,1,0:T(8,128)(2,1)}, bf16[4,128,896]{2,1,0:T(8,128)(2,1)}, u32[]{:S(2)}, u32[]{:S(2)}) collective-permute-start(bf16[4,128,896]{2,1,0:T(8,128)(2,1)} %get-tuple-element.269), channel_id=1, source_target_pairs={{0,4},{4,0},{1,5},{5,1},{2,6},{6,2},{3,7},{7,3},{8,12},{12,8},{9,1... | collective-permute-start | bytes 2752520 | tf_op jit(solution)/shard_map/ppermute | solution.py:787
  379.0 15.2 %collective-permute-start.52 = (bf16[512,256]{1,0:T(8,128)(2,1)}, bf16[512,256]{1,0:T(8,128)(2,1)}, u32[]{:S(2)}, u32[]{:S(2)}) collective-permute-start(bf16[512,256]{1,0:T(8,128)(2,1)} %fusion.49), channel_id=1, source_target_pairs={{0,2},{1,3},{2,0},{3,1},{4,6},{5,7},{6,4},{7,5},{8,10},{9,11},{10,... | collective-permute-start | bytes 786440 | tf_op jit(solution)/shard_map/ppermute | solution.py:787
  381.0 30.6 %collective-permute-start.50 = (bf16[2,512,512]{2,1,0:T(8,128)(2,1)}, bf16[2,512,512]{2,1,0:T(8,128)(2,1)S(1)}, u32[]{:S(2)}, u32[]{:S(2)}) collective-permute-start(bf16[2,512,512]{2,1,0:T(8,128)(2,1)} %get-tuple-element.243), channel_id=1, source_target_pairs={{0,1},{1,0},{2,3},{3,2},{4,5},{5,4},{6,7},{7,6},{8,9},{9,8},{10,11... | collective-permute-start | bytes 3145736 | tf_op jit(solution)/shard_map/ppermute | solution.py:787
  398.0 46.6 %collective-permute-start.49 = (bf16[512,1024]{1,0:T(8,128)(2,1)S(1)}, bf16[512,1024]{1,0:T(8,128)(2,1)S(1)}, u32[]{:S(2)}, u32[]{:S(2)}) collective-permute-start(bf16[512,1024]{1,0:T(8,128)(2,1)S(1)} %add_convert_fusion.1), channel_id=1, source_target_pairs={{0,1},{1,0},{2,3},{3,2},{4,5},{5,4},{6,7},{7,6},{8,9},{9,8},{10,11... | collective-permute-start | bytes 3145736 | tf_op jit(solution)/shard_map/ppermute | solution.py:787
  400.7 51.8 %collective-permute-start.55 = (bf16[2,128,1024]{2,1,0:T(8,128)(2,1)S(1)}, bf16[2,128,1024]{2,1,0:T(8,128)(2,1)S(1)}, u32[]{:S(2)}, u32[]{:S(2)}) collective-permute-start(bf16[2,128,1024]{2,1,0:T(8,128)(2,1)S(1)} %dynamic-slice_bitcast_fusion.11), channel_id=1, source_target_pairs={{0,16},{8,24},{16,0},{24,8},{1,17},{9,25},{17,1},{25,9},{2,18},{10... | collective-permute-start | bytes 1572872 | tf_op jit(solution)/shard_map/ppermute | solution.py:787
  402.1 50.4 %collective-permute-start.54 = (bf16[2,128,896]{2,1,0:T(8,128)(2,1)}, bf16[2,128,896]{2,1,0:T(8,128)(2,1)}, u32[]{:S(2)}, u32[]{:S(2)}) collective-permute-start(bf16[2,128,896]{2,1,0:T(8,128)(2,1)} %dynamic-slice_bitcast_fusion.12), channel_id=1, source_target_pairs={{0,8},{8,0},{16,24},{24,16},{1,9},{9,1},{17,25},{25,17},{2,10},{10... | collective-permute-start | bytes 1376264 | tf_op jit(solution)/shard_map/ppermute | solution.py:787
  411.8 44.8 %collective-permute-start.60 = (bf16[512,512]{1,0:T(8,128)(2,1)S(1)}, bf16[512,512]{1,0:T(8,128)(2,1)S(1)}, u32[]{:S(2)}, u32[]{:S(2)}) collective-permute-start(bf16[512,512]{1,0:T(8,128)(2,1)S(1)} %fusion.34), channel_id=1, source_target_pairs={{0,2},{1,3},{2,0},{3,1},{4,6},{5,7},{6,4},{7,5},{8,10},{9,11},{10,... | collective-permute-start | bytes 1572872 | tf_op jit(solution)/shard_map/ppermute | solution.py:787
  450.5 47.7 %collective-permute-start.53 = (bf16[512,1024]{1,0:T(8,128)(2,1)}, bf16[512,1024]{1,0:T(8,128)(2,1)S(1)}, u32[]{:S(2)}, u32[]{:S(2)}) collective-permute-start(bf16[512,1024]{1,0:T(8,128)(2,1)} %end.1), channel_id=1, source_target_pairs={{4,2},{2,4},{0,0},{6,6},{5,3},{3,5},{1,1},{7,7},{12,10},{10,12},{8... | collective-permute-start | bytes 3145736 | tf_op jit(solution)/shard_map/ppermute | solution.py:797
  452.6 11.6 %collective-permute-start.57 = (bf16[128,1024]{1,0:T(8,128)(2,1)S(1)}, bf16[128,1024]{1,0:T(8,128)(2,1)S(1)}, u32[]{:S(2)}, u32[]{:S(2)}) collective-permute-start(bf16[128,1024]{1,0:T(8,128)(2,1)S(1)} %fusion.43), channel_id=1, source_target_pairs={{0,8},{8,0},{16,24},{24,16},{1,9},{9,1},{17,25},{25,17},{2,10},{10... | collective-permute-start | bytes 786440 | tf_op jit(solution)/shard_map/ppermute | solution.py:787
  456.8 10.4 %collective-permute-start.61 = (bf16[2,128,512]{2,1,0:T(8,128)(2,1)S(1)}, bf16[2,128,512]{2,1,0:T(8,128)(2,1)S(1)}, u32[]{:S(2)}, u32[]{:S(2)}) collective-permute-start(bf16[2,128,512]{2,1,0:T(8,128)(2,1)S(1)} %dynamic-slice_bitcast_fusion.13), channel_id=1, source_target_pairs={{0,4},{4,0},{1,5},{5,1},{2,6},{6,2},{3,7},{7,3},{8,12},{12,8},{9,1... | collective-permute-start | bytes 786440 | tf_op jit(solution)/shard_map/ppermute | solution.py:787
  465.2 26.0 %collective-permute-start.58 = (bf16[128,1152]{1,0:T(8,128)(2,1)S(1)}, bf16[128,1152]{1,0:T(8,128)(2,1)S(1)}, u32[]{:S(2)}, u32[]{:S(2)}) collective-permute-start(bf16[128,1152]{1,0:T(8,128)(2,1)S(1)} %get-tuple-element.358), channel_id=1, source_target_pairs={{0,2},{1,3},{2,0},{3,1},{4,6},{5,7},{6,4},{7,5},{8,10},{9,11},{10,... | collective-permute-start | bytes 884744 | tf_op jit(solution)/shard_map/ppermute | solution.py:787
  (57 other events, 387.5 us)

commit v4 on v3

--- a/solution.py
+++ b/solution.py
@@ -324,12 +324,12 @@
 
 F32 = jnp.float32
 BF16 = jnp.bfloat16
-VMEM = 56 * 1024 * 1024
-
-
-def params(grid_rank):
+MIB = 1024 * 1024
+
+
+def params(grid_rank, mebibytes=24):
     return pltpu.CompilerParams(
-        dimension_semantics=("arbitrary",) * grid_rank, vmem_limit_bytes=VMEM
+        dimension_semantics=("arbitrary",) * grid_rank, vmem_limit_bytes=mebibytes * MIB
     )
 
 
@@ -438,18 +438,20 @@
     )(bounds, slot_of, q, k, v, pcol, prow, srow)
 
 
-def attend_back_kernel(tile, bounds, slot_of, q_ref, k_ref, v_ref, do_ref, o_ref, lse_ref, pcol_ref,
-                       prow_ref, srow_ref, cos_ref, sin_ref, g_ref,
-                       qm, dom, qtm, dotm, delta, dqt):
-    j = pl.program_id(1)
-    count = pl.num_programs(1)
-    rows = q_ref.shape[0]
-
+def attend_back_kernel(tile, first, steps, bounds, slot_of, q_ref, k_ref, v_ref, do_ref, o_ref,
+                       lse_ref, pcol_ref, prow_ref, srow_ref, cos_ref, sin_ref, *refs):
+    qm, dom, qtm, dotm, delta, dqt = refs[-6:]
+    count = q_ref.shape[0] // tile
+    last = first + steps
+    before = refs[0] if first else None
+    g_ref = refs[1 if first else 0]
+    after_ref = refs[1] if last < count else None
+    j = first + pl.program_id(1)
     span = do_ref.shape[1]
 
-    @pl.when(j == 0)
+    @pl.when(pl.program_id(1) == 0)
     def _():
-        for t in range(rows // tile):
+        for t in range(first, count):
             part = pl.ds(t * tile, tile)
             q = q_ref[part, :].astype(F32)
             do = jnp.concatenate(
@@ -469,7 +471,10 @@
                 delta[h : h + 1, part] = jnp.sum(
                     prod[h * 64 : h * 64 + 64], axis=0, keepdims=True
                 )
-        dqt[...] = jnp.zeros_like(dqt)
+        if before is None:
+            dqt[...] = jnp.zeros_like(dqt)
+        else:
+            dqt[:, first * tile :] = before[0]
 
     here = pl.ds(pl.multiple_of(j * tile, tile), tile)
     k = k_ref[here, :]
@@ -510,39 +515,55 @@
 
     grad_k, grad_v = unturned(dk, here), dv.astype(BF16)
     for b in range(tile // span):
-        at = slot_of[j * (tile // span) + b]
-        g_ref[1, at] = grad_k[b * span : (b + 1) * span]
-        g_ref[2, at] = grad_v[b * span : (b + 1) * span]
-
-    @pl.when(j == count - 1)
+        at = slot_of[j * (tile // span) + b] >> 1
+        g_ref[at, :, 128:256] = grad_k[b * span : (b + 1) * span]
+        g_ref[at, :, 256:384] = grad_v[b * span : (b + 1) * span]
+
+    @pl.when(pl.program_id(1) == steps - 1)
     def _():
-        for t in range(rows // tile):
+        for t in range(first, last):
             part = pl.ds(t * tile, tile)
             grad_q = unturned(dqt[:, part].T * 0.125, part)
             for b in range(tile // span):
-                at = slot_of[t * (tile // span) + b]
-                g_ref[0, at] = grad_q[b * span : (b + 1) * span]
-
-
-def attend_back(pair, q, k, v, do, o, lse, pcol, prow, srow, cosine, sine, bounds, slot_of, tile):
+                at = slot_of[t * (tile // span) + b] >> 1
+                g_ref[at, :, 0:128] = grad_q[b * span : (b + 1) * span]
+        if after_ref is not None:
+            after_ref[0] = dqt[:, last * tile :]
+
+
+def attend_back(half, q, k, v, do, o, lse, pcol, prow, srow, cosine, sine, bounds, slot_of, tile,
+                before):
     rows, width = q.shape
+    pairs = width // 128
     blocks, span, _ = do.shape
     count = rows // tile
-    whole = pl.BlockSpec((rows, 128), lambda p, j, b, t: (0, pair))
+    steps = count // 2
+    first = half * steps
+    whole = pl.BlockSpec((rows, 128), lambda p, j, b, t: (0, p))
     table = pl.BlockSpec((rows, 128), lambda p, j, b, t: (0, 0))
     line = pl.BlockSpec((1, rows), lambda p, j, b, t: (0, 0))
+    rest = pl.BlockSpec((1, 128, rows // 2), lambda p, j, b, t: (p, 0, 0))
+    outs = [
+        (
+            jax.ShapeDtypeStruct((blocks // 2, span, 3 * width), BF16),
+            pl.BlockSpec((blocks // 2, span, 384), lambda p, j, b, t: (0, 0, p)),
+        )
+    ]
+    if not half:
+        outs.append((jax.ShapeDtypeStruct((pairs, 128, rows // 2), F32), rest))
     grid_spec = pltpu.PrefetchScalarGridSpec(
         num_scalar_prefetch=2,
-        grid=(1, count),
+        grid=(pairs, steps),
         in_specs=[
             whole, whole, whole,
-            pl.BlockSpec((blocks, span, 128), lambda p, j, b, t: (0, 0, pair)),
-            table,
-            pl.BlockSpec((1, 2, rows), lambda p, j, b, t: (0, 0, 0)),
+            pl.BlockSpec((blocks, span, 128), lambda p, j, b, t: (0, 0, p)),
+            whole,
+            pl.BlockSpec((1, 2, rows), lambda p, j, b, t: (p, 0, 0)),
             pl.BlockSpec((rows, 1), lambda p, j, b, t: (0, 0)),
             line, line, table, table,
-        ],
-        out_specs=pl.BlockSpec((3, blocks, span, 128), lambda p, j, b, t: (0, 0, 0, 0)),
+        ]
+        + [rest] * len(before),
+        out_specs=[spec for _, spec in outs],
         scratch_shapes=[
             pltpu.VMEM((2, rows, 128), BF16), pltpu.VMEM((2, rows, 128), BF16),
             pltpu.VMEM((2, 128, rows), BF16), pltpu.VMEM((2, 128, rows), BF16),
@@ -550,13 +571,13 @@
         ],
     )
     return pl.pallas_call(
-        functools.partial(attend_back_kernel, tile),
+        functools.partial(attend_back_kernel, tile, first, steps),
         grid_spec=grid_spec,
-        out_shape=jax.ShapeDtypeStruct((3, blocks, span, 128), BF16),
-        compiler_params=params(2),
+        out_shape=[shape for shape, _ in outs],
+        compiler_params=params(2, 40),
         cost_estimate=lasting(23),
         name="attend_back",
-    )(bounds, slot_of, q, k, v, do, o, lse, pcol, prow, srow, cosine, sine)
+    )(bounds, slot_of, q, k, v, do, o, lse, pcol, prow, srow, cosine, sine, *before)
 
 
 def tile_bounds(starts_nat, tile):
@@ -612,46 +633,54 @@
     return pl.BlockSpec(shape, lambda *_: (0,) * len(shape))
 
 
-def project_kernel(slot_of, x0, x1, x2, x3, gain_ref, w_ref, cos_ref, sin_ref,
-                   q_ref, k_ref, v_ref, n_ref):
-    which = slot_of[pl.program_id(0)] >> 1
+def project_kernel(blocks, slots, near, far, gain_ref, w_ref, cos_ref, sin_ref, *refs):
+    q_ref, k_ref, v_ref, n_ref = refs[-4:]
     width = q_ref.shape[1]
-    near = jnp.where(which == 0, x0[0], x1[0])
-    far = jnp.where(which == 2, x2[0], x3[0])
-    x = jnp.where(which < 2, near, far).astype(F32)
+    x = jnp.where(slots[pl.program_id(0)] < 4, near[0], far[0]).astype(F32)
     normed = (normalized(x)[0] * gain_ref[0:1, :]).astype(BF16)
     n_ref[0] = normed
     linear = jnp.dot(normed, w_ref[...], preferred_element_type=F32)
     for at in range(0, width, 128):
-        q = turned(linear[:, at : at + 128], cos_ref[...], sin_ref[...])
-        k = turned(linear[:, width + at : width + at + 128], cos_ref[...], sin_ref[...])
+        q = turned(linear[:, 3 * at : 3 * at + 128], cos_ref[...], sin_ref[...])
+        k = turned(linear[:, 3 * at + 128 : 3 * at + 256], cos_ref[...], sin_ref[...])
         q_ref[:, at : at + 128] = q.astype(BF16) * jnp.asarray(0.125, BF16)
         k_ref[:, at : at + 128] = k.astype(BF16)
-    v_ref[...] = linear[:, 2 * width :].astype(BF16)
-
-
-def project(parts, gains, w, cosine, sine, slot_of):
-    count = slot_of.shape[0]
-    _, rows, depth = parts[0].shape
+        v_ref[:, at : at + 128] = linear[:, 3 * at + 256 : 3 * at + 384].astype(BF16)
+
+
+def project(near, far, gains, w, cosine, sine, blocks, slots, before):
+    _, rows, depth = near.shape
     width = w.shape[1] // 3
-    piece = pl.BlockSpec((1, rows, depth), lambda i, t: (t[i] & 1, 0, 0))
-    angle = pl.BlockSpec((rows, 128), lambda i, t: (i, 0))
-    out = shaped(BF16, count * rows, width), pl.BlockSpec((rows, width), lambda i, t: (i, 0))
-    normed = (
-        shaped(BF16, count, rows, depth),
-        pl.BlockSpec((1, rows, depth), lambda i, t: (t[i], 0, 0)),
-    )
-    return call(
-        project_kernel, "project", (count,), [slot_of],
-        [piece] * 4 + [fixed(*gains.shape), fixed(*w.shape), angle, angle],
-        [out, out, out, normed], 13, *parts, gains, w, cosine, sine,
-    )
+    count = 2 * blocks.shape[0]
+    piece = pl.BlockSpec((1, rows, depth), lambda i, b, s: (s[i] & 1, 0, 0))
+    angle = pl.BlockSpec((rows, 128), lambda i, b, s: (b[i], 0))
+    out = shaped(BF16, count * rows, width)
+    normed = shaped(BF16, count, rows, depth)
+    block = pl.BlockSpec((rows, width), lambda i, b, s: (b[i], 0))
+    return pl.pallas_call(
+        project_kernel,
+        grid_spec=pltpu.PrefetchScalarGridSpec(
+            num_scalar_prefetch=2,
+            grid=blocks.shape,
+            in_specs=[piece, piece, fixed(*gains.shape), fixed(*w.shape), angle, angle]
+            + [pl.BlockSpec(memory_space=pl.ANY)] * len(before),
+            out_specs=[
+                block, block, block,
+                pl.BlockSpec((1, rows, depth), lambda i, b, s: ((s[i] & 1) * 4 + (s[i] >> 1), 0, 0)),
+            ],
+        ),
+        out_shape=[out, out, out, normed],
+        input_output_aliases={8 + n: n for n in range(len(before))},
+        compiler_params=params(1),
+        cost_estimate=lasting(7),
+        name="project",
+    )(blocks, slots, near, far, gains, w, cosine, sine, *before)
 
 
 def mix_kernel(group, own, near, far, both, w_ref, x_ref, gain_ref,
                heads_ref, hat_ref, scale_ref, hidden_ref, mid_ref):
     width = own.shape[2]
-    for r, piece in enumerate((own[0], near[0], far[0], both[0])):
+    for r, piece in enumerate((own[0], far[0], near[0], both[0])):
         at = pl.ds(pl.multiple_of((group[0] ^ r) * width, width), width)
         heads_ref[:, at] = piece
     branch = jnp.dot(heads_ref[...], w_ref[...], preferred_element_type=F32)
@@ -762,25 +791,203 @@
     )
 
 
-def end_kernel(keep_ref, near_ref, far_ref, x_ref, grad_ref, gain_ref, o_ref):
-    upstream = keep_ref[...] + near_ref[...].astype(F32) + far_ref[...].astype(F32)
+def end_kernel(keep_ref, far_ref, x_ref, grad_ref, gain_ref, o_ref):
+    upstream = keep_ref[...] + far_ref[...].astype(F32)
     hat, scale = normalized(x_ref[...].astype(F32))
     grad = grad_ref[...] + normalized_back(hat, scale, upstream * gain_ref[0:1, :])
     o_ref[...] = grad.astype(BF16)
 
 
-def end(keep, near, far, x, grad, gains):
+def end(keep, far, x, grad, gains):
     total, width = x.shape
     rows = total // 2
     row = pl.BlockSpec((rows, width), lambda i: (i, 0))
     return call(
-        end_kernel, "end", (2,), [], [row] * 5 + [fixed(*gains.shape)],
-        [(shaped(BF16, total, width), row)], 20, keep, near, far, x, grad, gains,
+        end_kernel, "end", (2,), [], [row] * 4 + [fixed(*gains.shape)],
+        [(shaped(BF16, total, width), row)], 20, keep, far, x, grad, gains,
     )[0]
 
 
 def plain(x):
     return with_layout_constraint(x, Layout(tuple(range(x.ndim))))
+
+
+QKV_BLOCKS, OVER_BLOCKS, OUT_BLOCKS = 12, 2, 8
+LOW_BLOCKS = 11
+ALL_BLOCKS = QKV_BLOCKS + OVER_BLOCKS + OUT_BLOCKS + 1
+LEFT = ((0, 0), (0, 1), (1, 0))
+RIGHT = ((1, 1), (2, 0), (2, 1))
+
+
+def tiles(array):
+    return [array[:, at : at + 128] for at in range(0, array.shape[1], 128)]
+
+
+def plus(a, b):
+    return (a.astype(F32) + b.astype(F32)).astype(BF16)
+
+
+def spread_first_kernel(place, qkv_ref, out_ref, gain_ref, over_ref, far_ref, out_far,
+                        low, low_away, high, high_away):
+    lines = far_ref.shape[1]
+    spare = over_ref.shape[0] // 8
+    wide = qkv_ref.shape[1]
+    x_bit, y_bit, core = place[0], place[1], place[2]
+
+    def fill(line, low_out, high_out):
+        at = pl.ds(pl.multiple_of((2 * line + core) * lines, lines), lines)
+        near = tiles(qkv_ref[at, :])
+        far = tiles(far_ref[line, :, :wide])
+        blocks = [jnp.where(core == 0, a, b) for a, b in zip(near, far)]
+        blocks += [jnp.where(core == 0, a, b) for a, b in zip(far, near)]
+        for c in range(2):
+            rows = pl.ds(pl.multiple_of((2 * line + c) * spare, spare), spare)
+            blocks.append(jnp.concatenate(tiles(over_ref[rows, :]), axis=0))
+        blocks += [
+            plus(a, b)
+            for a, b in zip(tiles(out_ref[at, :]), tiles(out_far[line]))
+        ]
+        count = gain_ref.shape[1]
+        gain = jnp.concatenate(
+            [gain_ref[2 * line + core], jnp.zeros((lines - count, 128), BF16)], axis=0
+        )
+        blocks.append(plus(gain, far_ref[line, :, -128:]))
+        for n, block in enumerate(blocks):
+            if n < LOW_BLOCKS and low_out is not None:
+                low_out[n] = block
+            if n >= LOW_BLOCKS and high_out is not None:
+                high_out[n - LOW_BLOCKS] = block
+
+    for n in range(2):
+        fill(2 * n + x_bit, low.at[n], None)
+        fill(2 * n + 1 - x_bit, low_away.at[n], None)
+        fill(2 * y_bit + n, None, high.at[n])
+        fill(2 * (1 - y_bit) + n, None, high_away.at[n])
+
+
+def spread_first(place, qkv, out, gain, over, far, out_far):
+    lines = far.shape[1]
+    low = shaped(BF16, 2, LOW_BLOCKS, lines, 128), fixed(2, LOW_BLOCKS, lines, 128)
+    rest = ALL_BLOCKS - LOW_BLOCKS
+    high = shaped(BF16, 2, rest, lines, 128), fixed(2, rest, lines, 128)
+    arrays = (qkv, out, gain, over, far, out_far)
+    return call(
+        spread_first_kernel, "spread_first", (1,), [place], [fixed(*a.shape) for a in arrays],
+        [low, low, high, high], 2, *arrays,
+    )
+
+
+def spread_second_kernel(place, low, low_far, high, high_far, low_o, low_away, high_o, high_away):
+    for source, far, bit, near_o, away_o in (
+        (low, low_far, place[1], low_o, low_away), (high, high_far, place[0], high_o, high_away)
+    ):
+        near_o[...] = plus(source[bit], far[bit])
+        away_o[...] = plus(source[1 - bit], far[1 - bit])
+
+
+def spread_second(place, *arrays):
+    lows, highs = arrays[0].shape[1:], arrays[2].shape[1:]
+    outs = [(shaped(BF16, *s), fixed(*s)) for s in (lows, lows, highs, highs)]
+    return call(
+        spread_second_kernel, "spread_second", (1,), [place], [fixed(*a.shape) for a in arrays],
+        outs, 2, *arrays,
+    )
+
+
+def spread_third_kernel(place, low, low_far, high, high_far, near_o, away_o, over_o):
+    half = place[4]
+
+    def block(n):
+        if n < LOW_BLOCKS:
+            return plus(low[n], low_far[n])
+        return plus(high[n - LOW_BLOCKS], high_far[n - LOW_BLOCKS])
+
+    at = 0
+    for (left_t, left_c), (right_t, right_c) in zip(LEFT, RIGHT):
+        for pair in range(2):
+            left = block(left_c * 6 + pair * 3 + left_t)
+            right = block(right_c * 6 + pair * 3 + right_t)
+            near_o[at] = jnp.where(half == 0, left, right)
+            away_o[at] = jnp.where(half == 0, right, left)
+            at += 1
+    for c in range(2):
+        over_o[c] = block(QKV_BLOCKS + c)
+    first = QKV_BLOCKS + OVER_BLOCKS
+    for n in range(4):
+        left, right = block(first + n), block(first + 4 + n)
+        near_o[at] = jnp.where(half == 0, left, right)
+        away_o[at] = jnp.where(half == 0, right, left)
+        at += 1
+    near_o[at] = block(first + 8)
+    away_o[at] = block(first + 8)
+
+
+def spread_third(place, *arrays):
+    lines = arrays[0].shape[1]
+    part = shaped(BF16, 11, lines, 128), fixed(11, lines, 128)
+    over = shaped(BF16, 2, lines, 128), fixed(2, lines, 128)
+    return call(
+        spread_third_kernel, "spread_third", (1,), [place], [fixed(*a.shape) for a in arrays],
+        [part, part, over], 2, *arrays,
+    )
+
+
+def spread_fourth_kernel(place, near, far, near_o, away_o):
+    odd = place[3] == 1
+    blocks = [plus(near[n], far[n]) for n in range(11)]
+    for pair in range(2):
+        one, two, three = blocks[pair], blocks[2 + pair], blocks[4 + pair]
+        near_o[pair] = jnp.where(odd, two, one)
+        near_o[2 + pair] = jnp.where(odd, three, two)
+        away_o[pair] = jnp.where(odd, one, three)
+        near_o[4 + pair] = jnp.where(odd, blocks[8 + pair], blocks[6 + pair])
+        away_o[2 + pair] = jnp.where(odd, blocks[6 + pair], blocks[8 + pair])
+    near_o[6] = blocks[10]
+    away_o[4] = blocks[10]
+
+
+def spread_fourth(place, near, far):
+    lines = near.shape[1]
+    return call(
+        spread_fourth_kernel, "spread_fourth", (1,), [place], [fixed(*near.shape)] * 2,
+        [
+            (shaped(BF16, 7, lines, 128), fixed(7, lines, 128)),
+            (shaped(BF16, 5, lines, 128), fixed(5, lines, 128)),
+        ],
+        2, near, far,
+    )
+
+
+def spread_fifth_kernel(place, near, far, qkv_o, out_o, gain_o, gain_all):
+    for pair in range(2):
+        first, second = near[pair].astype(F32), near[2 + pair].astype(F32)
+        other = far[pair].astype(F32)
+        at = 128 * pair
+        qkv_o[:, at : at + 128] = first
+        qkv_o[:, 256 + at : 384 + at] = other
+        qkv_o[:, 512 + at : 640 + at] = second
+        out_o[:, at : at + 128] = near[4 + pair].astype(F32) + far[2 + pair].astype(F32)
+    gain_all[...] = near[6].astype(F32) + far[4].astype(F32)
+    gain_o[...] = gain_all[pl.ds(2 * place[4] + place[3], 1), :]
+
+
+def spread_fifth(place, near, far):
+    lines = near.shape[1]
+    outs = [(shaped(F32, *s), fixed(*s)) for s in ((lines, 768), (lines, 256), (1, 128))]
+    return pl.pallas_call(
+        spread_fifth_kernel,
+        grid_spec=pltpu.PrefetchScalarGridSpec(
+            num_scalar_prefetch=1,
+            grid=(1,),
+            in_specs=[fixed(*near.shape), fixed(*far.shape)],
+            out_specs=[spec for _, spec in outs],
+            scratch_shapes=[pltpu.VMEM((lines, 128), F32)],
+        ),
+        out_shape=[shape for shape, _ in outs],
+        compiler_params=params(1),
+        cost_estimate=lasting(2),
+        name="spread_fifth",
+    )(place, near, far)
 
 
 def flip(x, axis, bit):
@@ -793,8 +1000,13 @@
     pairs = []
     for z in range(half):
         low, high = cp + z, z + half
-        pairs += [(low, high), (high, low), (z, z), (cp + high, cp + high)]
+        pairs += [(low, high), (high, low)]
     return lax.ppermute(plain(x), ("core", "cp"), pairs)
+
+
+def settled(x, moved):
+    stays = (lax.axis_index("core") == 1) == (lax.axis_index("cp") >= lax.axis_size("cp") // 2)
+    return jnp.where(stays, x, moved)
 
 
 def ordered(first, mine, other, axis):
@@ -859,7 +1071,7 @@
     row_len = blocks * span
     own = 2 * span
     parity = z & 1
-    group = 2 * parity + core
+    group = parity + 2 * core
     part = width // cp_count
     hidden_part = up_weight.shape[1] // 2
     lines_each = width // xy_count
@@ -871,9 +1083,19 @@
     gain_rows = lax.dynamic_update_slice(gain_rows, norm_gains[None], (0, 0))
     w = jnp.concatenate([qkv_weight, gain_rows])
     w_far = flip(w, "cp", 2)
-    x = swap(after(tokens, w_far)[0])
-
-    up_weight, down_weight, out_weight = all_after((up_weight, down_weight, out_weight), w_far)
+
+    x = settled(tokens[0], swap(after(tokens, w_far)[0]))
+    w, w_far = jnp.where(z & 2 == 0, w, w_far), jnp.where(z & 2 == 0, w_far, w)
+    near = [w[:, n * part : (n + 1) * part] for n in range(3)]
+    near += [w_far[:, n * part : (n + 1) * part] for n in range(3)]
+    even = parity == 0
+    sent = jnp.concatenate([near[1], near[4]], axis=1)
+    gain_near = jnp.stack([w[lines, :128], w_far[lines, :128]])
+    sent = lax.dynamic_update_slice(sent, gain_near, (lines, 0))
+    far = flip(sent, "cp", 1)
+    up_weight, down_weight, out_weight = all_after((up_weight, down_weight, out_weight), far)
+    out_far = flip(out_weight, "cp", 2)
+
 
     def half_of(which):
         up = lax.dynamic_slice_in_dim(up_weight, which * hidden_part, hidden_part, 1)
@@ -887,32 +1109,22 @@
             [jnp.where(z & 2 == 0, mine, other), jnp.where(z & 2 == 0, other, mine)], axis=1
         )
 
-    out_far = flip(out_weight, "cp", 2)
-    w, w_far = jnp.where(z & 2 == 0, w, w_far), jnp.where(z & 2 == 0, w_far, w)
-    near = [w[:, n * part : (n + 1) * part] for n in range(3)]
-    near += [w_far[:, n * part : (n + 1) * part] for n in range(3)]
-    even = parity == 0
-    sent = jnp.concatenate(
-        [jnp.where(even, near[a], near[b]) for a, b in ((2, 1), (3, 2), (4, 3))], axis=1
-    )
-    gain_near = jnp.stack([w[lines, :128], w_far[lines, :128]])
-    sent = lax.dynamic_update_slice(sent, gain_near, (lines, 0))
-    far = flip(sent, "cp", 1)
     gain_far = far[lines : lines + 2, :128]
     gain_near, gain_far = (
         jnp.where(even, gain_near, gain_far), jnp.where(even, gain_far, gain_near)
     )
     gain_rows = jnp.stack([gain_near[0], gain_far[0], gain_near[1], gain_far[1]])
-    far = [far[:lines, n * part : (n + 1) * part] for n in range(3)]
+    far = [far[:lines, n * part : (n + 1) * part] for n in range(2)]
     near = [block[:lines] for block in near]
-    first_group = jnp.concatenate(
-        [jnp.where(even, a, b) for a, b in ((near[0], far[0]), (far[0], far[1]), (near[5], near[4]))],
-        axis=1,
-    )
-    second_group = jnp.concatenate(
-        [jnp.where(even, a, b) for a, b in ((near[1], near[0]), (far[1], far[2]), (far[2], near[5]))],
-        axis=1,
-    )
+
+    def by_pairs(*choices):
+        picked = [jnp.where(even, a, b) for a, b in choices]
+        return jnp.concatenate(
+            [block[:, at : at + 128] for at in range(0, part, 128) for block in picked], axis=1
+        )
+
+    first_group = by_pairs((near[0], far[0]), (far[0], near[2]), (near[5], near[3]))
+    second_group = by_pairs((near[2], near[0]), (near[3], far[1]), (far[1], near[5]))
     gain_block = jnp.zeros((16, 3 * part), BF16)
     gain_block = lax.dynamic_update_slice(gain_block, gain_rows, (0, 0))
     mine = jnp.concatenate([jnp.where(core == 0, first_group, second_group), gain_block])
@@ -971,8 +1183,10 @@
     gains = low[:, :, :, lines : lines + cp_count, :128]
     gains = gains.reshape(4, width).astype(F32)
 
+    sooner, later = jnp.array([0, 1, 4, 5], jnp.int32), jnp.array([2, 3, 6, 7], jnp.int32)
+    early = project(x, x_core, gains, qkv, cosine, sine, block_of[sooner], sooner, [])
+    x_chip, up_far, *early = lax.optimization_barrier((x_chip, up_far, *early))
     x_both = flip(x_chip, "core", 1)
-    x_chip, up_far = lax.optimization_barrier((x_chip, up_far))
     up_lines, up_far, down_lines, out_w, out_far = all_after(
         (up_lines, up_far, ffn[1], out_w, out_far), x_chip, qkv
     )
@@ -1000,57 +1214,56 @@
         high = ordered(xy & 1 == 0, high, high_far, 1).reshape(low.shape)
         return jnp.stack([low, high], axis=1).reshape(width, -1)
 
-    q, k, v, normed = project([x, x_chip, x_core, x_both], gains, qkv, cosine, sine, slot_of)
-    up_lines, up_far, down_lines, down_far, out_w, out_far = all_after(
-        (up_lines, up_far, down_lines, down_far, out_w, out_far), q
-    )
-    up_pair = halves(widened(z, up_lines, up_far))
-    up_far = send_lines(*up_pair)
+    q, k, v, normed = project(
+        x_chip, x_both, gains, qkv, cosine, sine, block_of[later], later, early
+    )
+    up_lines, up_far, out_w, out_far = all_after((up_lines, up_far, out_w, out_far), q)
+    up_lines = widened(z, up_lines, up_far)
+    up_full = lax.all_gather(up_lines, "xy", axis=0, tiled=True)
+    out_w = ordered(xy & 1 == 0, out_w, out_far, 0)
+    out_far = flip(out_w, "xy", 2)
+    q = after(q, up_lines, out_w)
+    first = attend(0, q, k, v, pcol, prow, srow, bounds, slot_of, tile)
+    down_lines, down_far, out_w, out_far = all_after(
+        (down_lines, down_far, out_w, out_far), first[0]
+    )
+    out_w = ordered(xy & 2 == 0, out_w, out_far, 0)
+    out_far = flip(out_w, "core", 1)
     down_lines = paired(down_lines, down_far)
     down_far = flip(down_lines, "cp", 1)
-    out_w = ordered(xy & 1 == 0, out_w, out_far, 0)
-    out_far = flip(out_w, "xy", 2)
-    q = after(q, *up_pair, down_lines, out_w)
-    first = attend(0, q, k, v, pcol, prow, srow, bounds, slot_of, tile)
-    up_pair, up_far = all_after(up_pair, first[0]), all_after(up_far, first[0])
-    down_lines, down_far, out_w, out_far = all_after(
-        (down_lines, down_far, out_w, out_far), first[0]
-    )
-    up_pair = join_lines(*up_pair, *up_far)
-    up_far = send_more(*up_pair)
-    out_w = ordered(xy & 2 == 0, out_w, out_far, 0)
-    out_far = flip(out_w, "core", 1)
-    down_pair = halves(widened(z, down_lines, down_far))
-    down_far = send_lines(*all_after(down_pair, *up_pair))
-    q = after(q, first[0], *down_pair, *up_pair, out_w)
+    q = after(q, first[0], down_lines, out_w)
     second = attend(1, q, k, v, pcol, prow, srow, bounds, slot_of, tile)
     attended, local, lse = zip(first, second)
     local = jnp.concatenate(local, axis=2)
-    out_w, out_far = all_after((out_w, out_far), local)
+    out_w, out_far, down_lines, down_far = all_after((out_w, out_far, down_lines, down_far), local)
     out_w = placed(core == 0, out_w, out_far, 1).reshape(width, width)
+    down_pair = halves(widened(z, down_lines, down_far))
+    down_far = send_lines(*down_pair)
     heads, branch_hat, branch_scale, hidden, mid = mix(
         group_at, local[:2], flip(local[4:6], "core", 1), flip(local[2:4], "cp", 1),
         flip_both(local[6:]), out_w, x, gains,
     )
 
-    dy = swap(after(cotangent.reshape(own, width), mid))
+    cotangent = cotangent.reshape(own, width)
+    dy_moved = swap(after(cotangent, mid))
 
     ffn_in = jnp.concatenate([mid, flip(mid, "core", 1)])
     down_pair, down_far = all_after(down_pair, mid), all_after(down_far, mid)
     down_pair = join_lines(*down_pair, *down_far)
     down_far = send_more(*down_pair)
-    up_full = join_all(*up_pair, *all_after(up_far, *down_pair))
+    ffn_in = after(ffn_in, *down_pair)
     act, slope = gelu_and_slope(dot(ffn_in, up_full, (1, 0)))
     down_full = join_all(*down_pair, *all_after(down_far, act))
     sent = flip(dot(act[own:], down_full, (1, 1)).astype(BF16), "core", 1)
     terms = dot(act[:own], down_full, (1, 1))
+    dy = settled(cotangent, dy_moved)
     mixed, grad_down, gain_four = finish(terms, sent, hidden, dy, gains)
     grad_down = jnp.concatenate([grad_down, flip(grad_down, "core", 1)])
 
     x_bit, y_bit = xy & 1, xy >> 1
 
     def cut_first(grads):
-        grads = [g.reshape(2, 2, 2, lines, -1) for g in grads]
+        grads = [g.reshape(2, 2, 2, -1, g.shape[-1]) for g in grads]
         low = [g[:, :, 0] for g in grads]
         high = [g[:, :, 1] for g in grads]
 
@@ -1099,6 +1312,10 @@
     grad_up = grad_up.astype(BF16)
     sent = flip(dot(grad_up[own:], up_full, (1, 1)).astype(BF16), "core", 1)
     up_local = plain(dot(ffn_in, grad_up, (0, 0)).astype(BF16))
+    spare = lines // 4
+    down_local = down_local.reshape(2 * xy_count, lines, -1)
+    over_local = down_local[:, lines - spare :].reshape(2 * xy_count * spare, -1)
+    down_local = down_local[:, : lines - spare].reshape(2 * xy_count * (lines - spare), -1)
     grad_near, grad_away = cut_first((up_local, down_local))
     grad_far = send_first(grad_away)
     terms = dot(after(grad_up, *grad_away)[:own], up_full, (1, 1))
@@ -1107,133 +1324,106 @@
     )
 
     grad_local = [
-        grad_heads[0], flip(grad_heads[2], "cp", 1), flip(grad_heads[1], "core", 1),
+        grad_heads[0], flip(grad_heads[1], "cp", 1), flip(grad_heads[2], "core", 1),
         flip_both(grad_heads[3]),
     ]
     out_local = dot(after(heads, grad_heads), grad_branch, (0, 0)).astype(BF16)
-    out_local = out_local.reshape(xy_count, 2, lines, width)
-    out_away = pick(out_local, 1 - core, 1)
     grad_local = plain(jnp.concatenate(grad_local))
-    out_away, mixed = all_after((out_away, mixed), grad_local)
-    out_far = flip(out_away, "core", 1)
-    mixed = swap(mixed).reshape(tokens.shape)
-    grad_local = after(grad_local, out_away)
+    out_away = pick(out_local.reshape(xy_count, 2, lines, width), 1 - core, 1)
+    out_away, over_local, mixed, grad_local = lax.optimization_barrier(
+        (out_away, over_local, mixed, grad_local)
+    )
+    over_near, over_away = split_columns(over_local, hidden_part)
+    over_far = flip(over_away, "cp", 1)
+    mixed_moved = swap(mixed)
+    grad_local = after(grad_local, over_away)
+
+    def back_to_tokens(grads):
+        two = 2 * span
+        rows = grads.reshape(4 * span, 3 * part)
+        send = dot(rows[two:], qkv, (1, 1)).astype(BF16)
+        sent = flip(send, "core", 1)
+        rows = after(rows, send)
+        own_sums = dot(rows[:two], qkv, (1, 1)) + sent.astype(F32)
+        far_away = own_sums[span:].astype(BF16)
+        return send, far_away, flip(far_away, "cp", 1), own_sums[:span]
 
     tables = (pcol, prow, srow, cosine, sine, bounds, slot_of, tile)
-    first = attend_back(0, q, k, v, grad_local, attended[0], lse[0], *tables)
-    grad_far = all_after(grad_far, first)
-    grad_near, grad_away = cut_second(grad_near, grad_far)
+    attended, lse = jnp.concatenate(attended, axis=1), jnp.concatenate(lse, axis=0)
+    first, unfinished = attend_back(0, q, k, v, grad_local, attended, lse, *tables, [])
+    first, mixed_moved, over_far, *grad_far = lax.optimization_barrier(
+        (first, mixed_moved, over_far, *grad_far)
+    )
+    over_near, over_away = cut_fourth(over_near, over_far)
+    over_far = flip(over_away, "cp", 2)
+    _, far_away, far_back, kept = back_to_tokens(after(first, over_away))
+    grad_near, grad_away = cut_second(grad_near, all_after(grad_far, far_away))
     grad_far = send_second(grad_away)
-    out_near, out_away = split_columns(
-        total(pick(out_local, core, 1), after(out_far, first)).reshape(-1, width), part
-    )
-    out_far = flip(out_away, "cp", 1)
+    out_far = flip(after(out_away, far_away), "core", 1)
     second = attend_back(
-        1, q, k, v, after(grad_local, first, *grad_away, out_away, mixed), attended[1], lse[1],
-        *tables,
-    )
-    first, second, grad_far, out_far = lax.optimization_barrier((first, second, grad_far, out_far))
-
-    def rows_of(low, high):
-        return jnp.concatenate(
-            [half[n, low:high].reshape(-1, 128) for n in range(3) for half in (first, second)],
-            axis=1,
-        )
-
-    half_rows = row_len // 2
-    grad_rows = rows_of(0, blocks)
-    send = dot(grad_rows[half_rows:], qkv, (1, 1)).astype(BF16)
-    sent = flip(send, "core", 1)
-    grad_near, grad_away = cut_third(grad_near, all_after(grad_far, send))
-    grad_far = flip(grad_away, "cp", 1)
-    out_near, out_away = cut_fourth(out_near, after(out_far, send))
-    out_far = flip(out_away, "cp", 2)
-    grad_rows = after(grad_rows, send, grad_away, out_away)
-    qkv_local = dot(normed.reshape(row_len, width), grad_rows, (0, 0)).astype(BF16)
+        1, q, k, v, after(grad_local, first, *grad_away, over_away, kept), attended, lse, *tables,
+        [unfinished],
+    )[0]
+    second, over_far, out_far, *grad_far = lax.optimization_barrier(
+        (second, over_far, out_far, *grad_far)
+    )
+
+    ended = end(kept, after(far_back, second), x[0], grad_hidden[:span], gains)
+    moved = swap(ended)
+    second = after(second, ended)
+    send, far_away, far, kept = back_to_tokens(second)
+    qkv_local = sum(
+        dot(normed[4 * h : 4 * h + 4].reshape(4 * span, width), g.reshape(4 * span, -1), (0, 0))
+        for h, g in enumerate((first, after(second, send)))
+    ).astype(BF16)
     gain_one = jnp.sum(qkv_local.astype(F32) * qkv.astype(F32), axis=1) / gains[0]
     gain_sum = jnp.concatenate([gain_one[None], gain_two, gain_three, gain_four])
     gain_sum = gain_sum.reshape(2 * xy_count, cp_count, 128).astype(BF16)
-    gain_sum = jnp.pad(gain_sum, ((0, 0), (0, lines - cp_count), (0, 0)))
-    rest = plain(jnp.concatenate([qkv_local, gain_sum.reshape(width, 128)], axis=1))
-    rest = rest.reshape(xy_count, 2, lines, -1)
-    rest_near, rest_away = pick(rest, core, 1), pick(rest, 1 - core, 1)
-    rest_far = flip(rest_away, "core", 1)
-    grad_rows = after(grad_rows, rest_away)
-    far_away = total(dot(grad_rows[own:half_rows], qkv, (1, 1)), sent[own:])
-    far = flip(far_away, "cp", 1)
-    keep = dot(after(grad_rows, far_away)[:own], qkv, (1, 1))
-
-    out_sum = total(out_near, out_far).reshape(xy_count, lines, part)
-    rest_far = after(rest_far, far_away)
-    three = 3 * part
-    summed = total(rest_near[..., three:], rest_far[..., three:])
-    rest_near, rest_far = rest_near[..., :three], rest_far[..., :three]
-    rest = jnp.concatenate(
+    place = jnp.stack([x_bit, y_bit, core, parity, z >> 1]).astype(jnp.int32)
+    locals_ = (qkv_local, out_local, gain_sum)
+    rest_away = jnp.concatenate(
         [
-            jnp.where(core == 0, rest_near, rest_far), jnp.where(core == 0, rest_far, rest_near),
-            out_sum, summed,
+            pick(qkv_local.reshape(xy_count, 2, lines, 3 * part), 1 - core, 1),
+            jnp.pad(
+                pick(gain_sum.reshape(xy_count, 2, cp_count, 128), 1 - core, 1),
+                ((0, 0), (0, lines - cp_count), (0, 0)),
+            ),
         ],
         axis=2,
     )
-    rest = plain(rest).reshape(2, 2, lines, -1)
-    cut = rest.shape[3] // 256 * 128
-    low, high = rest[..., :cut], rest[..., cut:]
-    rest_near = pick(low, x_bit, 1), pick(high, y_bit, 0)
-    rest_away = pick(low, 1 - x_bit, 1), pick(high, 1 - y_bit, 0)
-    rest_far = send_first(rest_away)
-    grad_near, grad_away = cut_fourth(grad_near, after(grad_far, *rest_away))
+    rest_far = flip(rest_away, "core", 1)
+
+    over = total(over_near, over_far)
+    rest_far, over = all_after((rest_far, over), kept)
+    low, low_away, high, high_away = spread_first(place, *locals_, over, rest_far, out_far)
+    rest_far = flip(low_away, "xy", 1), flip(high_away, "xy", 2)
+    grad_near, grad_away = cut_third(grad_near, all_after(grad_far, low_away))
+    grad_far = flip(grad_away, "cp", 1)
+    ended_last = end(kept, after(far, moved), x[1], grad_hidden[span:], gains)
+    moved_last = swap(ended_last)
+    rest_far, grad_far = all_after(rest_far, ended_last), after(grad_far, ended_last)
+    grad_near, grad_away = cut_fourth(grad_near, grad_far)
     grad_far = flip(grad_away, "cp", 2)
-    far = after(far, grad_away)
-    tokens_grad = end(keep, sent[:own], far, x.reshape(own, width), grad_hidden, gains)
-    ended = tokens_grad
-    tokens_grad = swap(tokens_grad)
-
-    rest_far = all_after(rest_far, far)
-    rest_near, rest_away = cut_second(rest_near, rest_far)
-    rest_far = send_second(rest_away)
-    rest = jnp.concatenate([total(a, b) for a, b in zip(rest_near, rest_far)], axis=1)
-    qkv_sum = rest[:, : 2 * three].reshape(lines, 2, 3, part).transpose(2, 1, 0, 3)
-    out_grad = rest[:, 2 * three : 2 * three + part].astype(F32)
-    gain_sum = rest[:, 2 * three + part :]
-    right = z >= 2
-    even = parity == 0
-    send_at = (
-        jnp.where(right, 0, jnp.where(even, 2, 1)), jnp.where(right, jnp.where(even, 1, 0), 2)
-    )
-    keep_at = (
-        jnp.where(right, jnp.where(even, 2, 1), 0), jnp.where(right, 2, jnp.where(even, 1, 0))
-    )
-
-    def flat(qkv_blocks, gain_block):
-        return jnp.concatenate([*qkv_blocks.reshape(-1, lines, part), gain_block], axis=1)
-
-    rest = flat(jnp.stack([pick(qkv_sum, at, 0) for at in keep_at]), gain_sum)
-    rest_away = flat(jnp.stack([pick(qkv_sum, at, 0) for at in send_at]), gain_sum)
-    rest = total(rest, flip(rest_away, "cp", 2))
-    blocks_of = [rest[:, n * part : (n + 1) * part] for n in range(4)]
-    gain_sum = rest[:, 4 * part :]
-    slots = jnp.stack([jnp.stack(blocks_of[:2]), jnp.stack(blocks_of[2:4])])
-    rest_away = flat(pick(slots, jnp.where(z == 0, 1, 0), 0), gain_sum)
-    rest_far = flip(rest_away, "cp", 1)
-    sent = [rest_far[:, :part], rest_far[:, part : 2 * part]]
-
-    def choice(*four):
-        return jnp.where(
-            z == 0, four[0], jnp.where(z == 1, four[1], jnp.where(z == 2, four[2], four[3]))
-        )
-
-    qkv_grad = jnp.concatenate(
-        [
-            choice(slots[0, 0], slots[0, 1], sent[0], sent[1]),
-            choice(slots[0, 1], sent[0], sent[1], slots[1, 0]),
-            choice(sent[0], sent[1], slots[0, 0], slots[1, 1]),
-        ],
-        axis=1,
-    ).astype(F32)
-    gains_grad = pick(gain_sum.astype(F32) + rest_far[:, 2 * part :].astype(F32), z, 0)
-    tokens_grad = after(tokens_grad, rest_away).astype(F32).reshape(tokens.shape)
-
-    both = plain(total(grad_near, after(grad_far, ended))).reshape(2, 2, lines, hidden_part)
+    rest_far = all_after(rest_far, grad_away)
+    low, low_away, high, high_away = spread_second(place, low, rest_far[0], high, rest_far[1])
+    rest_far = flip(low_away, "xy", 2), flip(high_away, "xy", 1)
+    rest, rest_away, over = spread_third(place, low, rest_far[0], high, rest_far[1])
+    gather_away = rest_away
+    rest, rest_away = spread_fourth(place, rest, flip(rest_away, "cp", 2))
+    moved_last = after(moved_last, rest_away)
+    qkv_grad, out_grad, gains_grad = spread_fifth(place, rest, flip(rest_away, "cp", 1))
+    gains_grad = gains_grad.reshape(-1)
+    tokens_grad = jnp.stack([settled(ended, moved), settled(ended_last, moved_last)])
+    tokens_grad = tokens_grad.astype(F32).reshape(tokens.shape)
+    mixed = settled(after(mixed, gather_away), mixed_moved).reshape(tokens.shape)
+
+    both = total(grad_near, after(grad_far, gather_away))
+    both = plain(both).reshape(2, 2 * lines - spare, hidden_part)
+    over = [
+        jnp.concatenate([block[n * spare : (n + 1) * spare] for n in range(4)], axis=1)
+        for block in over
+    ]
+    both = jnp.concatenate([both, jnp.stack(over)], axis=1).reshape(2, 2, lines, hidden_part)
     mine, other = pick(both, core, 0), flip(pick(both, 1 - core, 0), "core", 1)
     up_grad = ordered(core == 0, mine[0], other[0], 1).astype(F32)
     down_grad = ordered(core == 0, mine[1], other[1], 1).T.astype(F32)

time: 508 us -> 495 us (0.974)
  Pallas kernels: 116 us -> 86.1 us
  other arithmetic: 50.8 us -> 75.7 us
  waiting for transfers between devices: 162 us -> 145 us
  between operations: 2.62 us -> 16.3 us
  starting transfers between devices: 75.4 us -> 64.1 us
  local copies, waits for them, and re-layouts: 38.6 us -> 49.4 us
    pallas_call x5 -> x9, Pallas kernels: 38.2 us -> 16.4 us  [call(): pl.pallas_call(kernel, grid_spec=pltpu.PrefetchScalarGridSpec(num_scalar_...]
    ppermute x56 -> x54, waiting for transfers between devices: 154 us -> 136 us  [flip(): lax.ppermute(plain(x), axis, [(i, i ^ bit) for i in range(lax.axis_size(a...]
    pallas_call x2 -> x1, Pallas kernels: 30.8 us -> 13.4 us  [attend(): pl.pallas_call(functools.partial(attend_kernel, tile), grid_spec=grid_spe...]
    pallas_call x0 -> x1, other arithmetic: none -> 15.1 us  [attend(): pl.pallas_call(functools.partial(attend_kernel, tile), grid_spec=grid_spe...]
    unnamed x107 -> x210, local copies, waits for them, and re-layouts: 17 us -> 30.2 us
    pallas_call x2 -> x5, Pallas kernels: 46.8 us -> 56.2 us  [the longest x2 43 us: attend_back(): pl.pallas_call(functools.partial(attend_back_kernel, tile, first, steps),...]
    ppermute x4 -> x5, starting transfers between devices: 14.2 us -> 7.19 us  [swap(): return lax.ppermute(plain(x), ('core', 'cp'), pairs)]
    ppermute x56 -> x54, starting transfers between devices: 59.6 us -> 55.4 us  [flip(): lax.ppermute(plain(x), axis, [(i, i ^ bit) for i in range(lax.axis_size(a...]
  transfers between devices with their start and end apart: 62 -> 62, of which waited for: 27 -> 24; matrix products, arithmetic and copies ran while one was open for 20% -> 23% of each run, Pallas kernels for 22% -> 16%
where the time goes in v4:
time: 495 us; the launch traced here: 489 us
  waiting for transfers between devices  145 us (29%)
  Pallas kernels  86.1 us (17%)
  other arithmetic  75.7 us (15%)
  starting transfers between devices  64.1 us (13%)
  matrix products  53 us (11%)
  local copies, waits for them, and re-layouts  49.4 us (10%)
  between operations  16.3 us (3%)
    ppermute x54, waiting for transfers between devices, flip(): lax.ppermute(plain(x), axis, [(i, i ^ bit) for i in range(lax.axis_size(a...  136 us
    ppermute x54, starting transfers between devices, flip(): lax.ppermute(plain(x), axis, [(i, i ^ bit) for i in range(lax.axis_size(a...  55.4 us
    dot_general x15, matrix products, dot(): lax.dot_general(a, b, ((dims[:1], dims[1:]), ((), ())), preferred_element...  53 us
    pallas_call x2, Pallas kernels, attend_back(): pl.pallas_call(functools.partial(attend_back_kernel, tile, first, steps),...  43 us
    unnamed x210, local copies, waits for them, and re-layouts  30.2 us
    pallas_call x9, Pallas kernels, call(): pl.pallas_call(kernel, grid_spec=pltpu.PrefetchScalarGridSpec(num_scalar_...  16.4 us
    pallas_call x1, other arithmetic, attend(): pl.pallas_call(functools.partial(attend_kernel, tile), grid_spec=grid_spe...  15.1 us
    convert_element_type x8, other arithmetic, total(): return (a.astype(F32) + b.astype(F32)).astype(BF16)  14 us
  transfers between devices with their start and end apart: 62, of which 24 were waited for; matrix products, arithmetic and copies ran while one was open for 23% of the time, Pallas kernels for 16%

profile of v4, /device:TPU:0, one launch (start us, length us, event | category | flops | bytes accessed | tf_op | source)
XLA Modules:
  0.0 489.3 jit_solution(18087938002990868074)
XLA Ops:
  8.2 4.1 collective-permute-start
  14.4 8.1 %collective-permute-done = bf16[144,768]{1,0:T(8,128)(2,1)S(1)} collective-permute-done((bf16[144,768]{1,0:T(8,128)(2,1)S(1)}, bf16[144,768]{1,0:T(8,128)(2,1)S(1)}, u32[]{:S(2)}, u32[]{:S(2)}) %collective-permute-start) | collective-permute-done | bytes 221216 | tf_op jit(solution)/shard_map/ppermute | solution.py:994
  29.3 5.1 %collective-permute-done.4 = bf16[144,512]{1,0:T(8,128)(2,1)} collective-permute-done((bf16[144,512]{1,0:T(8,128)(2,1)}, bf16[144,512]{1,0:T(8,128)(2,1)}, u32[]{:S(2)}, u32[]{:S(2)}) %collective-permute-start.4) | collective-permute-done | bytes 147488 | tf_op jit(solution)/shard_map/ppermute | solution.py:994
  37.5 6.9 %collective-permute-start.9 = (bf16[144,768]{1,0:T(8,128)(2,1)S(1)}, bf16[144,768]{1,0:T(8,128)(2,1)S(1)}, u32[]{:S(2)}, u32[]{:S(2)}) collective-permute-start(bf16[144,768]{1,0:T(8,128)(2,1)S(1)} %pad_maximum_fusion.24), channel_id=1, source_target_pairs={{0,4},{4,0},{1,5},{5,1},{2,6},{6,2},{3,7},{7,3},{8,12},{12,8},{9,1... | collective-permute-start | bytes 663560 | tf_op jit(solution)/shard_map/ppermute | solution.py:994
  44.7 5.1 %collective-permute-start.6 = (bf16[128,256]{1,0:T(8,128)(2,1)S(1)}, bf16[128,256]{1,0:T(8,128)(2,1)}, u32[]{:S(2)}, u32[]{:S(2)}) collective-permute-start(bf16[128,256]{1,0:T(8,128)(2,1)S(1)} %copy-done.90), channel_id=1, source_target_pairs={{0,2},{1,3},{2,0},{3,1},{4,6},{5,7},{6,4},{7,5},{8,10},{9,11},{10,... | collective-permute-start | bytes 196616 | tf_op jit(solution)/shard_map/ppermute | solution.py:994
  53.8 3.3 collective-permute-done.10
  62.0 6.3 %collective-permute-done.11 = bf16[2,2,144,384]{3,2,1,0:T(8,128)(2,1)S(1)} collective-permute-done((bf16[2,2,144,384]{3,2,1,0:T(8,128)(2,1)S(1)}, bf16[2,2,144,384]{3,2,1,0:T(8,128)(2,1)S(1)}, u32[]{:S(2)}, u32[]{:S(2)}) %collective-permute-start.11) | collective-permute-done | bytes 442400 | tf_op jit(solution)/shard_map/ppermute | solution.py:994
  75.5 5.8 %project.2 = (bf16[2048,256]{1,0:T(8,128)(2,1)S(1)}, bf16[2048,256]{1,0:T(8,128)(2,1)S(1)}, bf16[2048,256]{1,0:T(8,128)(2,1)S(1)}, bf16[8,256,1024]{2,1,0:T(8,128)(2,1)S(1)}) custom-call(s32[4]{0:T(128)S(1)} %gather_fusion.1, s32[4]{0:T(128)S(1)} %copy-done.53, bf16[2,256,1024]{2,1,0:T(8,128)(2,1)S(1)} %bitcast_select_fusion.near.x_ref, ...), custom_call_target="tpu_custom_call" | custom-call | flops 70000000 | bytes 1024 | tf_op jit(solution)/shard_map/project/pallas_call | solution.py:660
  86.3 4.2 collective-permute-done.7
  90.5 2.3 collective-permute-done.3.near
  102.2 2.2 copy-done.34
  104.4 6.1 %project.3 = (bf16[2048,256]{1,0:T(8,128)(2,1)S(1)}, bf16[2048,256]{1,0:T(8,128)(2,1)S(1)}, bf16[2048,256]{1,0:T(8,128)(2,1)S(1)}, bf16[8,256,1024]{2,1,0:T(8,128)(2,1)S(1)}) custom-call(s32[4]{0:T(128)S(1)} %gather_fusion, s32[4]{0:T(128)S(1)} %copy-done.54, ...), custom_call_target="tpu_custom_call", output_to_operand_aliasing={{0}: (8, {}), {1}: (9, {}), {2}: (10, {}), {3}: (11, {})} | custom-call | flops 70000000 | bytes 1024 | tf_op jit(solution)/shard_map/project/pallas_call | solution.py:660
  121.1 13.4 %attend.2 = (f32[2048,128]{1,0:T(8,128)S(1)}, bf16[8,256,128]{2,1,0:T(8,128)(2,1)S(1)}, f32[1,2,2048]{2,1,0:T(2,128)S(1)}) custom-call(s32[4,4]{1,0:T(4,128)S(1)} %pad_add_fusion.bounds, s32[8]{0:T(128)S(1)} %convert_add_fusion.6.slot_of, bf16[2048,256]{1,0:T(8,128)(2,1)S(1)} %copy-done.3, bf16[2048,256]{1,0:T(8,128)(2,1)S(1)} %copy-done.8, ...), custom_call_target="tpu_custom_call" | custom-call | flops 140000000 | bytes 1024 | tf_op jit(solution)/shard_map/attend/pallas_call | solution.py:427
  140.6 15.1 %attend.3 = (f32[2,2,2048]{2,1,0:T(2,128)S(1)}, bf16[8,256,128]{2,1,0:T(8,128)(2,1)S(1)}, f32[2048,128]{1,0:T(8,128)}) fusion(f32[2,2,2048]{2,1,0:T(2,128)S(1)} %constant_dynamic-update-slice_fusion.19, s32[4,4]{1,0:T(4,128)S(1)} %pad_add_fusion.bounds, s32[8]{0:T(128)S(1)} %convert_add_fusion.6.slot_of, bf16[2048,256]{1,0:T(8,128)(2,1)} %copy-done.2, ...), kind=kCustom, calls=%fused_computation.257 | custom fusion | flops 140000000 | bytes 5802496 | tf_op jit(solution)/shard_map/attend/pallas_call | solution.py:427
  163.1 5.2 %collective-permute-done.21.far = bf16[2,256,256]{2,1,0:T(8,128)(2,1)S(1)} collective-permute-done((bf16[2,256,256]{2,1,0:T(8,128)(2,1)S(1)}, bf16[2,256,256]{2,1,0:T(8,128)(2,1)S(1)}, u32[]{:S(2)}, u32[]{:S(2)}) %collective-permute-start.21) | collective-permute-done | bytes 262176 | tf_op jit(solution)/shard_map/ppermute | solution.py:994
  168.3 4.7 collective-permute-done.22.both
  173.1 2.9 mix.1
  187.9 11.8 %add_convert_fusion = (bf16[1024,2048]{1,0:T(8,128)(2,1)}, bf16[1024,2048]{1,0:T(8,128)(2,1)S(1)}) fusion(bf16[1024,1024]{1,0:T(8,128)(2,1)} %pad_maximum_fusion.2, bf16[1024,2048]{1,0:T(8,128)(2,1)} %all-gather.2.cloned.1.call-done), kind=kOutput, calls=%fused_computation.3 | convolution fusion | flops 4330618880 | bytes 14680064 | tf_op jit(solution)/shard_map/dot_general | solution.py:1042
  199.7 8.5 %collective-permute-done.28 = bf16[2,128,2048]{2,1,0:T(8,128)(2,1)} collective-permute-done((bf16[2,128,2048]{2,1,0:T(8,128)(2,1)}, bf16[2,128,2048]{2,1,0:T(8,128)(2,1)}, u32[]{:S(2)}, u32[]{:S(2)}) %collective-permute-start.28) | collective-permute-done | bytes 1048608 | tf_op jit(solution)/shard_map/ppermute | solution.py:994
  208.2 2.6 collective-permute-done.29
  215.1 2.4 fusion.13
  219.0 2.4 fusion.7.terms_ref
  221.4 2.7 finish.1
  228.8 7.5 %convolution_convert_fusion.1 = bf16[1024,2048]{1,0:T(8,128)(2,1)S(1)} fusion(bf16[1024,1024]{1,0:T(8,128)(2,1)S(1)} %constant_dynamic-update-slice_fusion.14, bf16[1024,2048]{1,0:T(8,128)(2,1)} %copy-done.94), kind=kOutput, calls=%fused_computation.10 | convolution fusion | flops 4297064448 | bytes 10485760 | tf_op jit(solution)/shard_map/dot_general | solution.py:1042
  239.8 4.7 multiply_convert_fusion
  244.5 5.1 %convolution_convert_fusion = bf16[1024,2048]{1,0:T(8,128)(2,1)S(1)} fusion(bf16[1024,1024]{1,0:T(8,128)(2,1)S(1)} %copy-done.78, bf16[1024,2048]{1,0:T(8,128)(2,1)S(1)} %multiply_convert_fusion), kind=kOutput, calls=%fused_computation.9 | convolution fusion | flops 4297064448 | bytes 10485760 | tf_op jit(solution)/shard_map/dot_general | solution.py:1042
  253.9 2.4 fusion.16
  264.0 2.4 fusion.3.terms_ref
  266.4 4.3 turn.1
  275.6 3.9 collective-permute-done.36
  279.5 5.7 %collective-permute-done.34 = bf16[2,256,256]{2,1,0:T(8,128)(2,1)S(1)} collective-permute-done((bf16[2,256,256]{2,1,0:T(8,128)(2,1)S(1)}, bf16[2,256,256]{2,1,0:T(8,128)(2,1)S(1)}, u32[]{:S(2)}, u32[]{:S(2)}) %collective-permute-start.34) | collective-permute-done | bytes 262176 | tf_op jit(solution)/shard_map/ppermute | solution.py:994
  293.0 28.1 %attend_back.2 = (bf16[4,256,768]{2,1,0:T(8,128)(2,1)S(1)}, f32[2,128,1024]{2,1,0:T(8,128)S(1)}) custom-call(s32[4,4]{1,0:T(4,128)S(1)} %pad_add_fusion.bounds, s32[8]{0:T(128)S(1)} %convert_add_fusion.6.slot_of, bf16[2048,256]{1,0:T(8,128)(2,1)S(1)} %copy-done.4, bf16[2048,256]{1,0:T(8,128)(2,1)S(1)} %copy-done.9, bf16[2048,256]{1,0:T(8,128)(2,1)S(1)} %copy-done.14, ...), custom_call_target="tpu_custom_call" | custom-call | flops 230000000 | bytes 1024 | tf_op jit(solution)/shard_map/attend_back/pallas_call | solution.py:573
  325.7 2.3 collective-permute-done.41
  330.3 2.6 fusion.20
  334.2 2.6 fusion.21
  338.8 2.6 collective-permute-start.42
  342.2 3.6 fusion.88
  345.8 14.8 %attend_back.3 = bf16[4,256,768]{2,1,0:T(8,128)(2,1)S(1)} custom-call(s32[4,4]{1,0:T(4,128)S(1)} %pad_add_fusion.bounds, s32[8]{0:T(128)S(1)} %convert_add_fusion.6.slot_of, bf16[2048,256]{1,0:T(8,128)(2,1)S(1)} %copy-done.4, bf16[2048,256]{1,0:T(8,128)(2,1)S(1)} %copy-done.9, bf16[2048,256]{1,0:T(8,128)(2,1)S(1)} %copy-done.14, ...), custom_call_target="tpu_custom_call" | custom-call | flops 230000000 | bytes 1024 | tf_op jit(solution)/shard_map/attend_back/pallas_call | solution.py:573
  364.3 3.2 multiply_reduce_fusion
  371.7 2.4 convert_add_fusion
  375.7 2.3 spread_first.1
  386.3 35.1 %collective-permute-done.51.far_ref = bf16[256,1024]{1,0:T(8,128)(2,1)S(1)} collective-permute-done((bf16[256,1024]{1,0:T(8,128)(2,1)S(1)}, bf16[256,1024]{1,0:T(8,128)(2,1)S(1)}, u32[]{:S(2)}, u32[]{:S(2)}) %collective-permute-start.51) | collective-permute-done | bytes 524320 | tf_op jit(solution)/shard_map/ppermute | solution.py:994
  426.2 2.6 collective-permute-start.59
  432.1 2.4 collective-permute-done.54.low_far
  436.2 26.8 %collective-permute-done.59 = bf16[448,512]{1,0:T(8,128)(2,1)S(1)} collective-permute-done((bf16[448,512]{1,0:T(8,128)(2,1)}, bf16[448,512]{1,0:T(8,128)(2,1)S(1)}, u32[]{:S(2)}, u32[]{:S(2)}) %collective-permute-start.59) | collective-permute-done | bytes 458784 | tf_op jit(solution)/shard_map/ppermute | solution.py:994
  464.4 2.3 broadcast_select_fusion.4
  468.6 6.3 %collective-permute-done.57.far = bf16[11,128,128]{2,1,0:T(8,128)(2,1)S(1)} collective-permute-done((bf16[11,128,128]{2,1,0:T(8,128)(2,1)S(1)}, bf16[11,128,128]{2,1,0:T(8,128)(2,1)S(1)}, u32[]{:S(2)}, u32[]{:S(2)}) %collective-permute-start.57) | collective-permute-done | bytes 360480 | tf_op jit(solution)/shard_map/ppermute | solution.py:994
  477.2 3.7 collective-permute-done.58.far
  (475 shorter events, 162.2 us)
Async XLA Ops:
  7.2 180.7 %all-gather.2.cloned.1.call-start = ((), (), s32[]{:S(2)}) async-start(), calls=%async_computation | async-start | bytes 5242880 | tf_op jit(solution)/shard_map/all_gather | solution.py:1222
  8.2 14.3 %collective-permute-start = (bf16[144,768]{1,0:T(8,128)(2,1)S(1)}, bf16[144,768]{1,0:T(8,128)(2,1)S(1)}, u32[]{:S(2)}, u32[]{:S(2)}) collective-permute-start(bf16[144,768]{1,0:T(8,128)(2,1)S(1)} %fusion.53), channel_id=1, source_target_pairs={{0,2},{1,3},{2,0},{3,1},{4,6},{5,7},{6,4},{7,5},{8,10},{9,11},{10,... | collective-permute-start | bytes 663560 | tf_op jit(solution)/shard_map/ppermute | solution.py:994
  23.6 36.8 %collective-permute-start.2 = (bf16[2,256,1024]{2,1,0:T(8,128)(2,1)}, bf16[2,256,1024]{2,1,0:T(8,128)(2,1)}, u32[]{:S(2)}, u32[]{:S(2)}) collective-permute-start(bf16[2,256,1024]{2,1,0:T(8,128)(2,1)} %bitcast.6), channel_id=1, source_target_pairs={{4,2},{2,4},{5,3},{3,5},{12,10},{10,12},{13,11},{11,13},{20,18},{1... | collective-permute-start | bytes 3145736 | tf_op jit(solution)/shard_map/ppermute | solution.py:1004
  26.5 7.9 %collective-permute-start.4 = (bf16[144,512]{1,0:T(8,128)(2,1)}, bf16[144,512]{1,0:T(8,128)(2,1)}, u32[]{:S(2)}, u32[]{:S(2)}) collective-permute-start(bf16[144,512]{1,0:T(8,128)(2,1)} %constant_dynamic-update-slice_fusion.20), channel_id=1, source_target_pairs={{0,1},{1,0},{2,3},{3,2},{4,5},{5,4},{6,7},{7,6},{8,9},{9,8},{10,11... | collective-permute-start | bytes 442376 | tf_op jit(solution)/shard_map/ppermute | solution.py:994
  37.5 12.2 %collective-permute-start.9 = (bf16[144,768]{1,0:T(8,128)(2,1)S(1)}, bf16[144,768]{1,0:T(8,128)(2,1)S(1)}, u32[]{:S(2)}, u32[]{:S(2)}) collective-permute-start(bf16[144,768]{1,0:T(8,128)(2,1)S(1)} %pad_maximum_fusion.24), channel_id=1, source_target_pairs={{0,4},{4,0},{1,5},{5,1},{2,6},{6,2},{3,7},{7,3},{8,12},{12,8},{9,1... | collective-permute-start | bytes 663560 | tf_op jit(solution)/shard_map/ppermute | solution.py:994
  44.6 8.4 %collective-permute-start.5 = (bf16[2,128,512]{2,1,0:T(8,128)(2,1)S(1)}, bf16[2,128,512]{2,1,0:T(8,128)(2,1)S(1)}, u32[]{:S(2)}, u32[]{:S(2)}) collective-permute-start(bf16[2,128,512]{2,1,0:T(8,128)(2,1)S(1)} %pad_maximum_fusion.28), channel_id=1, source_target_pairs={{0,4},{4,0},{1,5},{5,1},{2,6},{6,2},{3,7},{7,3},{8,12},{12,8},{9,1... | collective-permute-start | bytes 786440 | tf_op jit(solution)/shard_map/ppermute | solution.py:994
  44.7 26.1 %collective-permute-start.6 = (bf16[128,256]{1,0:T(8,128)(2,1)S(1)}, bf16[128,256]{1,0:T(8,128)(2,1)}, u32[]{:S(2)}, u32[]{:S(2)}) collective-permute-start(bf16[128,256]{1,0:T(8,128)(2,1)S(1)} %copy-done.90), channel_id=1, source_target_pairs={{0,2},{1,3},{2,0},{3,1},{4,6},{5,7},{6,4},{7,5},{8,10},{9,11},{10,... | collective-permute-start | bytes 196616 | tf_op jit(solution)/shard_map/ppermute | solution.py:994
  57.2 11.1 %collective-permute-start.11 = (bf16[2,2,144,384]{3,2,1,0:T(8,128)(2,1)S(1)}, bf16[2,2,144,384]{3,2,1,0:T(8,128)(2,1)S(1)}, u32[]{:S(2)}, u32[]{:S(2)}) collective-permute-start(bf16[2,2,144,384]{3,2,1,0:T(8,128)(2,1)S(1)} %pad_maximum_fusion.22), channel_id=1, source_target_pairs={{0,16},{8,24},{16,0},{24,8},{1,17},{9,25},{17,1},{25,9},{2,18},{10... | collective-permute-start | bytes 1327112 | tf_op jit(solution)/shard_map/ppermute | solution.py:994
  58.9 10.8 %collective-permute-start.13 = (bf16[2,2,144,384]{3,2,1,0:T(8,128)(2,1)S(1)}, bf16[2,2,144,384]{3,2,1,0:T(8,128)(2,1)S(1)}, u32[]{:S(2)}, u32[]{:S(2)}) collective-permute-start(bf16[2,2,144,384]{3,2,1,0:T(8,128)(2,1)S(1)} %pad_maximum_fusion.23), channel_id=1, source_target_pairs={{0,8},{8,0},{16,24},{24,16},{1,9},{9,1},{17,25},{25,17},{2,10},{10... | collective-permute-start | bytes 1327112 | tf_op jit(solution)/shard_map/ppermute | solution.py:994
  61.8 30.9 %collective-permute-start.3 = (bf16[2,256,1024]{2,1,0:T(8,128)(2,1)S(1)}, bf16[2,256,1024]{2,1,0:T(8,128)(2,1)}, u32[]{:S(2)}, u32[]{:S(2)}) collective-permute-start(bf16[2,256,1024]{2,1,0:T(8,128)(2,1)S(1)} %bitcast_select_fusion.near.x_ref), channel_id=1, source_target_pairs={{0,1},{1,0},{2,3},{3,2},{4,5},{5,4},{6,7},{7,6},{8,9},{9,8},{10,11... | collective-permute-start | bytes 3145736 | tf_op jit(solution)/shard_map/ppermute | solution.py:994
  61.9 13.0 %collective-permute-start.8 = (bf16[2,256,1024]{2,1,0:T(8,128)(2,1)S(1)}, bf16[2,256,1024]{2,1,0:T(8,128)(2,1)}, u32[]{:S(2)}, u32[]{:S(2)}) collective-permute-start(bf16[2,256,1024]{2,1,0:T(8,128)(2,1)S(1)} %bitcast_select_fusion.near.x_ref), channel_id=1, source_target_pairs={{0,4},{4,0},{1,5},{5,1},{2,6},{6,2},{3,7},{7,3},{8,12},{12,8},{9,1... | collective-permute-start | bytes 3145736 | tf_op jit(solution)/shard_map/ppermute | solution.py:994
  70.8 19.7 %collective-permute-start.7 = (bf16[256,512]{1,0:T(8,128)(2,1)S(1)}, bf16[256,512]{1,0:T(8,128)(2,1)S(1)}, u32[]{:S(2)}, u32[]{:S(2)}) collective-permute-start(bf16[256,512]{1,0:T(8,128)(2,1)S(1)} %get-tuple-element.157), channel_id=1, source_target_pairs={{0,2},{1,3},{2,0},{3,1},{4,6},{5,7},{6,4},{7,5},{8,10},{9,11},{10,... | collective-permute-start | bytes 786440 | tf_op jit(solution)/shard_map/ppermute | solution.py:994
  73.2 20.8 %collective-permute-start.15 = (bf16[128,512]{1,0:T(8,128)(2,1)S(1)}, bf16[128,512]{1,0:T(8,128)(2,1)S(1)}, u32[]{:S(2)}, u32[]{:S(2)}) collective-permute-start(bf16[128,512]{1,0:T(8,128)(2,1)S(1)} %pad_maximum_fusion.31), channel_id=1, source_target_pairs={{0,1},{1,0},{2,3},{3,2},{4,5},{5,4},{6,7},{7,6},{8,9},{9,8},{10,11... | collective-permute-start | bytes 393224 | tf_op jit(solution)/shard_map/ppermute | solution.py:994
  95.0 17.4 %collective-permute-start.16 = (bf16[256,1024]{1,0:T(8,128)(2,1)}, bf16[256,1024]{1,0:T(8,128)(2,1)}, u32[]{:S(2)}, u32[]{:S(2)}) collective-permute-start(bf16[256,1024]{1,0:T(8,128)(2,1)} %pad_maximum_fusion.16), channel_id=1, source_target_pairs={{0,1},{1,0},{2,3},{3,2},{4,5},{5,4},{6,7},{7,6},{8,9},{9,8},{10,11... | collective-permute-start | bytes 1572872 | tf_op jit(solution)/shard_map/ppermute | solution.py:994
  95.4 17.1 %collective-permute-start.17 = (bf16[1,128,1024]{2,1,0:T(8,128)(2,1)S(1)}, bf16[1,128,1024]{2,1,0:T(8,128)(2,1)}, u32[]{:S(2)}, u32[]{:S(2)}) collective-permute-start(bf16[1,128,1024]{2,1,0:T(8,128)(2,1)S(1)} %maximum_bitcast_fusion.2), channel_id=1, source_target_pairs={{0,8},{8,0},{16,24},{24,16},{1,9},{9,1},{17,25},{25,17},{2,10},{10... | collective-permute-start | bytes 786440 | tf_op jit(solution)/shard_map/ppermute | solution.py:994
  117.1 19.1 %collective-permute-start.19 = (bf16[2,128,1024]{2,1,0:T(8,128)(2,1)S(1)}, bf16[2,128,1024]{2,1,0:T(8,128)(2,1)S(1)}, u32[]{:S(2)}, u32[]{:S(2)}) collective-permute-start(bf16[2,128,1024]{2,1,0:T(8,128)(2,1)S(1)} %pad_maximum_fusion.17), channel_id=1, source_target_pairs={{0,16},{8,24},{16,0},{24,8},{1,17},{9,25},{17,1},{25,9},{2,18},{10... | collective-permute-start | bytes 1572872 | tf_op jit(solution)/shard_map/ppermute | solution.py:994
  118.3 16.2 %collective-permute-start.18 = (bf16[256,512]{1,0:T(8,128)(2,1)}, bf16[256,512]{1,0:T(8,128)(2,1)S(1)}, u32[]{:S(2)}, u32[]{:S(2)}) collective-permute-start(bf16[256,512]{1,0:T(8,128)(2,1)} %get-tuple-element.171), channel_id=1, source_target_pairs={{0,2},{1,3},{2,0},{3,1},{4,6},{5,7},{6,4},{7,5},{8,10},{9,11},{10,... | collective-permute-start | bytes 786440 | tf_op jit(solution)/shard_map/ppermute | solution.py:994
  137.3 18.5 %collective-permute-start.23 = (bf16[4,128,1024]{2,1,0:T(8,128)(2,1)}, bf16[4,128,1024]{2,1,0:T(8,128)(2,1)}, u32[]{:S(2)}, u32[]{:S(2)}) collective-permute-start(bf16[4,128,1024]{2,1,0:T(8,128)(2,1)} %pad_maximum_fusion.9), channel_id=1, source_target_pairs={{0,4},{4,0},{1,5},{5,1},{2,6},{6,2},{3,7},{7,3},{8,12},{12,8},{9,1... | collective-permute-start | bytes 3145736 | tf_op jit(solution)/shard_map/ppermute | solution.py:994
  138.2 17.6 %collective-permute-start.24 = (bf16[256,1024]{1,0:T(8,128)(2,1)}, bf16[256,1024]{1,0:T(8,128)(2,1)}, u32[]{:S(2)}, u32[]{:S(2)}) collective-permute-start(bf16[256,1024]{1,0:T(8,128)(2,1)} %pad_maximum_fusion.18), channel_id=1, source_target_pairs={{0,1},{1,0},{2,3},{3,2},{4,5},{5,4},{6,7},{7,6},{8,9},{9,8},{10,11... | collective-permute-start | bytes 1572872 | tf_op jit(solution)/shard_map/ppermute | solution.py:994
  157.4 23.7 %collective-permute-start.26 = (bf16[1,128,2048]{2,1,0:T(8,128)(2,1)S(1)}, bf16[1,128,2048]{2,1,0:T(8,128)(2,1)S(1)}, u32[]{:S(2)}, u32[]{:S(2)}) collective-permute-start(bf16[1,128,2048]{2,1,0:T(8,128)(2,1)S(1)} %get-tuple-element.183), channel_id=1, source_target_pairs={{0,8},{8,0},{16,24},{24,16},{1,9},{9,1},{17,25},{25,17},{2,10},{10... | collective-permute-start | bytes 1572872 | tf_op jit(solution)/shard_map/ppermute | solution.py:994
  157.5 23.6 %collective-permute-start.27 = (bf16[1,128,2048]{2,1,0:T(8,128)(2,1)S(1)}, bf16[1,128,2048]{2,1,0:T(8,128)(2,1)S(1)}, u32[]{:S(2)}, u32[]{:S(2)}) collective-permute-start(bf16[1,128,2048]{2,1,0:T(8,128)(2,1)S(1)} %get-tuple-element.185), channel_id=1, source_target_pairs={{0,16},{8,24},{16,0},{24,8},{1,17},{9,25},{17,1},{25,9},{2,18},{10... | collective-permute-start | bytes 1572872 | tf_op jit(solution)/shard_map/ppermute | solution.py:994
  159.2 9.2 %collective-permute-start.21 = (bf16[2,256,256]{2,1,0:T(8,128)(2,1)S(1)}, bf16[2,256,256]{2,1,0:T(8,128)(2,1)S(1)}, u32[]{:S(2)}, u32[]{:S(2)}) collective-permute-start(bf16[2,256,256]{2,1,0:T(8,128)(2,1)S(1)} %get-tuple-element.355), channel_id=1, source_target_pairs={{0,1},{1,0},{2,3},{3,2},{4,5},{5,4},{6,7},{7,6},{8,9},{9,8},{10,11... | collective-permute-start | bytes 786440 | tf_op jit(solution)/shard_map/ppermute | solution.py:994
  160.3 12.7 %collective-permute-start.22 = (bf16[2,256,256]{2,1,0:T(8,128)(2,1)S(1)}, bf16[2,256,256]{2,1,0:T(8,128)(2,1)S(1)}, u32[]{:S(2)}, u32[]{:S(2)}) collective-permute-start(bf16[2,256,256]{2,1,0:T(8,128)(2,1)S(1)} %get-tuple-element.354), channel_id=1, source_target_pairs={{0,5},{1,4},{2,7},{3,6},{4,1},{5,0},{6,3},{7,2},{8,13},{9,12},{10,... | collective-permute-start | bytes 786440 | tf_op jit(solution)/shard_map/ppermute | solution.py:1036
  176.9 9.5 %collective-permute-start.25 = (bf16[512,1024]{1,0:T(8,128)(2,1)S(1)}, bf16[512,1024]{1,0:T(8,128)(2,1)S(1)}, u32[]{:S(2)}, u32[]{:S(2)}) collective-permute-start(bf16[512,1024]{1,0:T(8,128)(2,1)S(1)} %get-tuple-element.180), channel_id=1, source_target_pairs={{0,4},{4,0},{1,5},{5,1},{2,6},{6,2},{3,7},{7,3},{8,12},{12,8},{9,1... | collective-permute-start | bytes 3145736 | tf_op jit(solution)/shard_map/ppermute | solution.py:994
  177.6 40.0 %collective-permute-start.31 = (bf16[512,1024]{1,0:T(8,128)(2,1)}, bf16[512,1024]{1,0:T(8,128)(2,1)}, u32[]{:S(2)}, u32[]{:S(2)}) collective-permute-start(bf16[512,1024]{1,0:T(8,128)(2,1)} %bitcast.40), channel_id=1, source_target_pairs={{4,2},{2,4},{5,3},{3,5},{12,10},{10,12},{13,11},{11,13},{20,18},{1... | collective-permute-start | bytes 3145736 | tf_op jit(solution)/shard_map/ppermute | solution.py:1004
  182.4 25.8 %collective-permute-start.28 = (bf16[2,128,2048]{2,1,0:T(8,128)(2,1)}, bf16[2,128,2048]{2,1,0:T(8,128)(2,1)}, u32[]{:S(2)}, u32[]{:S(2)}) collective-permute-start(bf16[2,128,2048]{2,1,0:T(8,128)(2,1)} %pad_maximum_fusion.11), channel_id=1, source_target_pairs={{0,16},{8,24},{16,0},{24,8},{1,17},{9,25},{17,1},{25,9},{2,18},{10... | collective-permute-start | bytes 3145736 | tf_op jit(solution)/shard_map/ppermute | solution.py:994
  185.8 25.0 %collective-permute-start.29 = (bf16[2,1,128,2048]{3,2,1,0:T(8,128)(2,1)}, bf16[2,1,128,2048]{3,2,1,0:T(8,128)(2,1)}, u32[]{:S(2)}, u32[]{:S(2)}) collective-permute-start(bf16[2,1,128,2048]{3,2,1,0:T(8,128)(2,1)} %maximum_bitcast_fusion.1), channel_id=1, source_target_pairs={{0,8},{8,0},{16,24},{24,16},{1,9},{9,1},{17,25},{25,17},{2,10},{10... | collective-permute-start | bytes 3145736 | tf_op jit(solution)/shard_map/ppermute | solution.py:994
  256.3 10.1 %collective-permute-start.33 = (bf16[512,1024]{1,0:T(8,128)(2,1)S(1)}, bf16[512,1024]{1,0:T(8,128)(2,1)S(1)}, u32[]{:S(2)}, u32[]{:S(2)}) collective-permute-start(bf16[512,1024]{1,0:T(8,128)(2,1)S(1)} %fusion.16), channel_id=1, source_target_pairs={{0,4},{4,0},{1,5},{5,1},{2,6},{6,2},{3,7},{7,3},{8,12},{12,8},{9,1... | collective-permute-start | bytes 3145736 | tf_op jit(solution)/shard_map/ppermute | solution.py:994
  260.5 60.7 %collective-permute-start.39 = (bf16[2,224,2048]{2,1,0:T(8,128)(2,1)}, bf16[2,224,2048]{2,1,0:T(8,128)(2,1)}, u32[]{:S(2)}, u32[]{:S(2)}) collective-permute-start(bf16[2,224,2048]{2,1,0:T(8,128)(2,1)} %pad_maximum_fusion.4), channel_id=1, source_target_pairs={{0,8},{8,0},{16,24},{24,16},{1,9},{9,1},{17,25},{25,17},{2,10},{10... | collective-permute-start | bytes 5505032 | tf_op jit(solution)/shard_map/ppermute | solution.py:994
  262.7 58.5 %collective-permute-start.40 = (bf16[2,224,2048]{2,1,0:T(8,128)(2,1)}, bf16[2,224,2048]{2,1,0:T(8,128)(2,1)}, u32[]{:S(2)}, u32[]{:S(2)}) collective-permute-start(bf16[2,224,2048]{2,1,0:T(8,128)(2,1)} %pad_maximum_fusion.5), channel_id=1, source_target_pairs={{0,16},{8,24},{16,0},{24,8},{1,17},{9,25},{17,1},{25,9},{2,18},{10... | collective-permute-start | bytes 5505032 | tf_op jit(solution)/shard_map/ppermute | solution.py:994
  270.8 8.6 %collective-permute-start.36 = (bf16[2,256,256]{2,1,0:T(8,128)(2,1)S(1)}, bf16[2,256,256]{2,1,0:T(8,128)(2,1)S(1)}, u32[]{:S(2)}, u32[]{:S(2)}) collective-permute-start(bf16[2,256,256]{2,1,0:T(8,128)(2,1)S(1)} %get-tuple-element.343), channel_id=1, source_target_pairs={{0,5},{1,4},{2,7},{3,6},{4,1},{5,0},{6,3},{7,2},{8,13},{9,12},{10,... | collective-permute-start | bytes 786440 | tf_op jit(solution)/shard_map/ppermute | solution.py:1036
  272.5 12.6 %collective-permute-start.34 = (bf16[2,256,256]{2,1,0:T(8,128)(2,1)S(1)}, bf16[2,256,256]{2,1,0:T(8,128)(2,1)S(1)}, u32[]{:S(2)}, u32[]{:S(2)}) collective-permute-start(bf16[2,256,256]{2,1,0:T(8,128)(2,1)S(1)} %get-tuple-element.345), channel_id=1, source_target_pairs={{0,1},{1,0},{2,3},{3,2},{4,5},{5,4},{6,7},{7,6},{8,9},{9,8},{10,11... | collective-permute-start | bytes 786440 | tf_op jit(solution)/shard_map/ppermute | solution.py:994
  286.3 34.9 %collective-permute-start.37 = (bf16[512,1024]{1,0:T(8,128)(2,1)}, bf16[512,1024]{1,0:T(8,128)(2,1)}, u32[]{:S(2)}, u32[]{:S(2)}) collective-permute-start(bf16[512,1024]{1,0:T(8,128)(2,1)} %get-tuple-element.256), channel_id=1, source_target_pairs={{4,2},{2,4},{5,3},{3,5},{12,10},{10,12},{13,11},{11,13},{20,18},{1... | collective-permute-start | bytes 3145736 | tf_op jit(solution)/shard_map/ppermute | solution.py:1004
  289.1 32.1 %collective-permute-start.38 = (bf16[2,256,512]{2,1,0:T(8,128)(2,1)}, bf16[2,256,512]{2,1,0:T(8,128)(2,1)}, u32[]{:S(2)}, u32[]{:S(2)}) collective-permute-start(bf16[2,256,512]{2,1,0:T(8,128)(2,1)} %get-tuple-element.337), channel_id=1, source_target_pairs={{0,1},{1,0},{2,3},{3,2},{4,5},{5,4},{6,7},{7,6},{8,9},{9,8},{10,11... | collective-permute-start | bytes 1572872 | tf_op jit(solution)/shard_map/ppermute | solution.py:994
  329.9 30.8 %collective-permute-start.43 = (bf16[4,128,1024]{2,1,0:T(8,128)(2,1)}, bf16[4,128,1024]{2,1,0:T(8,128)(2,1)S(1)}, u32[]{:S(2)}, u32[]{:S(2)}) collective-permute-start(bf16[4,128,1024]{2,1,0:T(8,128)(2,1)} %dynamic-slice_bitcast_fusion.2), channel_id=1, source_target_pairs={{0,4},{4,0},{1,5},{5,1},{2,6},{6,2},{3,7},{7,3},{8,12},{12,8},{9,1... | collective-permute-start | bytes 3145736 | tf_op jit(solution)/shard_map/ppermute | solution.py:994
  332.9 27.8 %collective-permute-start.44 = (bf16[224,2048]{1,0:T(8,128)(2,1)}, bf16[224,2048]{1,0:T(8,128)(2,1)S(1)}, u32[]{:S(2)}, u32[]{:S(2)}) collective-permute-start(bf16[224,2048]{1,0:T(8,128)(2,1)} %fusion.20), channel_id=1, source_target_pairs={{0,16},{8,24},{16,0},{24,8},{1,17},{9,25},{17,1},{25,9},{2,18},{10... | collective-permute-start | bytes 2752520 | tf_op jit(solution)/shard_map/ppermute | solution.py:994
  336.8 23.9 %collective-permute-start.45 = (bf16[224,2048]{1,0:T(8,128)(2,1)}, bf16[224,2048]{1,0:T(8,128)(2,1)}, u32[]{:S(2)}, u32[]{:S(2)}) collective-permute-start(bf16[224,2048]{1,0:T(8,128)(2,1)} %fusion.21), channel_id=1, source_target_pairs={{0,8},{8,0},{16,24},{24,16},{1,9},{9,1},{17,25},{25,17},{2,10},{10... | collective-permute-start | bytes 2752520 | tf_op jit(solution)/shard_map/ppermute | solution.py:994
  338.8 21.8 %collective-permute-start.42 = (bf16[256,512]{1,0:T(8,128)(2,1)}, bf16[256,512]{1,0:T(8,128)(2,1)S(1)}, u32[]{:S(2)}, u32[]{:S(2)}) collective-permute-start(bf16[256,512]{1,0:T(8,128)(2,1)} %fusion.48), channel_id=1, source_target_pairs={{0,2},{1,3},{2,0},{3,1},{4,6},{5,7},{6,4},{7,5},{8,10},{9,11},{10,... | collective-permute-start | bytes 786440 | tf_op jit(solution)/shard_map/ppermute | solution.py:994
  341.4 19.3 %collective-permute-start.46 = (bf16[256,1024]{1,0:T(8,128)(2,1)}, bf16[256,1024]{1,0:T(8,128)(2,1)S(1)}, u32[]{:S(2)}, u32[]{:S(2)}) collective-permute-start(bf16[256,1024]{1,0:T(8,128)(2,1)} %slice.664), channel_id=1, source_target_pairs={{0,1},{1,0},{2,3},{3,2},{4,5},{5,4},{6,7},{7,6},{8,9},{9,8},{10,11... | collective-permute-start | bytes 1572872 | tf_op jit(solution)/shard_map/ppermute | solution.py:994
  382.2 40.9 %collective-permute-start.53 = (bf16[2,448,512]{2,1,0:T(8,128)(2,1)S(1)}, bf16[2,448,512]{2,1,0:T(8,128)(2,1)S(1)}, u32[]{:S(2)}, u32[]{:S(2)}) collective-permute-start(bf16[2,448,512]{2,1,0:T(8,128)(2,1)S(1)} %get-tuple-element.325), channel_id=1, source_target_pairs={{0,1},{1,0},{2,3},{3,2},{4,5},{5,4},{6,7},{7,6},{8,9},{9,8},{10,11... | collective-permute-start | bytes 2752520 | tf_op jit(solution)/shard_map/ppermute | solution.py:994
  383.6 39.5 %collective-permute-start.50 = (bf16[2,12,128,128]{3,2,1,0:T(8,128)(2,1)S(1)}, bf16[2,12,128,128]{3,2,1,0:T(8,128)(2,1)S(1)}, u32[]{:S(2)}, u32[]{:S(2)}) collective-permute-start(bf16[2,12,128,128]{3,2,1,0:T(8,128)(2,1)S(1)} %get-tuple-element.239), channel_id=1, source_target_pairs={{0,16},{8,24},{16,0},{24,8},{1,17},{9,25},{17,1},{25,9},{2,18},{10... | collective-permute-start | bytes 2359304 | tf_op jit(solution)/shard_map/ppermute | solution.py:994
  384.4 38.7 %collective-permute-start.49 = (bf16[2,11,128,128]{3,2,1,0:T(8,128)(2,1)S(1)}, bf16[2,11,128,128]{3,2,1,0:T(8,128)(2,1)S(1)}, u32[]{:S(2)}, u32[]{:S(2)}) collective-permute-start(bf16[2,11,128,128]{3,2,1,0:T(8,128)(2,1)S(1)} %get-tuple-element.238), channel_id=1, source_target_pairs={{0,8},{8,0},{16,24},{24,16},{1,9},{9,1},{17,25},{25,17},{2,10},{10... | collective-permute-start | bytes 2162696 | tf_op jit(solution)/shard_map/ppermute | solution.py:994
  385.5 35.9 %collective-permute-start.51 = (bf16[256,1024]{1,0:T(8,128)(2,1)S(1)}, bf16[256,1024]{1,0:T(8,128)(2,1)S(1)}, u32[]{:S(2)}, u32[]{:S(2)}) collective-permute-start(bf16[256,1024]{1,0:T(8,128)(2,1)S(1)} %slice.663), channel_id=1, source_target_pairs={{0,1},{1,0},{2,3},{3,2},{4,5},{5,4},{6,7},{7,6},{8,9},{9,8},{10,11... | collective-permute-start | bytes 1572872 | tf_op jit(solution)/shard_map/ppermute | solution.py:994
  424.9 10.2 %collective-permute-start.55 = (bf16[12,128,128]{2,1,0:T(8,128)(2,1)S(1)}, bf16[12,128,128]{2,1,0:T(8,128)(2,1)S(1)}, u32[]{:S(2)}, u32[]{:S(2)}) collective-permute-start(bf16[12,128,128]{2,1,0:T(8,128)(2,1)S(1)} %get-tuple-element.254), channel_id=1, source_target_pairs={{0,8},{8,0},{16,24},{24,16},{1,9},{9,1},{17,25},{25,17},{2,10},{10... | collective-permute-start | bytes 1179656 | tf_op jit(solution)/shard_map/ppermute | solution.py:994
  425.0 9.5 %collective-permute-start.54 = (bf16[11,128,128]{2,1,0:T(8,128)(2,1)S(1)}, bf16[11,128,128]{2,1,0:T(8,128)(2,1)S(1)}, u32[]{:S(2)}, u32[]{:S(2)}) collective-permute-start(bf16[11,128,128]{2,1,0:T(8,128)(2,1)S(1)} %get-tuple-element.252), channel_id=1, source_target_pairs={{0,16},{8,24},{16,0},{24,8},{1,17},{9,25},{17,1},{25,9},{2,18},{10... | collective-permute-start | bytes 1081352 | tf_op jit(solution)/shard_map/ppermute | solution.py:994
  426.2 36.9 %collective-permute-start.59 = (bf16[448,512]{1,0:T(8,128)(2,1)}, bf16[448,512]{1,0:T(8,128)(2,1)S(1)}, u32[]{:S(2)}, u32[]{:S(2)}) collective-permute-start(bf16[448,512]{1,0:T(8,128)(2,1)} %fusion.38), channel_id=1, source_target_pairs={{0,2},{1,3},{2,0},{3,1},{4,6},{5,7},{6,4},{7,5},{8,10},{9,11},{10,... | collective-permute-start | bytes 1376264 | tf_op jit(solution)/shard_map/ppermute | solution.py:994
  430.7 45.0 %collective-permute-start.56 = (bf16[256,1024]{1,0:T(8,128)(2,1)}, bf16[256,1024]{1,0:T(8,128)(2,1)}, u32[]{:S(2)}, u32[]{:S(2)}) collective-permute-start(bf16[256,1024]{1,0:T(8,128)(2,1)} %copy-done.42), channel_id=1, source_target_pairs={{4,2},{2,4},{5,3},{3,5},{12,10},{10,12},{13,11},{11,13},{20,18},{1... | collective-permute-start | bytes 1572872 | tf_op jit(solution)/shard_map/ppermute | solution.py:1004
  435.9 39.0 %collective-permute-start.57 = (bf16[11,128,128]{2,1,0:T(8,128)(2,1)S(1)}, bf16[11,128,128]{2,1,0:T(8,128)(2,1)S(1)}, u32[]{:S(2)}, u32[]{:S(2)}) collective-permute-start(bf16[11,128,128]{2,1,0:T(8,128)(2,1)S(1)} %get-tuple-element.255), channel_id=1, source_target_pairs={{0,2},{1,3},{2,0},{3,1},{4,6},{5,7},{6,4},{7,5},{8,10},{9,11},{10,... | collective-permute-start | bytes 1081352 | tf_op jit(solution)/shard_map/ppermute | solution.py:994
  (110 other events, 689.0 us)
Sparse Core Ops, SparseCore 0:
  115.9 63.8 all-gather.1
